TPU v7x, 32 devices: a whole 2x2x4 slice. The times are simulated.
32 devices in a mesh: fsdp: 8 (over z, y), dp: 4 (over x, core).
Axes of the slice: x: 2, y: 2, z: 4, core: 2. Of those that a mesh axis runs over, the one named last changes fastest.
Arguments:
- tokens: bfloat16 [65536, 384], P(('fsdp', 'dp')), may hold values from -6 to 6
- cotangent: bfloat16 [65536, 384], P(('fsdp', 'dp')), may hold values from -6 to 6
- size_group: int32 [256], replicated, may hold values from 0 to 2
- assignment: int32 [256], replicated, may hold values from 0 to 31, as said below
- ln1_gain: bfloat16 [384], P('fsdp'), may hold values from 0.5 to 1.5
- ln1_bias: bfloat16 [384], P('fsdp'), may hold values from -2 to 2
- w_qkv: bfloat16 [442368], P('fsdp'), may hold values from -0.4375 to 0.4375
- q_bias: bfloat16 [384], P('fsdp'), may hold values from -3 to 3
- v_bias: bfloat16 [384], P('fsdp'), may hold values from -3 to 3
- w_proj: bfloat16 [147456], P('fsdp'), may hold values from -1.25 to 1.25
- proj_bias: bfloat16 [384], P('fsdp'), may hold values from -2 to 2
- ln2_gain: bfloat16 [384], P('fsdp'), may hold values from 0.5 to 1.5
- ln2_bias: bfloat16 [384], P('fsdp'), may hold values from -2 to 2
- w_up: bfloat16 [589824], P('fsdp'), may hold values from -0.3125 to 0.3125
- up_bias: bfloat16 [1536], P('fsdp'), may hold values from -3 to 3
- w_down: bfloat16 [589824], P('fsdp'), may hold values from -0.21875 to 0.21875
- down_bias: bfloat16 [384], P('fsdp'), may hold values from -2 to 2
Outputs:
- layer_out: bfloat16 [65536, 384], P(('fsdp', 'dp'))
- input_grad: bfloat16 [65536, 384], P(('fsdp', 'dp'))
- grad_ln1_gain: float32 [384], P('fsdp')
- grad_ln1_bias: float32 [384], P('fsdp')
- grad_w_qkv: float32 [442368], P('fsdp')
- grad_q_bias: float32 [384], P('fsdp')
- grad_v_bias: float32 [384], P('fsdp')
- grad_w_proj: float32 [147456], P('fsdp')
- grad_proj_bias: float32 [384], P('fsdp')
- grad_ln2_gain: float32 [384], P('fsdp')
- grad_ln2_bias: float32 [384], P('fsdp')
- grad_w_up: float32 [589824], P('fsdp')
- grad_up_bias: float32 [1536], P('fsdp')
- grad_w_down: float32 [589824], P('fsdp')
- grad_down_bias: float32 [384], P('fsdp')
Inputs may be any that keep to these rules, and one draw needn't show every extreme that they name: `assignment`: every device receives exactly 8 images whose tokens number at most 2048, and some device holds exactly 2048; a device's rows of tokens and cotangent hold its images in increasing image order from its first row, then unused rows.
All inputs are finite; a program needn't handle non-finite values.
Results may differ from a plain program's by a relative error of at most 0.014.
The roundings to bfloat16 on the way count: a program that leaves them out, or rounds other values in their place, can miss the bound.
Values may be sent and summed in bfloat16 or wider, within the bound.
No kernel may reach another device: no remote copies, remote signals or barrier semaphores. Data moves between devices by JAX's collectives and lax.ppermute only.
A program may use at most 256 MiB of HBM per device.

v0:
```python
from functools import partial
import math

import jax
import jax.numpy as jnp
from jax import lax
from jax.sharding import PartitionSpec as P

HEAD_DIM = 96
LEN_S = 196
LEN_M = 256
LEN_L = 400


def row_layout(size_group, assignment, device, rows_cap):
    lengths = jnp.where(size_group == 0, LEN_S, jnp.where(size_group == 1, LEN_M, LEN_L)).astype(
        jnp.int32
    )
    owned_mask = (assignment == device).astype(jnp.int32)
    image_ends = jnp.cumsum(lengths * owned_mask)
    positions = jnp.arange(rows_cap, dtype=jnp.int32)
    finished = (image_ends[None, :] <= positions[:, None]) & (owned_mask[None, :] == 1)
    segment = jnp.sum(finished.astype(jnp.int32), axis=1)
    valid_rows = (positions < image_ends[-1]).astype(jnp.float32)
    return (segment, valid_rows)


def product(former, latter):
    return jnp.dot(former, latter, preferred_element_type=jnp.float32)


def weight_outer(former, latter):
    return lax.dot_general(
        former, latter, (((0,), (0,)), ((), ())), preferred_element_type=jnp.float32
    )


def times_transpose(former, latter):
    return lax.dot_general(
        former, latter, (((1,), (1,)), ((), ())), preferred_element_type=jnp.float32
    )


def normalize_rows(values):
    center = values - jnp.mean(values, axis=-1, keepdims=True)
    variance = jnp.mean(center * center, axis=-1, keepdims=True)
    inverse = lax.rsqrt(variance + 1e-06)
    return (center * inverse, inverse)


def norm_back(upstream, scaled, inverse, gain):
    shaped = upstream * gain
    return inverse * (
        shaped
        - jnp.mean(shaped, axis=-1, keepdims=True)
        - scaled * jnp.mean(shaped * scaled, axis=-1, keepdims=True)
    )


def shaped_params(gathered):
    (
        gain_one,
        bias_one,
        qkv_flat,
        query_bias,
        value_bias,
        proj_flat,
        proj_add,
        gain_two,
        bias_two,
        up_flat,
        up_add,
        down_flat,
        down_add,
    ) = gathered
    model_width = gain_one.shape[0]
    hidden_units = up_add.shape[0]
    return (
        gain_one.astype(jnp.float32),
        bias_one.astype(jnp.float32),
        qkv_flat.reshape(model_width, 3 * model_width),
        query_bias.astype(jnp.float32),
        value_bias.astype(jnp.float32),
        proj_flat.reshape(model_width, model_width),
        proj_add.astype(jnp.float32),
        gain_two.astype(jnp.float32),
        bias_two.astype(jnp.float32),
        up_flat.reshape(model_width, hidden_units),
        up_add.astype(jnp.float32),
        down_flat.reshape(hidden_units, model_width),
        down_add.astype(jnp.float32),
    )


def masked_scores(query_block, keys_all, segment_block, segment, score_scale):
    scores = (
        jnp.einsum("qhd,khd->hqk", query_block, keys_all, preferred_element_type=jnp.float32)
        * score_scale
    )
    same_image = segment_block[:, None] == segment[None, :]
    return jnp.where(same_image[None], scores, -1e30)


def body(
    tokens,
    cotangent,
    size_group,
    assignment,
    ln1_gain,
    ln1_bias,
    w_qkv,
    q_bias,
    v_bias,
    w_proj,
    proj_bias,
    ln2_gain,
    ln2_bias,
    w_up,
    up_bias,
    w_down,
    down_bias,
):
    (
        gain_one,
        bias_one,
        qkv_mat,
        query_bias,
        value_bias,
        proj_mat,
        proj_add,
        gain_two,
        bias_two,
        up_mat,
        up_add,
        down_mat,
        down_add,
    ) = shaped_params(
        (
            lax.all_gather(ln1_gain, "fsdp", axis=0, tiled=True),
            lax.all_gather(ln1_bias, "fsdp", axis=0, tiled=True),
            lax.all_gather(w_qkv, "fsdp", axis=0, tiled=True),
            lax.all_gather(q_bias, "fsdp", axis=0, tiled=True),
            lax.all_gather(v_bias, "fsdp", axis=0, tiled=True),
            lax.all_gather(w_proj, "fsdp", axis=0, tiled=True),
            lax.all_gather(proj_bias, "fsdp", axis=0, tiled=True),
            lax.all_gather(ln2_gain, "fsdp", axis=0, tiled=True),
            lax.all_gather(ln2_bias, "fsdp", axis=0, tiled=True),
            lax.all_gather(w_up, "fsdp", axis=0, tiled=True),
            lax.all_gather(up_bias, "fsdp", axis=0, tiled=True),
            lax.all_gather(w_down, "fsdp", axis=0, tiled=True),
            lax.all_gather(down_bias, "fsdp", axis=0, tiled=True),
        )
    )
    rows_cap = tokens.shape[0]
    model_width = tokens.shape[1]
    head_count = model_width // HEAD_DIM
    score_scale = 1.0 / math.sqrt(HEAD_DIM)
    block_rows = min(512, rows_cap)
    blocks = rows_cap // block_rows
    device = lax.axis_index("fsdp") * lax.axis_size("dp") + lax.axis_index("dp")
    segment, valid_rows = row_layout(size_group, assignment, device, rows_cap)
    inputs = tokens.astype(jnp.float32)
    scaled_one, inverse_one = normalize_rows(inputs)
    normed_one = (scaled_one * gain_one + bias_one).astype(jnp.bfloat16)
    bias_full = jnp.concatenate([query_bias, jnp.zeros_like(query_bias), value_bias])
    qkv_rows = (product(normed_one, qkv_mat) + bias_full).astype(jnp.bfloat16)
    queries = qkv_rows[:, :model_width].reshape(rows_cap, head_count, HEAD_DIM)
    keys_all = qkv_rows[:, model_width : 2 * model_width].reshape(rows_cap, head_count, HEAD_DIM)
    values_all = qkv_rows[:, 2 * model_width :].reshape(rows_cap, head_count, HEAD_DIM)
    mixed_parts = []
    logsum_parts = []
    for block_num in range(blocks):
        first_row = block_num * block_rows
        scores = masked_scores(
            queries[first_row : first_row + block_rows],
            keys_all,
            segment[first_row : first_row + block_rows],
            segment,
            score_scale,
        )
        row_max = jnp.max(scores, axis=-1, keepdims=True)
        exponent = jnp.exp(scores - row_max)
        row_sum = jnp.sum(exponent, axis=-1, keepdims=True)
        probs_low = (exponent / row_sum).astype(jnp.bfloat16)
        logsum_parts.append(row_max + jnp.log(row_sum))
        mixed_block = jnp.einsum(
            "hqk,khd->qhd", probs_low, values_all, preferred_element_type=jnp.float32
        )
        mixed_parts.append(mixed_block.reshape(block_rows, model_width))
    attn_rows = jnp.concatenate(mixed_parts, axis=0).astype(jnp.bfloat16)
    residual = inputs + product(attn_rows, proj_mat) + proj_add
    scaled_two, inverse_two = normalize_rows(residual)
    normed_two = (scaled_two * gain_two + bias_two).astype(jnp.bfloat16)
    preact = product(normed_two, up_mat) + up_add
    active, gelu_back = jax.vjp(partial(jax.nn.gelu, approximate=False), preact)
    active_low = active.astype(jnp.bfloat16)
    layer_out = (
        (residual + product(active_low, down_mat) + down_add) * valid_rows[:, None]
    ).astype(jnp.bfloat16)
    back_params = shaped_params(
        (
            lax.all_gather(ln1_gain, "fsdp", axis=0, tiled=True),
            lax.all_gather(ln1_bias, "fsdp", axis=0, tiled=True),
            lax.all_gather(w_qkv, "fsdp", axis=0, tiled=True),
            lax.all_gather(q_bias, "fsdp", axis=0, tiled=True),
            lax.all_gather(v_bias, "fsdp", axis=0, tiled=True),
            lax.all_gather(w_proj, "fsdp", axis=0, tiled=True),
            lax.all_gather(proj_bias, "fsdp", axis=0, tiled=True),
            lax.all_gather(ln2_gain, "fsdp", axis=0, tiled=True),
            lax.all_gather(ln2_bias, "fsdp", axis=0, tiled=True),
            lax.all_gather(w_up, "fsdp", axis=0, tiled=True),
            lax.all_gather(up_bias, "fsdp", axis=0, tiled=True),
            lax.all_gather(w_down, "fsdp", axis=0, tiled=True),
            lax.all_gather(down_bias, "fsdp", axis=0, tiled=True),
        )
    )
    back_gain_one = back_params[0]
    back_qkv = back_params[2]
    back_proj = back_params[5]
    back_gain_two = back_params[7]
    back_up = back_params[9]
    back_down = back_params[11]
    upstream = cotangent.astype(jnp.float32) * valid_rows[:, None]
    upstream_low = upstream.astype(jnp.bfloat16)
    grad_down_bias = jnp.sum(upstream, axis=0)
    grad_down = weight_outer(active_low, upstream_low)
    grad_active = times_transpose(upstream_low, back_down)
    grad_pre = gelu_back(grad_active)[0]
    grad_pre_low = grad_pre.astype(jnp.bfloat16)
    grad_up_bias = jnp.sum(grad_pre, axis=0)
    grad_up = weight_outer(normed_two, grad_pre_low)
    grad_normed_two = times_transpose(grad_pre_low, back_up)
    grad_gain_two = jnp.sum(grad_normed_two * scaled_two, axis=0)
    grad_bias_two = jnp.sum(grad_normed_two, axis=0)
    grad_resid = upstream + norm_back(grad_normed_two, scaled_two, inverse_two, back_gain_two)
    grad_resid_low = grad_resid.astype(jnp.bfloat16)
    grad_proj_bias = jnp.sum(grad_resid, axis=0)
    grad_proj = weight_outer(attn_rows, grad_resid_low)
    grad_attn = (
        times_transpose(grad_resid_low, back_proj)
        .astype(jnp.bfloat16)
        .reshape(rows_cap, head_count, HEAD_DIM)
    )
    grad_query_parts = []
    grad_keys = jnp.zeros((rows_cap, head_count, HEAD_DIM), jnp.float32)
    grad_values = jnp.zeros((rows_cap, head_count, HEAD_DIM), jnp.float32)
    for block_num in range(blocks):
        first_row = block_num * block_rows
        query_block = queries[first_row : first_row + block_rows]
        scores = masked_scores(
            query_block, keys_all, segment[first_row : first_row + block_rows], segment, score_scale
        )
        probs_full = jnp.exp(scores - logsum_parts[block_num])
        probs_low = probs_full.astype(jnp.bfloat16)
        grad_block = grad_attn[first_row : first_row + block_rows]
        grad_probs = jnp.einsum(
            "qhd,khd->hqk", grad_block, values_all, preferred_element_type=jnp.float32
        )
        grad_values = grad_values + jnp.einsum(
            "hqk,qhd->khd", probs_low, grad_block, preferred_element_type=jnp.float32
        )
        grad_scores = (
            probs_full * (grad_probs - jnp.sum(probs_full * grad_probs, axis=-1, keepdims=True))
        ).astype(jnp.bfloat16)
        grad_query_parts.append(
            jnp.einsum("hqk,khd->qhd", grad_scores, keys_all, preferred_element_type=jnp.float32)
            * score_scale
        )
        grad_keys = (
            grad_keys
            + jnp.einsum(
                "hqk,qhd->khd", grad_scores, query_block, preferred_element_type=jnp.float32
            )
            * score_scale
        )
    grad_queries = jnp.concatenate(grad_query_parts, axis=0).reshape(rows_cap, model_width)
    grad_values_rows = grad_values.reshape(rows_cap, model_width)
    grad_qkv = jnp.concatenate(
        [grad_queries, grad_keys.reshape(rows_cap, model_width), grad_values_rows], axis=1
    )
    grad_query_bias = jnp.sum(grad_queries, axis=0)
    grad_value_bias = jnp.sum(grad_values_rows, axis=0)
    grad_qkv_low = grad_qkv.astype(jnp.bfloat16)
    grad_qkv_mat = weight_outer(normed_one, grad_qkv_low)
    grad_normed_one = times_transpose(grad_qkv_low, back_qkv)
    grad_gain_one = jnp.sum(grad_normed_one * scaled_one, axis=0)
    grad_bias_one = jnp.sum(grad_normed_one, axis=0)
    grad_input = (
        grad_resid + norm_back(grad_normed_one, scaled_one, inverse_one, back_gain_one)
    ).astype(jnp.bfloat16)
    flat_qkv = grad_qkv_mat.reshape(-1)
    flat_proj = grad_proj.reshape(-1)
    flat_up = grad_up.reshape(-1)
    flat_down = grad_down.reshape(-1)
    (
        part_gain_one,
        part_bias_one,
        part_qkv,
        part_query,
        part_value,
        part_proj,
        part_proj_bias,
        part_gain_two,
        part_bias_two,
        part_up,
        part_up_bias,
        part_down,
        part_down_bias,
    ) = (
        lax.psum_scatter(grad_gain_one, "fsdp", scatter_dimension=0, tiled=True),
        lax.psum_scatter(grad_bias_one, "fsdp", scatter_dimension=0, tiled=True),
        lax.psum_scatter(flat_qkv, "fsdp", scatter_dimension=0, tiled=True),
        lax.psum_scatter(grad_query_bias, "fsdp", scatter_dimension=0, tiled=True),
        lax.psum_scatter(grad_value_bias, "fsdp", scatter_dimension=0, tiled=True),
        lax.psum_scatter(flat_proj, "fsdp", scatter_dimension=0, tiled=True),
        lax.psum_scatter(grad_proj_bias, "fsdp", scatter_dimension=0, tiled=True),
        lax.psum_scatter(grad_gain_two, "fsdp", scatter_dimension=0, tiled=True),
        lax.psum_scatter(grad_bias_two, "fsdp", scatter_dimension=0, tiled=True),
        lax.psum_scatter(flat_up, "fsdp", scatter_dimension=0, tiled=True),
        lax.psum_scatter(grad_up_bias, "fsdp", scatter_dimension=0, tiled=True),
        lax.psum_scatter(flat_down, "fsdp", scatter_dimension=0, tiled=True),
        lax.psum_scatter(grad_down_bias, "fsdp", scatter_dimension=0, tiled=True),
    )
    totals = (
        lax.psum(part_gain_one.astype(jnp.bfloat16), "dp").astype(jnp.float32),
        lax.psum(part_bias_one.astype(jnp.bfloat16), "dp").astype(jnp.float32),
        lax.psum(part_qkv.astype(jnp.bfloat16), "dp").astype(jnp.float32),
        lax.psum(part_query.astype(jnp.bfloat16), "dp").astype(jnp.float32),
        lax.psum(part_value.astype(jnp.bfloat16), "dp").astype(jnp.float32),
        lax.psum(part_proj.astype(jnp.bfloat16), "dp").astype(jnp.float32),
        lax.psum(part_proj_bias.astype(jnp.bfloat16), "dp").astype(jnp.float32),
        lax.psum(part_gain_two.astype(jnp.bfloat16), "dp").astype(jnp.float32),
        lax.psum(part_bias_two.astype(jnp.bfloat16), "dp").astype(jnp.float32),
        lax.psum(part_up.astype(jnp.bfloat16), "dp").astype(jnp.float32),
        lax.psum(part_up_bias.astype(jnp.bfloat16), "dp").astype(jnp.float32),
        lax.psum(part_down.astype(jnp.bfloat16), "dp").astype(jnp.float32),
        lax.psum(part_down_bias.astype(jnp.bfloat16), "dp").astype(jnp.float32),
    )
    return (layer_out, grad_input) + tuple(totals)


def solution(mesh):
    return jax.shard_map(
        body,
        mesh=mesh,
        in_specs=(
            P(("fsdp", "dp"), None),
            P(("fsdp", "dp"), None),
            P(),
            P(),
            P("fsdp"),
            P("fsdp"),
            P("fsdp"),
            P("fsdp"),
            P("fsdp"),
            P("fsdp"),
            P("fsdp"),
            P("fsdp"),
            P("fsdp"),
            P("fsdp"),
            P("fsdp"),
            P("fsdp"),
            P("fsdp"),
        ),
        out_specs=(
            P(("fsdp", "dp"), None),
            P(("fsdp", "dp"), None),
            P("fsdp"),
            P("fsdp"),
            P("fsdp"),
            P("fsdp"),
            P("fsdp"),
            P("fsdp"),
            P("fsdp"),
            P("fsdp"),
            P("fsdp"),
            P("fsdp"),
            P("fsdp"),
            P("fsdp"),
            P("fsdp"),
        ),
        check_vma=False,
    )
```

profile of v0, /device:TPU:0, one launch (start us, length us, event | category | flops | bytes accessed | tf_op | source)
XLA Modules:
  0.0 850.0 jit_solution(1238161921247626066)
XLA Ops:
  19.0 39.3 %all-reduce.23 = (bf16[384]{0:T(512)(128)(2,1)}, bf16[384]{0:T(512)(128)(2,1)S(1)}, bf16[384]{0:T(512)(128)(2,1)S(1)}, bf16[384]{0:T(512)(128)(2,1)S(1)}, bf16[3...) all-reduce(bf16[384]{0:T(512)(128)(2,1)S(1)} %dynamic-update-slice., ...), channel_id=1, replica_groups=mesh['fsdp'=8,'dp'=4] {'fsdp'}, use_global_device_ids=true, to_apply=%add.4 | all-reduce | flops 4608 | bytes 18432
  58.3 33.5 %all_gather.47 = bf16[442368]{0:T(1024)(128)(2,1)S(1)} all-gather(bf16[55296]{0:T(1024)(128)(2,1)} %param.23), channel_id=1, replica_groups=mesh['fsdp'=8,'dp'=4] {'fsdp'}, dimensions={0}, use_global_device_ids=true | all-gather | bytes 995328 | tf_op jit(solution)/shard_map/all_gather | solution.py:141
  105.1 8.5 %fusion.93 = (f32[4,512]{1,0:T(4,128)S(1)}, f32[4,512,2048]{2,1,0:T(8,128)}) fusion(bf16[512,4,96]{0,2,1:T(8,128)(2,1)} %bitcast.132, bf16[2048,4,96]{0,2,1:T(8,128)(2,1)S(1)} %bitcast.106, pred[512,2048]{1,0:T(8,128)(4,1)S(1)} %get-tuple-element.142), kind=kOutput, calls=%fused_computation.183 | convolution fusion | flops 817887232 | bytes 19800064 | tf_op jit(solution)/shard_map/qhd,khd->hqk/dot_general | solution.py:97
  122.4 8.2 fusion.65
  147.4 8.2 fusion.68
  163.1 8.1 fusion.2
  171.9 8.2 fusion.66
  187.8 8.1 fusion.1
  196.6 8.2 fusion.67
  209.4 32.8 %all_gather.50 = bf16[147456]{0:T(1024)(128)(2,1)} all-gather(bf16[18432]{0:T(1024)(128)(2,1)S(1)} %copy-done.47), channel_id=1, replica_groups=mesh['fsdp'=8,'dp'=4] {'fsdp'}, dimensions={0}, use_global_device_ids=true | all-gather | bytes 331776 | tf_op jit(solution)/shard_map/all_gather | solution.py:144
  254.0 35.1 %multiply_convert_fusion.4 = (bf16[2048,1536]{1,0:T(8,128)(2,1)}, f32[2048,1536]{1,0:T(8,128)}, f32[2048,1536]{1,0:T(8,128)}) fusion(f32[1536]{0:T(1024)S(1)} %convert_element_type.211, bf16[384,1536]{1,0:T(8,128)(2,1)} %reshape.348, f32[2048,384]{0,1:T(8,128)} %copy-done.8, f32[384]{0:T(512)S(1)} %convert_element_type.209, ...), kind=kOutput, calls=%fused_computation.35 | convolution fusion | flops 2627469312 | bytes 35808256 | tf_op jit(solution)/shard_map/dot_general | solution.py:29
  292.2 13.8 %fusion.100 = (f32[1536]{0:T(1024)}, bf16[2048,1536]{1,0:T(8,128)(2,1)S(1)}) fusion(f32[2048,1536]{1,0:T(8,128)} %get-tuple-element.119, bf16[1536,384]{1,0:T(8,128)(2,1)} %reshape.349, bf16[2048,384]{0,1:T(8,128)(2,1)S(1)} %copy-done.15, f32[2048]{0:T(1024)S(1)} %fusion.72, f32[2048,1536]{1,0:T(8,128)} %get-tuple-element.159, ...), kind=kOutput, calls=%fused_computation.190 | convolution fusion | flops 2468608512 | bytes 34230272 | tf_op jit(solution)/shard_map/dot_general | solution.py:39
  341.4 10.5 %multiply_convert_fusion.3 = bf16[4,512,2048]{2,1,0:T(8,128)(2,1)} fusion(f32[4,512,2048]{2,1,0:T(8,128)} %get-tuple-element.161, f32[4,512,2048]{2,1,0:T(8,128)S(1)} %bitcast.101, f32[4,512]{1,0:T(4,128)S(1)} %get-tuple-element.160, f32[4,512]{1,0:T(4,128)S(1)} %copy-done.40), kind=kLoop, calls=%fused_computation.10 | loop fusion | flops 16777216 | bytes 41959424 | tf_op jit(solution)/shard_map/convert_element_type | solution.py:264
  362.9 10.8 %fusion.18 = f32[4,96,2048]{2,1,0:T(8,128)} fusion(bf16[512,4,96]{0,2,1:T(8,128)(2,1)S(1)} %bitcast.138, f32[4,512,2048]{2,1,0:T(8,128)} %get-tuple-element.154, f32[4,512]{1,0:T(4,128)S(1)} %copy-done.42), kind=kOutput, calls=%fused_computation.52 | convolution fusion | flops 813694976 | bytes 20324352 | tf_op jit(solution)/shard_map/hqk,qhd->khd/dot_general | solution.py:259
  373.7 9.3 %multiply_reduce_fusion.2 = (f32[4,512]{1,0:T(4,128)S(1)}, f32[4,512,2048]{2,1,0:T(8,128)}) fusion(f32[4,512,2048]{2,1,0:T(8,128)S(1)} %bitcast.105, f32[4,512]{1,0:T(4,128)S(1)} %copy-done.42, bf16[512,4,96]{0,2,1:T(8,128)(2,1)S(1)} %bitcast.139, bf16[2048,4,96]{0,2,1:T(8,128)(2,1)} %bitcast.119), kind=kOutput, calls=%fused_computation.8 | convolution fusion | flops 817887232 | bytes 35536896 | tf_op jit(solution)/shard_map/qhd,khd->hqk/dot_general | solution.py:256
  383.1 15.8 %multiply_convert_fusion.2 = bf16[4,512,2048]{2,1,0:T(8,128)(2,1)} fusion(f32[4,512,2048]{2,1,0:T(8,128)} %get-tuple-element.163, f32[4,512,2048]{2,1,0:T(8,128)} %get-tuple-element.154, f32[4,512]{1,0:T(4,128)S(1)} %get-tuple-element.162, f32[4,512]{1,0:T(4,128)S(1)} %copy-done.42), kind=kLoop, calls=%fused_computation.7 | loop fusion | flops 16777216 | bytes 41959424 | tf_op jit(solution)/shard_map/convert_element_type | solution.py:264
  417.5 9.3 %multiply_reduce_fusion.1 = (f32[4,512]{1,0:T(4,128)S(1)}, f32[4,512,2048]{2,1,0:T(8,128)}) fusion(f32[4,512,2048]{2,1,0:T(8,128)S(1)} %bitcast.103, f32[4,512]{1,0:T(4,128)S(1)} %copy-done.41, bf16[512,4,96]{0,2,1:T(8,128)(2,1)S(1)} %bitcast.137, bf16[2048,4,96]{0,2,1:T(8,128)(2,1)} %bitcast.120), kind=kOutput, calls=%fused_computation.5 | convolution fusion | flops 817887232 | bytes 35536896 | tf_op jit(solution)/shard_map/qhd,khd->hqk/dot_general | solution.py:256
  426.8 15.8 %multiply_convert_fusion.1 = bf16[4,512,2048]{2,1,0:T(8,128)(2,1)} fusion(f32[4,512,2048]{2,1,0:T(8,128)} %get-tuple-element.165, f32[4,512,2048]{2,1,0:T(8,128)} %get-tuple-element.152, f32[4,512]{1,0:T(4,128)S(1)} %get-tuple-element.164, f32[4,512]{1,0:T(4,128)S(1)} %copy-done.41), kind=kLoop, calls=%fused_computation.4 | loop fusion | flops 16777216 | bytes 41959424 | tf_op jit(solution)/shard_map/convert_element_type | solution.py:264
  461.1 9.3 %multiply_reduce_fusion = (f32[4,512]{1,0:T(4,128)S(1)}, f32[4,512,2048]{2,1,0:T(8,128)}) fusion(f32[4,512,2048]{2,1,0:T(8,128)S(1)} %bitcast.99, f32[4,512]{1,0:T(4,128)S(1)} %copy-done.39, bf16[512,4,96]{0,2,1:T(8,128)(2,1)S(1)} %bitcast.135, bf16[2048,4,96]{0,2,1:T(8,128)(2,1)} %bitcast.121), kind=kOutput, calls=%fused_computation.2 | convolution fusion | flops 817887232 | bytes 35536896 | tf_op jit(solution)/shard_map/qhd,khd->hqk/dot_general | solution.py:256
  470.4 10.7 %multiply_convert_fusion = bf16[4,512,2048]{2,1,0:T(8,128)(2,1)} fusion(f32[4,512,2048]{2,1,0:T(8,128)} %get-tuple-element.167, f32[4,512,2048]{2,1,0:T(8,128)S(1)} %bitcast.99, f32[4,512]{1,0:T(4,128)S(1)} %get-tuple-element.166, f32[4,512]{1,0:T(4,128)S(1)} %copy-done.39), kind=kLoop, calls=%fused_computation.1 | loop fusion | flops 16777216 | bytes 41959424 | tf_op jit(solution)/shard_map/convert_element_type | solution.py:264
  488.8 12.6 %bitcast_convert_fusion = (bf16[2048,4,96]{0,2,1:T(8,128)(2,1)S(1)}, f32[4,96,2048]{2,1,0:T(8,128)}) fusion(f32[4,96,2048]{2,1,0:T(8,128)} %fusion.14, f32[4,96,2048]{2,1,0:T(8,128)} %fusion.16, f32[4,96,2048]{2,1,0:T(8,128)S(1)} %copy-done.11, bf16[512,4,96]{0,2,1:T(8,128)(2,1)S(1)} %bitcast.125, f32[4,512,2048]{2,1,0:T(8,128)} %get-tuple-element.156, ...), kind=kOutput, calls=%fused_computation.84 | convolution fusion | flops 816840704 | bytes 31334400 | tf_op jit(solution)/shard_map/hqk,qhd->khd/dot_general | solution.py:259
  542.5 255.5 %all-reduce.30 = (bf16[384]{0:T(512)(128)(2,1)S(1)}, bf16[384]{0:T(512)(128)(2,1)S(1)}, bf16[442368]{0:T(1024)(128)(2,1)}, bf16[384]{0:T(512)(128)(2,1)S(1)}, bf...) all-reduce(f32[384]{0:T(512)S(1)} %get-tuple-element.77, ...), channel_id=2, replica_groups=mesh['fsdp'=8,'dp'=4] {'fsdp'}, use_global_device_ids=true, to_apply=%region_24.25.clone | all-reduce | flops 1774080 | bytes 10644480
  812.2 12.1 %all-reduce.24 = (bf16[48]{0:T(256)(128)(2,1)S(1)}, bf16[48]{0:T(256)(128)(2,1)S(1)}, bf16[48]{0:T(256)(128)(2,1)S(1)}, bf16[48]{0:T(256)(128)(2,1)S(1)}, bf16[1...) all-reduce(bf16[48]{0:T(256)(128)(2,1)S(1)} %dynamic-slice.60, ...), channel_id=1, replica_groups=mesh['fsdp'=8,'dp'=4] {'dp'}, use_global_device_ids=true, to_apply=%region_25.26 | all-reduce | flops 19008 | bytes 76032 | tf_op jit(solution)/shard_map/psum | solution.py:325
  829.7 8.7 %all-reduce.29.cloned.1.call-done = (bf16[55296]{0:T(1024)(128)(2,1)}, bf16[73728]{0:T(1024)(128)(2,1)}, bf16[73728]{0:T(1024)(128)(2,1)}) async-done(((bf16[55296]{0:T(1024)(128)(2,1)}, bf16[73728]{0:T(1024)(128)(2,1)}, bf16[73728]{0:T(1024)(128)(2,1)}), (bf16[55296]{0:T(1024)(128)(2,1)}, bf16[73728]{0:T(1024)(128)(2,1)}, bf16[73728]{0:T(1024)(128)(2,1)})) %all-reduce.29.cloned.1.call-update) | async-done | bytes 405520 | tf_op jit(solution)/shard_map/psum | solution.py:327
  (334 shorter events, 237.7 us)
Async XLA Ops:
  7.2 243.3 %all-gather.3.cloned.1.call-start = ((), (), s32[]{:S(2)}) async-start(), calls=%async_computation | async-start | bytes 1327104 | tf_op jit(solution)/shard_map/all_gather | solution.py:148
  7.9 281.2 %all-gather.5.cloned.1.call-start = ((), (), s32[]{:S(2)}) async-start(), calls=%async_computation.1 | async-start | bytes 1327104 | tf_op jit(solution)/shard_map/all_gather | solution.py:150
  8.7 829.8 %all-reduce.29.cloned.1.call-start = ((), (), s32[]{:S(2)}) async-start(), calls=%async_computation.2 | async-start | bytes 811008 | tf_op jit(solution)/shard_map/psum | solution.py:327
  58.3 40.2 %copy-start.50 = (f32[384]{0:T(512)}, f32[384]{0:T(512)S(1)}, u32[]{:S(2)}) copy-start(f32[384]{0:T(512)S(1)} %convert_element_type.195) | copy-start | bytes 4612
  58.3 40.2 %copy-start.60 = (f32[384]{0:T(512)}, f32[384]{0:T(512)S(1)}, u32[]{:S(2)}) copy-start(f32[384]{0:T(512)S(1)} %convert_element_type.196) | copy-start | bytes 4612
  99.6 55.9 %copy-start.17 = (bf16[512,384]{0,1:T(8,128)(2,1)}, bf16[512,384]{0,1:T(8,128)(2,1)S(1)}, u32[]{:S(2)}) copy-start(bf16[512,384]{0,1:T(8,128)(2,1)S(1)} %get-tuple-element.122) | copy-start | bytes 1179652
  99.9 80.2 %copy-start = (bf16[2048,384]{0,1:T(8,128)(2,1)}, bf16[2048,384]{0,1:T(8,128)(2,1)S(1)}, u32[]{:S(2)}) copy-start(bf16[2048,384]{0,1:T(8,128)(2,1)S(1)} %get-tuple-element.124) | copy-start | bytes 4718596
  99.9 233.7 %copy-start.2 = (bf16[2048,384]{0,1:T(8,128)(2,1)}, bf16[2048,384]{0,1:T(8,128)(2,1)S(1)}, u32[]{:S(2)}) copy-start(bf16[2048,384]{0,1:T(8,128)(2,1)S(1)} %get-tuple-element.125) | copy-start | bytes 4718596
  196.6 49.3 %copy-start.5 = (bf16[2048,384]{0,1:T(8,128)(2,1)S(1)}, bf16[2048,384]{0,1:T(8,128)(2,1)}, u32[]{:S(2)}) copy-start(bf16[2048,384]{0,1:T(8,128)(2,1)} %copy-done.4) | copy-start | bytes 4718596
  209.3 115.1 %copy-start.48 = (f32[2048]{0:T(1024)}, f32[2048]{0:T(1024)S(1)}, u32[]{:S(2)}) copy-start(f32[2048]{0:T(1024)S(1)} %fusion.72) | copy-start | bytes 24580
  254.0 38.2 %copy-start.15 = (bf16[2048,384]{0,1:T(8,128)(2,1)S(1)}, bf16[2048,384]{0,1:T(8,128)(2,1)}, u32[]{:S(2)}) copy-start(bf16[2048,384]{0,1:T(8,128)(2,1)} %copy.61) | copy-start | bytes 4718596
  292.2 13.8 %copy-start.35 = (bf16[384,1536]{1,0:T(8,128)(2,1)S(1)}, bf16[384,1536]{1,0:T(8,128)(2,1)}, u32[]{:S(2)}) copy-start(bf16[384,1536]{1,0:T(8,128)(2,1)} %reshape.348) | copy-start | bytes 3538948
  319.7 13.8 %slice-start.4 = ((s8[16777216]{0:T(1024)(128)(4,1)}), s8[4194304]{0:T(1024)(128)(4,1)S(1)}, s32[]{:S(2)}) async-start(s8[16777216]{0:T(1024)(128)(4,1)} %bitcast.100), calls=%async_computation.7 | async-start | bytes 8388608
  359.7 14.0 %slice-start.12 = ((s8[16777216]{0:T(1024)(128)(4,1)}), s8[4194304]{0:T(1024)(128)(4,1)S(1)}, s32[]{:S(2)}) async-start(s8[16777216]{0:T(1024)(128)(4,1)} %bitcast.104), calls=%async_computation.15 | async-start | bytes 8388608
  359.7 14.0 %slice-start.13 = ((s8[16777216]{0:T(1024)(128)(4,1)}), s8[4194304]{0:T(1024)(128)(4,1)S(1)}, s32[]{:S(2)}) async-start(s8[16777216]{0:T(1024)(128)(4,1)} %bitcast.104), calls=%async_computation.16 | async-start | bytes 8388608
  383.1 29.9 %slice-start.8 = ((s8[16777216]{0:T(1024)(128)(4,1)}), s8[4194304]{0:T(1024)(128)(4,1)S(1)}, s32[]{:S(2)}) async-start(s8[16777216]{0:T(1024)(128)(4,1)} %bitcast.102), calls=%async_computation.11 | async-start | bytes 8388608
  383.1 29.9 %slice-start.9 = ((s8[16777216]{0:T(1024)(128)(4,1)}), s8[4194304]{0:T(1024)(128)(4,1)S(1)}, s32[]{:S(2)}) async-start(s8[16777216]{0:T(1024)(128)(4,1)} %bitcast.102), calls=%async_computation.12 | async-start | bytes 8388608
  383.1 29.9 %slice-start.10 = ((s8[16777216]{0:T(1024)(128)(4,1)}), s8[4194304]{0:T(1024)(128)(4,1)S(1)}, s32[]{:S(2)}) async-start(s8[16777216]{0:T(1024)(128)(4,1)} %bitcast.102), calls=%async_computation.13 | async-start | bytes 8388608
  398.9 14.1 %slice-start.11 = ((s8[16777216]{0:T(1024)(128)(4,1)}), s8[4194304]{0:T(1024)(128)(4,1)S(1)}, s32[]{:S(2)}) async-start(s8[16777216]{0:T(1024)(128)(4,1)} %bitcast.102), calls=%async_computation.14 | async-start | bytes 8388608
  426.8 30.0 %slice-start = ((s8[16777216]{0:T(1024)(128)(4,1)}), s8[4194304]{0:T(1024)(128)(4,1)S(1)}, s32[]{:S(2)}) async-start(s8[16777216]{0:T(1024)(128)(4,1)} %bitcast.98), calls=%async_computation.3 | async-start | bytes 8388608
  426.8 30.0 %slice-start.1 = ((s8[16777216]{0:T(1024)(128)(4,1)}), s8[4194304]{0:T(1024)(128)(4,1)S(1)}, s32[]{:S(2)}) async-start(s8[16777216]{0:T(1024)(128)(4,1)} %bitcast.98), calls=%async_computation.4 | async-start | bytes 8388608
  426.8 30.0 %slice-start.2 = ((s8[16777216]{0:T(1024)(128)(4,1)}), s8[4194304]{0:T(1024)(128)(4,1)S(1)}, s32[]{:S(2)}) async-start(s8[16777216]{0:T(1024)(128)(4,1)} %bitcast.98), calls=%async_computation.5 | async-start | bytes 8388608
  442.6 14.1 %slice-start.3 = ((s8[16777216]{0:T(1024)(128)(4,1)}), s8[4194304]{0:T(1024)(128)(4,1)S(1)}, s32[]{:S(2)}) async-start(s8[16777216]{0:T(1024)(128)(4,1)} %bitcast.98), calls=%async_computation.6 | async-start | bytes 8388608
  481.1 20.3 %slice-start.16 = ((s8[8388608]{0:T(1024)(128)(4,1)}), s8[4194304]{0:T(1024)(128)(4,1)S(1)}, s32[]{:S(2)}) async-start(s8[8388608]{0:T(1024)(128)(4,1)} %bitcast.122), calls=%async_computation.19 | async-start | bytes 8388608
  (72 other events, 482.2 us)
Sparse Core Ops, SparseCore 0:
  10.2 44.2 all-gather.2
  56.6 42.9 all-gather.4
  802.8 35.5 all-reduce.28
where the time goes:
time: 854 us; the launch traced here: 850 us
  blocking collectives  373 us (44%)
  matrix products  269 us (31%)
  other arithmetic  124 us (15%)
  local copies, waits for them, and re-layouts  54.4 us (6%)
  between operations  19.7 us (2%)
  waiting for transfers between devices  10.2 us (1%)
    unnamed x2, blocking collectives  295 us
    convert_element_type x4, other arithmetic, body(): grad_scores = (probs_full * (grad_probs - jnp.sum(probs_full * grad_probs...  52.8 us
    dot_general x4, matrix products, product(): return jnp.dot(former, latter, preferred_element_type=jnp.float32)  44.3 us
    dot_general x4, matrix products, body(): jnp.einsum('qhd,khd->hqk', grad_block, values_all, preferred_element_type...  35.8 us
    all_gather x1, blocking collectives, body(): lax.all_gather(w_qkv, 'fsdp', axis=0, tiled=True)  33.5 us
    dot_general x4, matrix products, body(): jnp.einsum('hqk,khd->qhd', probs_low, values_all, preferred_element_type=...  32.9 us
    all_gather x1, blocking collectives, body(): lax.all_gather(w_proj, 'fsdp', axis=0, tiled=True)  32.8 us
    reduce_sum x4, other arithmetic, body(): row_sum = jnp.sum(exponent, axis=-1, keepdims=True)  32.5 us
  transfers between devices with their start and end apart: 3, of which 1 were waited for; matrix products, arithmetic and copies ran while one was open for 22% of the time, Pallas kernels for 0%

commit v1 on v0

v1 whole, which is shorter than its diff:
```python
from functools import partial
import math

import jax
import jax.numpy as jnp
from jax import lax
from jax.experimental import pallas as pl
from jax.experimental.pallas import tpu as pltpu
from jax.sharding import PartitionSpec as P

HEAD_DIM = 96
HEAD_PAD = 128
LENS = (196, 256, 400)
SLOT = 400
ROW_PAD = 32
VEC = 128
SCALE = 1.0 / math.sqrt(HEAD_DIM)
EXP_SCALE = SCALE * math.log2(math.e)
VMEM_LIMIT = 56 * 1024 * 1024
F32 = jnp.float32
BF16 = jnp.bfloat16


def dot_nn(a, b):
    return lax.dot_general(a, b, (((1,), (0,)), ((), ())), preferred_element_type=F32)


def dot_nt(a, b):
    return lax.dot_general(a, b, (((1,), (1,)), ((), ())), preferred_element_type=F32)


def dot_tn(a, b):
    return lax.dot_general(a, b, (((0,), (0,)), ((), ())), preferred_element_type=F32)


def pad_heads(values):
    rows, cols = values.shape
    gap = jnp.zeros((rows, HEAD_PAD - HEAD_DIM), values.dtype)
    parts = []
    for h in range(cols // HEAD_DIM):
        parts += [values[:, h * HEAD_DIM : (h + 1) * HEAD_DIM], gap]
    return jnp.concatenate(parts, axis=1)


def unpad_heads(values):
    rows, cols = values.shape
    return jnp.concatenate(
        [values[:, h * HEAD_PAD : h * HEAD_PAD + HEAD_DIM] for h in range(cols // HEAD_PAD)], axis=1
    )


def row_norm(x):
    center = x - jnp.mean(x, axis=-1, keepdims=True)
    inverse = lax.rsqrt(jnp.mean(center * center, axis=-1, keepdims=True) + 1e-6)
    return center * inverse, inverse


def row_norm_back(e, xhat, inverse):
    return inverse * (
        e - jnp.mean(e, axis=-1, keepdims=True) - xhat * jnp.mean(e * xhat, axis=-1, keepdims=True)
    )


def load_rows(ref, start, count):
    base = pl.multiple_of((start // 8) * 8, 8)
    window = ref[pl.ds(base, count + 8), :]
    moved = pltpu.roll(window, count + 4, 0)
    return jnp.where(start % 8 == 0, window, moved)[:count]


def store_rows(ref, start, length, values, cols):
    count = -(-length // 8) * 8
    base = pl.multiple_of((start // 8) * 8, 8)
    window = jnp.concatenate([values[:count], jnp.zeros((8, values.shape[1]), values.dtype)], axis=0)
    window = jnp.where(start % 8 == 0, window, pltpu.roll(window, 4, 0))
    row = lax.broadcasted_iota(jnp.int32, window.shape, 0) - start % 8
    held = ref[pl.ds(base, count + 8), cols]
    ref[pl.ds(base, count + 8), cols] = jnp.where((row >= 0) & (row < length), window, held)


def by_group(group, work):
    for g, length in enumerate(LENS):
        pl.when(group == g)(partial(work, length, -(-length // 16) * 16))


def attn_fwd_kernel(meta, tok, w1, attn, qkv, lse, wpad, tok32, out32, bias, *, heads):
    i = pl.program_id(0)
    rows, width = tok.shape
    hp = heads * HEAD_PAD

    @pl.when(i == 0)
    def _():
        tok32[:rows] = tok[...].astype(F32)
        tok32[rows:] = jnp.zeros((tok32.shape[0] - rows, width), F32)
        out32[...] = jnp.zeros(out32.shape, F32)
        wpad[...] = pad_heads(w1[:, : 3 * width].astype(F32)).astype(BF16)
        vec = w1[:, 3 * width :].astype(F32).T
        bias[0:1, :width] = vec[0:1]
        bias[1:2, :width] = vec[1:2]
        bias[2:3, :] = jnp.concatenate(
            [pad_heads(vec[2:3]), jnp.zeros((1, hp), F32), pad_heads(vec[3:4])], axis=1
        )

    start = meta[i]

    def work(length, padded):
        x = load_rows(tok32, start, padded)
        xhat, _ = row_norm(x)
        normed = (xhat * bias[0:1, :width] + bias[1:2, :width]).astype(BF16)
        qkv[0, :padded, :] = (dot_nn(normed, wpad[...]) + bias[2:3, :]).astype(BF16)
        for h in range(heads):
            at = h * HEAD_PAD
            q = qkv[0, :padded, at : at + HEAD_PAD]
            k = qkv[0, :padded, hp + at : hp + at + HEAD_PAD]
            v = qkv[0, :padded, 2 * hp + at : 2 * hp + at + HEAD_PAD]
            s = dot_nt(k, q)
            if length < padded:
                key = lax.broadcasted_iota(jnp.int32, s.shape, 0)
                s = jnp.where(key < length, s, -1e30)
            top = jnp.max(s, axis=0, keepdims=True)
            e = jnp.exp2((s - top) * EXP_SCALE)
            total = jnp.sum(e, axis=0, keepdims=True)
            p = (e * (1.0 / total)).astype(BF16)
            lse[0, h : h + 1, :padded] = top * EXP_SCALE + jnp.log2(total)
            o = dot_tn(p, v)
            store_rows(out32, start, length, o, pl.ds(at, HEAD_PAD))

    by_group(meta[8 + i], work)

    @pl.when(i == pl.num_programs(0) - 1)
    def _():
        attn[...] = out32[:rows].astype(BF16)


def attn_fwd(meta, tokens, w1):
    rows, width = tokens.shape
    heads = width // HEAD_DIM
    hp = heads * HEAD_PAD
    slots = (meta.shape[0] - 1) // 2
    return pl.pallas_call(
        partial(attn_fwd_kernel, heads=heads),
        grid_spec=pltpu.PrefetchScalarGridSpec(
            num_scalar_prefetch=1,
            grid=(slots,),
            in_specs=[
                pl.BlockSpec((rows, width), lambda i, m: (0, 0)),
                pl.BlockSpec(w1.shape, lambda i, m: (0, 0)),
            ],
            out_specs=[
                pl.BlockSpec((rows, hp), lambda i, m: (0, 0)),
                pl.BlockSpec((1, SLOT, 3 * hp), lambda i, m: (i, 0, 0)),
                pl.BlockSpec((1, 8, 512), lambda i, m: (i, 0, 0)),
                pl.BlockSpec((width, 3 * hp), lambda i, m: (0, 0)),
            ],
            scratch_shapes=[
                pltpu.VMEM((rows + ROW_PAD, width), F32),
                pltpu.VMEM((rows + ROW_PAD, hp), F32),
                pltpu.VMEM((8, 3 * hp), F32),
            ],
        ),
        out_shape=[
            jax.ShapeDtypeStruct((rows, hp), BF16),
            jax.ShapeDtypeStruct((slots, SLOT, 3 * hp), BF16),
            jax.ShapeDtypeStruct((slots, 8, 512), F32),
            jax.ShapeDtypeStruct((width, 3 * hp), BF16),
        ],
        compiler_params=pltpu.CompilerParams(vmem_limit_bytes=VMEM_LIMIT),
        name="attn_fwd",
    )(meta, tokens, w1)


INV_SQRT2 = 1.0 / math.sqrt(2.0)
ERF = (0.254829592, -0.284496736, 1.421413741, -1.453152027, 1.061405429)
ERF_T = 0.3275911


def gelu_pair(u):
    tail = 1.0 / (1.0 + (ERF_T * INV_SQRT2) * jnp.abs(u))
    poly = ERF[4] * tail + ERF[3]
    for c in (ERF[2], ERF[1], ERF[0]):
        poly = poly * tail + c
    bell = jnp.exp2((u * u) * (-0.5 * math.log2(math.e)))
    half = (0.5 * tail) * poly * bell
    cdf = jnp.where(u >= 0, 1.0 - half, half)
    return u * cdf, cdf + u * (bell * (1.0 / math.sqrt(2.0 * math.pi)))


def mlp_kernel(
    meta, tok, cot, attn, w2, out, dx1, dattn, grads, wproj, rowvec, gd, gu, gp, gsum, *, heads, chunk
):
    i = pl.program_id(0)
    rows, width = tok.shape
    hp = heads * HEAD_PAD
    hidden = 4 * width

    @pl.when(i == 0)
    def _():
        proj = w2[:, :width]
        wproj[...] = jnp.zeros(wproj.shape, BF16)
        for h in range(heads):
            wproj[h * HEAD_PAD : h * HEAD_PAD + HEAD_DIM] = proj[h * HEAD_DIM : (h + 1) * HEAD_DIM]
        vec = w2[:, width + 2 * hidden :].astype(F32).T
        for r in range(4):
            rowvec[r : r + 1, :width] = vec[r : r + 1]
            rowvec[4:5, r * width : (r + 1) * width] = vec[4 + r : 5 + r]
        gd[...] = jnp.zeros(gd.shape, F32)
        gu[...] = jnp.zeros(gu.shape, F32)
        gp[...] = jnp.zeros(gp.shape, F32)
        gsum[...] = jnp.zeros(gsum.shape, F32)

    proj_bias, gain, shift, down_bias = [rowvec[r : r + 1, :width] for r in range(4)]
    row = lax.broadcasted_iota(jnp.int32, (rows, 1), 0) + i * rows
    valid = (row < meta[16]).astype(F32)
    attn_rows = attn[...]
    x1 = tok[...].astype(F32) + dot_nn(attn_rows, wproj[...]) + proj_bias
    xhat, inverse = row_norm(x1)
    normed = (xhat * gain + shift).astype(BF16)
    dy = cot[...].astype(F32) * valid
    dyb = dy.astype(BF16)
    y = x1 + down_bias
    dn = jnp.zeros((rows, width), F32)
    for c in range(hidden // chunk):
        at = c * chunk
        up = w2[:, width + at : width + at + chunk]
        pre = dot_nn(normed, up) + rowvec[4:5, at : at + chunk]
        act, slope = gelu_pair(pre)
        actb = act.astype(BF16)
        if chunk <= width:
            blk, off = divmod(at, width)
            base = width + hidden + blk * width
            down = w2[off : off + chunk, base : base + width]
            y = y + dot_nn(actb, down)
            dact = dot_nt(dyb, down)
        dpre = dact * slope
        dpreb = dpre.astype(BF16)
        gd[at : at + chunk, :] += dot_tn(actb, dyb)
        gu[:, at : at + chunk] += dot_tn(normed, dpreb)
        gsum[4:5, at : at + chunk] += jnp.sum(dpre, axis=0, keepdims=True)
        dn = dn + dot_nt(dpreb, up)
    out[...] = (y * valid).astype(BF16)
    dx = dy + row_norm_back(dn * gain, xhat, inverse)
    dx1[...] = dx
    dxb = dx.astype(BF16)
    gp[...] += dot_tn(attn_rows, dxb)
    dattn[...] = dot_nt(dxb, wproj[...]).astype(BF16)
    gsum[0:1, :width] += jnp.sum(dx, axis=0, keepdims=True)
    gsum[1:2, :width] += jnp.sum(dn * xhat, axis=0, keepdims=True)
    gsum[2:3, :width] += jnp.sum(dn, axis=0, keepdims=True)
    gsum[3:4, :width] += jnp.sum(dy, axis=0, keepdims=True)

    @pl.when(i == pl.num_programs(0) - 1)
    def _():
        for h in range(heads):
            grads[h * HEAD_DIM : (h + 1) * HEAD_DIM, :width] = gp[
                h * HEAD_PAD : h * HEAD_PAD + HEAD_DIM
            ].astype(BF16)
        grads[:, width : width + hidden] = gu[...].astype(BF16)
        for c in range(4):
            base = width + hidden + c * width
            grads[:, base : base + width] = gd[c * width : (c + 1) * width].astype(BF16)
        vec = jnp.concatenate(
            [gsum[0:4, :width]]
            + [gsum[4:5, c * width : (c + 1) * width] for c in range(4)]
            + [jnp.zeros((120, width), F32)],
            axis=0,
        )
        grads[:, width + 2 * hidden :] = vec.T.astype(BF16)


def mlp(meta, tokens, cotangent, attn, w2, block=256, chunk=384):
    rows, width = tokens.shape
    heads = width // HEAD_DIM
    hp = heads * HEAD_PAD
    hidden = 4 * width
    by_row = lambda cols: pl.BlockSpec((block, cols), lambda i, m: (i, 0))
    return pl.pallas_call(
        partial(mlp_kernel, heads=heads, chunk=chunk),
        grid_spec=pltpu.PrefetchScalarGridSpec(
            num_scalar_prefetch=1,
            grid=(rows // block,),
            in_specs=[
                by_row(width),
                by_row(width),
                by_row(hp),
                pl.BlockSpec(w2.shape, lambda i, m: (0, 0)),
            ],
            out_specs=[
                by_row(width),
                by_row(width),
                by_row(hp),
                pl.BlockSpec(w2.shape, lambda i, m: (0, 0)),
            ],
            scratch_shapes=[
                pltpu.VMEM((hp, width), BF16),
                pltpu.VMEM((8, hidden), F32),
                pltpu.VMEM((hidden, width), F32),
                pltpu.VMEM((width, hidden), F32),
                pltpu.VMEM((hp, width), F32),
                pltpu.VMEM((8, hidden), F32),
            ],
        ),
        out_shape=[
            jax.ShapeDtypeStruct((rows, width), BF16),
            jax.ShapeDtypeStruct((rows, width), F32),
            jax.ShapeDtypeStruct((rows, hp), BF16),
            jax.ShapeDtypeStruct(w2.shape, BF16),
        ],
        compiler_params=pltpu.CompilerParams(vmem_limit_bytes=VMEM_LIMIT),
        name="mlp",
    )(meta, tokens, cotangent, attn, w2)


def attn_bwd_kernel(
    meta, tok, qkv, lse, dattn, dx1, wpad, w1, din, grads, tok32, da32, gw, gsum, dq, bias, *, heads
):
    i = pl.program_id(0)
    rows, width = tok.shape
    hp = heads * HEAD_PAD

    @pl.when(i == 0)
    def _():
        tok32[:rows] = tok[...].astype(F32)
        tok32[rows:] = jnp.zeros((tok32.shape[0] - rows, width), F32)
        da32[:rows] = dattn[...].astype(F32)
        da32[rows:] = jnp.zeros((da32.shape[0] - rows, hp), F32)
        vec = w1[:, 3 * width :].astype(F32).T
        bias[0:1, :width] = vec[0:1]
        gw[...] = jnp.zeros(gw.shape, F32)
        gsum[...] = jnp.zeros(gsum.shape, F32)

    start = meta[i]

    def work(length, padded):
        da = load_rows(da32, start, padded)
        if length < padded:
            keep = lax.broadcasted_iota(jnp.int32, (padded, 1), 0) < length
            da = jnp.where(keep, da, 0.0)
        da = da.astype(BF16)
        for h in range(heads):
            at = h * HEAD_PAD
            q = qkv[0, :padded, at : at + HEAD_PAD]
            k = qkv[0, :padded, hp + at : hp + at + HEAD_PAD]
            v = qkv[0, :padded, 2 * hp + at : 2 * hp + at + HEAD_PAD]
            dah = da[:, at : at + HEAD_PAD]
            s = dot_nt(k, q)
            p = jnp.exp2(s * EXP_SCALE - lse[0, h : h + 1, :padded])
            if length < padded:
                key = lax.broadcasted_iota(jnp.int32, s.shape, 0)
                p = jnp.where(key < length, p, 0.0)
            dp = dot_nt(v, dah)
            mean = jnp.sum(p * dp, axis=0, keepdims=True)
            ds = (p * (dp - mean)).astype(BF16)
            dv = dot_nn(p.astype(BF16), dah)
            dk = dot_nn(ds, q) * SCALE
            dqh = dot_tn(ds, k) * SCALE
            gsum[2:3, at : at + HEAD_PAD] += jnp.sum(dqh, axis=0, keepdims=True)
            gsum[2:3, 2 * hp + at : 2 * hp + at + HEAD_PAD] += jnp.sum(dv, axis=0, keepdims=True)
            dq[:padded, at : at + HEAD_PAD] = dqh.astype(BF16)
            dq[:padded, hp + at : hp + at + HEAD_PAD] = dk.astype(BF16)
            dq[:padded, 2 * hp + at : 2 * hp + at + HEAD_PAD] = dv.astype(BF16)
        xhat, inverse = row_norm(load_rows(tok32, start, padded))
        gain = bias[0:1, :width]
        d = dq[:padded, :]
        gw[...] += dot_tn(xhat.astype(BF16), d)
        gsum[3:4, :] += jnp.sum(d.astype(F32), axis=0, keepdims=True)
        dn = dot_nt(d, wpad[...])
        dx = row_norm_back(dn * gain, xhat, inverse)
        base = pl.multiple_of((start // 8) * 8, 8)
        store_rows(da32, start, length, dx, pl.ds(0, width))

    by_group(meta[8 + i], work)

    @pl.when(i == pl.num_programs(0) - 1)
    def _():
        row = lax.broadcasted_iota(jnp.int32, (rows, 1), 0)
        din[...] = jnp.where(row < meta[16], dx1[...] + da32[:rows, :width], 0.0).astype(BF16)
        vec = w1[:, 3 * width :].astype(F32)
        w = wpad[...].astype(F32)
        raw = gw[...]
        col = gsum[3:4, :]
        gain_term = jnp.sum(raw * w, axis=1, keepdims=True)
        bias_term = jnp.sum(col * w, axis=1, keepdims=True)
        g = raw * vec[:, 0:1] + vec[:, 1:2] * col
        grads[:, : 3 * width] = unpad_heads(g).astype(BF16)
        sums = jnp.concatenate(
            [
                unpad_heads(gsum[2:3, :hp]),
                unpad_heads(gsum[2:3, 2 * hp :]),
                jnp.zeros((126, width), F32),
            ],
            axis=0,
        ).T
        lane = lax.broadcasted_iota(jnp.int32, (width, 128), 1)
        moved = pltpu.roll(sums, 2, 1)
        tail = jnp.where(lane == 0, gain_term, jnp.where(lane == 1, bias_term, moved))
        grads[:, 3 * width :] = tail.astype(BF16)


def attn_bwd(meta, tokens, qkv, lse, dattn, dx1, wpad, w1):
    rows, width = tokens.shape
    heads = width // HEAD_DIM
    hp = heads * HEAD_PAD
    slots = (meta.shape[0] - 1) // 2
    whole = lambda a: pl.BlockSpec(a.shape, lambda i, m: (0, 0))
    return pl.pallas_call(
        partial(attn_bwd_kernel, heads=heads),
        grid_spec=pltpu.PrefetchScalarGridSpec(
            num_scalar_prefetch=1,
            grid=(slots,),
            in_specs=[
                whole(tokens),
                pl.BlockSpec((1, SLOT, 3 * hp), lambda i, m: (i, 0, 0)),
                pl.BlockSpec((1, 8, 512), lambda i, m: (i, 0, 0)),
                whole(dattn),
                whole(dx1),
                whole(wpad),
                whole(w1),
            ],
            out_specs=[whole(tokens), whole(w1)],
            scratch_shapes=[
                pltpu.VMEM((rows + ROW_PAD, width), F32),
                pltpu.VMEM((rows + ROW_PAD, hp), F32),
                pltpu.VMEM((width, 3 * hp), F32),
                pltpu.VMEM((8, 3 * hp), F32),
                pltpu.VMEM((SLOT, 3 * hp), BF16),
                pltpu.VMEM((8, 3 * hp), F32),
            ],
        ),
        out_shape=[
            jax.ShapeDtypeStruct((rows, width), BF16),
            jax.ShapeDtypeStruct(w1.shape, BF16),
        ],
        compiler_params=pltpu.CompilerParams(vmem_limit_bytes=VMEM_LIMIT),
        name="attn_bwd",
    )(meta, tokens, qkv, lse, dattn, dx1, wpad, w1)


def swap(value, axis, bit):
    size = lax.axis_size(axis)
    return lax.ppermute(value, axis, [(i, i ^ bit) for i in range(size)])


def bit_of(axis, bit):
    return (lax.axis_index(axis) & bit) != 0


def halves(value, axis, dim):
    size = value.shape[dim] // 2
    low = lax.slice_in_dim(value, 0, size, axis=dim)
    high = lax.slice_in_dim(value, size, 2 * size, axis=dim)
    return low, high


def split_by(value, axis, bit, dim):
    low, high = halves(value, axis, dim)
    mine = bit_of(axis, bit)
    return jnp.where(mine, high, low), jnp.where(mine, low, high)


def join_by(own, other, axis, bit, dim):
    mine = bit_of(axis, bit)
    return jnp.where(
        mine,
        jnp.concatenate([other, own], axis=dim),
        jnp.concatenate([own, other], axis=dim),
    )


def bits_of(axis):
    size = lax.axis_size(axis)
    return [1 << b for b in range(size.bit_length() - 1)]


def gather_rows(shard):
    rows, cols = shard.shape
    part, _ = split_by(shard, "dp", 1, 1)
    part = part[None]
    for bit in bits_of("fsdp")[1:]:
        part = join_by(part, swap(part, "fsdp", bit), "fsdp", bit, 0)
    part = join_by(part[:, None], swap(part, "fsdp", 1)[:, None], "fsdp", 1, 1)
    part = part.reshape(-1, cols // 2)
    return join_by(part, swap(part, "dp", 1), "dp", 1, 1)


def sum_half(value, axis, bit, dim):
    keep, send = split_by(value, axis, bit, dim)
    got = swap(send, axis, bit)
    return (keep.astype(F32) + got.astype(F32)).astype(BF16)


def reduce_rows(value):
    size = lax.axis_size("fsdp")
    rows, cols = value.shape
    part = sum_half(value, "dp", 1, 1)
    part = part.reshape(size, rows // size, cols // 2)
    for bit in bits_of("dp")[1:]:
        part = sum_half(part, "dp", bit, 1)
    part = part.reshape(size // 2, 2, *part.shape[1:])
    part = sum_half(part, "fsdp", 1, 1)
    part = part.reshape(part.shape[0], *part.shape[2:])
    for bit in reversed(bits_of("fsdp")[1:]):
        part = sum_half(part, "fsdp", bit, 0)
    part = part[0]
    for bit in reversed(bits_of("dp")[1:]):
        part = join_by(part, swap(part, "dp", bit), "dp", bit, 0)
    return join_by(part, swap(part, "dp", 1), "dp", 1, 1)


def image_table(size_group, assignment, device, slots):
    owned = assignment == device
    rank = jnp.cumsum(owned.astype(jnp.int32)) - 1
    slot = jnp.arange(slots, dtype=jnp.int32)
    here = owned[None, :] & (rank[None, :] == slot[:, None])
    groups = jnp.sum(jnp.where(here, size_group[None, :], 0), axis=1)
    lengths = jnp.where(groups == 0, LENS[0], jnp.where(groups == 1, LENS[1], LENS[2]))
    ends = jnp.sum(jnp.where(slot[None, :] <= slot[:, None], lengths[None, :], 0), axis=1)
    return jnp.concatenate([ends - lengths, groups, ends[-1:]]).astype(jnp.int32)


def column(vector, size):
    return vector.reshape(-1, size).T


def body(
    tokens,
    cotangent,
    size_group,
    assignment,
    ln1_gain,
    ln1_bias,
    w_qkv,
    q_bias,
    v_bias,
    w_proj,
    proj_bias,
    ln2_gain,
    ln2_bias,
    w_up,
    up_bias,
    w_down,
    down_bias,
):
    width = tokens.shape[1]
    shards = lax.axis_size("fsdp")
    size = width // shards
    ratio = up_bias.shape[0] // size
    hidden = ratio * width
    devices = shards * lax.axis_size("dp")
    device = lax.axis_index("fsdp") * lax.axis_size("dp") + lax.axis_index("dp")
    table = image_table(size_group, assignment, device, size_group.shape[0] // devices)

    first = jnp.concatenate(
        [w_qkv.reshape(size, 3 * width)]
        + [column(v, size) for v in (ln1_gain, ln1_bias, q_bias, v_bias)]
        + [jnp.zeros((size, VEC - 4), BF16)],
        axis=1,
    )
    up = w_up.reshape(size, shards, ratio, size).transpose(0, 2, 1, 3).reshape(size, hidden)
    down = w_down.reshape(ratio, size, width)
    second = jnp.concatenate(
        [w_proj.reshape(size, width), up]
        + [down[c] for c in range(ratio)]
        + [column(v, size) for v in (proj_bias, ln2_gain, ln2_bias, down_bias, up_bias)]
        + [jnp.zeros((size, VEC - 4 - ratio), BF16)],
        axis=1,
    )
    first = gather_rows(first)
    second = gather_rows(second)

    attn, qkv, lse, padded = attn_fwd(table, tokens, first)
    layer_out, dx1, dattn, grad_second = mlp(table, tokens, cotangent, attn, second)
    grad_second = reduce_rows(grad_second).astype(F32)
    grad_input, grad_first = attn_bwd(table, tokens, qkv, lse, dattn, dx1, padded, first)
    grad_first = reduce_rows(grad_first).astype(F32)

    one = lambda r: grad_first[:, 3 * width + r]
    base = width + 2 * hidden
    two = lambda r: grad_second[:, base + r]
    grad_up = grad_second[:, width : width + hidden]
    grad_up = grad_up.reshape(size, ratio, shards, size).transpose(0, 2, 1, 3).reshape(-1)
    grad_down = grad_second[:, width + hidden : base].reshape(size, ratio, width)
    grad_up_bias = grad_second[:, base + 4 : base + 4 + ratio].T.reshape(-1)
    return (
        layer_out,
        grad_input,
        one(0),
        one(1),
        grad_first[:, : 3 * width].reshape(-1),
        one(2),
        one(3),
        grad_second[:, :width].reshape(-1),
        two(0),
        two(1),
        two(2),
        grad_up,
        grad_up_bias,
        grad_down.transpose(1, 0, 2).reshape(-1),
        two(3),
    )


def solution(mesh):
    rows = P(("fsdp", "dp"), None)
    flat = P("fsdp")
    return jax.shard_map(
        body,
        mesh=mesh,
        in_specs=(rows, rows, P(), P()) + (flat,) * 13,
        out_specs=(rows, rows) + (flat,) * 13,
        check_vma=False,
    )
```

time: 854 us -> 225 us (0.26)
  blocking collectives: 373 us -> 0 us
  matrix products: 269 us -> 0 us
  other arithmetic: 124 us -> 15.1 us
  Pallas kernels: 0 us -> 96.3 us
  waiting for transfers between devices: 10.2 us -> 74 us
  local copies, waits for them, and re-layouts: 54.4 us -> 16 us
  starting transfers between devices: 0.11 us -> 21.6 us
  between operations: 19.7 us -> 1.13 us
    unnamed x2 -> x0, blocking collectives: 295 us -> none
    dot_general x36 -> x0, matrix products: 269 us -> none  [the longest x4 44.3 us: product(): return jnp.dot(former, latter, preferred_element_type=jnp.float32)]
    pallas_call x0 -> x3, Pallas kernels: none -> 96.3 us  [the longest x1 47 us: mlp(): pl.pallas_call(partial(mlp_kernel, heads=heads, chunk=chunk), grid_spec=p...]
    ppermute x0 -> x22, waiting for transfers between devices: none -> 74 us  [swap(): return lax.ppermute(value, axis, [(i, i ^ bit) for i in range(size)])]
    all_gather x2 -> x0, blocking collectives: 66.3 us -> none  [the longest x1 33.5 us: body(): lax.all_gather(w_qkv, 'fsdp', axis=0, tiled=True)]
    convert_element_type x28 -> x10, other arithmetic: 68.1 us -> 3.95 us  [the longest x8 3.81 us: sum_half(): return (keep.astype(F32) + got.astype(F32)).astype(BF16)]
    reduce_sum x13 -> x2, other arithmetic: 49 us -> 0.23 us  [the longest x1 0.12 us: image_table(): groups = jnp.sum(jnp.where(here, size_group[None, :], 0), axis=1)]
    unnamed x222 -> x16, local copies, waits for them, and re-layouts: 25.9 us -> 0.54 us
  transfers between devices with their start and end apart: 3 -> 22, of which waited for: 1 -> 14; matrix products, arithmetic and copies ran while one was open for 22% -> 6% of each run, Pallas kernels for 0% -> 22%
where the time goes in v1:
time: 225 us; the launch traced here: 224 us
  Pallas kernels  96.3 us (43%)
  waiting for transfers between devices  74 us (33%)
  starting transfers between devices  21.6 us (10%)
  local copies, waits for them, and re-layouts  16 us (7%)
  other arithmetic  15.1 us (7%)
    ppermute x22, waiting for transfers between devices, swap(): return lax.ppermute(value, axis, [(i, i ^ bit) for i in range(size)])  74 us
    pallas_call x1, Pallas kernels, mlp(): pl.pallas_call(partial(mlp_kernel, heads=heads, chunk=chunk), grid_spec=p...  47 us
    pallas_call x1, Pallas kernels, attn_bwd(): pl.pallas_call(partial(attn_bwd_kernel, heads=heads), grid_spec=pltpu.Pre...  31.4 us
    ppermute x22, starting transfers between devices, swap(): return lax.ppermute(value, axis, [(i, i ^ bit) for i in range(size)])  21.6 us
    pallas_call x1, Pallas kernels, attn_fwd(): pl.pallas_call(partial(attn_fwd_kernel, heads=heads), grid_spec=pltpu.Pre...  17.9 us
    select_n x10, other arithmetic, split_by(): return (jnp.where(mine, high, low), jnp.where(mine, low, high))  5.36 us
  transfers between devices with their start and end apart: 22, of which 14 were waited for; matrix products, arithmetic and copies ran while one was open for 6% of the time, Pallas kernels for 22%

profile of v1, /device:TPU:0, one launch (start us, length us, event | category | flops | bytes accessed | tf_op | source)
XLA Modules:
  0.0 224.1 jit_solution(16749581347075135481)
XLA Ops:
  8.5 3.1 %collective-permute-start.4 = (bf16[1,48,1792]{2,1,0:T(8,128)(2,1)S(1)}, bf16[1,48,1792]{2,1,0:T(8,128)(2,1)S(1)}, u32[]{:S(2)}, u32[]{:S(2)}) collective-permute-start(bf16[1,48,1792]{2,1,0:T(8,128)(2,1)S(1)} %fusion.4), channel_id=1, source_target_pairs={{0,8},{4,12},{8,0},{12,4},{16,24},{20,28},{24,16},{28,20},{1,9},{5... | collective-permute-start | bytes 516104 | tf_op jit(solution)/shard_map/ppermute | solution.py:440
  12.4 4.2 %collective-permute-done.4 = bf16[1,48,1792]{2,1,0:T(8,128)(2,1)S(1)} collective-permute-done((bf16[1,48,1792]{2,1,0:T(8,128)(2,1)S(1)}, bf16[1,48,1792]{2,1,0:T(8,128)(2,1)S(1)}, u32[]{:S(2)}, u32[]{:S(2)}) %collective-permute-start.4) | collective-permute-done | bytes 172064 | tf_op jit(solution)/shard_map/ppermute | solution.py:440
  16.6 2.8 %collective-permute-start.5 = (bf16[2,48,1792]{2,1,0:T(8,128)(2,1)S(1)}, bf16[2,48,1792]{2,1,0:T(8,128)(2,1)S(1)}, u32[]{:S(2)}, u32[]{:S(2)}) collective-permute-start(bf16[2,48,1792]{2,1,0:T(8,128)(2,1)S(1)} %maximum_select_fusion.6), channel_id=1, source_target_pairs={{0,16},{4,20},{8,24},{12,28},{16,0},{20,4},{24,8},{28,12},{1,17},{... | collective-permute-start | bytes 1032200 | tf_op jit(solution)/shard_map/ppermute | solution.py:440
  20.1 13.5 %collective-permute-done.5 = bf16[2,48,1792]{2,1,0:T(8,128)(2,1)S(1)} collective-permute-done((bf16[2,48,1792]{2,1,0:T(8,128)(2,1)S(1)}, bf16[2,48,1792]{2,1,0:T(8,128)(2,1)S(1)}, u32[]{:S(2)}, u32[]{:S(2)}) %collective-permute-start.5) | collective-permute-done | bytes 344096 | tf_op jit(solution)/shard_map/ppermute | solution.py:440
  35.3 8.0 %collective-permute-done.1 = bf16[2,48,640]{2,1,0:T(8,128)(2,1)S(1)} collective-permute-done((bf16[2,48,640]{2,1,0:T(8,128)(2,1)S(1)}, bf16[2,48,640]{2,1,0:T(8,128)(2,1)S(1)}, u32[]{:S(2)}, u32[]{:S(2)}) %collective-permute-start.1) | collective-permute-done | bytes 122912 | tf_op jit(solution)/shard_map/ppermute | solution.py:440
  44.0 8.2 %collective-permute-done.6 = bf16[4,48,1792]{2,1,0:T(8,128)(2,1)S(1)} collective-permute-done((bf16[4,48,1792]{2,1,0:T(8,128)(2,1)S(1)}, bf16[4,48,1792]{2,1,0:T(8,128)(2,1)S(1)}, u32[]{:S(2)}, u32[]{:S(2)}) %collective-permute-start.6) | collective-permute-done | bytes 688160 | tf_op jit(solution)/shard_map/ppermute | solution.py:440
  53.2 2.2 collective-permute-done.2
  58.7 17.9 %attn_fwd.1 = (bf16[2048,512]{1,0:T(8,128)(2,1)}, bf16[8,400,1536]{2,1,0:T(8,128)(2,1)}, f32[8,8,512]{2,1,0:T(8,128)}, bf16[384,1536]{1,0:T(8,128)(2,1)}) custom-call(s32[17]{0:T(128)} %pad_add_fusion.meta, bf16[2048,384]{1,0:T(8,128)(2,1)} %tok.5, bf16[384,1280]{1,0:T(8,128)(2,1)} %maximum_select_fusion.2.w1), custom_call_target="tpu_custom_call" | custom-call | tf_op jit(solution)/shard_map/attn_fwd/pallas_call | solution.py:140
  76.6 1.9 maximum_select_fusion.w2
  78.5 47.0 %mlp.1 = (bf16[2048,384]{1,0:T(8,128)(2,1)}, f32[2048,384]{1,0:T(8,128)}, bf16[2048,512]{1,0:T(8,128)(2,1)}, bf16[384,3584]{1,0:T(8,128)(2,1)}) custom-call(s32[17]{0:T(128)} %pad_add_fusion.meta, bf16[2048,384]{1,0:T(8,128)(2,1)} %tok.5, bf16[2048,384]{1,0:T(8,128)(2,1)} %cot.1, bf16[2048,512]{1,0:T(8,128)(2,1)} %get-tuple-element.25.attn, ...), custom_call_target="tpu_custom_call" | custom-call | tf_op jit(solution)/shard_map/mlp/pallas_call | solution.py:276
  125.5 3.0 %broadcast_select_fusion = bf16[384,1792]{1,0:T(8,128)(2,1)} fusion(pred[]{:T(512)S(6)} %ne.10, bf16[384,3584]{1,0:T(8,128)(2,1)} %get-tuple-element.34), kind=kLoop, calls=%fused_computation.4 | loop fusion | flops 688128 | bytes 4128769 | tf_op jit(solution)/shard_map/jit(_where)/select_n | solution.py:457
  128.5 31.4 %attn_bwd.1 = (bf16[2048,384]{1,0:T(8,128)(2,1)}, bf16[384,1280]{1,0:T(8,128)(2,1)}) custom-call(s32[17]{0:T(128)} %pad_add_fusion.meta, bf16[2048,384]{1,0:T(8,128)(2,1)} %tok.5, bf16[8,400,1536]{2,1,0:T(8,128)(2,1)} %get-tuple-element.27.qkv, f32[8,8,512]{2,1,0:T(8,128)} %get-tuple-element.28.lse, bf16[2048,512]{1,0:T(8,128)(2,1)} %get-tuple-element.29.dattn, ...), custom_call_target="tpu_custom_call" | custom-call | tf_op jit(solution)/shard_map/attn_bwd/pallas_call | solution.py:405
  159.9 2.2 broadcast_select_fusion.2
  162.0 2.1 collective-permute-done.8
  166.6 1.8 add_convert_fusion
  169.6 4.8 %collective-permute-done.9 = bf16[8,24,640]{2,1,0:T(8,128)(2,1)S(1)} collective-permute-done((bf16[8,24,640]{2,1,0:T(8,128)(2,1)S(1)}, bf16[8,24,640]{2,1,0:T(8,128)(2,1)S(1)}, u32[]{:S(2)}, u32[]{:S(2)}) %collective-permute-start.9) | collective-permute-done | bytes 245792 | tf_op jit(solution)/shard_map/ppermute | solution.py:440
  175.4 4.0 %collective-permute-done.10 = bf16[4,1,24,640]{3,2,1,0:T(8,128)(2,1)S(1)} collective-permute-done((bf16[4,1,24,640]{3,2,1,0:T(8,128)(2,1)S(1)}, bf16[4,1,24,640]{3,2,1,0:T(8,128)(2,1)S(1)}, u32[]{:S(2)}, u32[]{:S(2)}) %collective-permute-start.10) | collective-permute-done | bytes 122912 | tf_op jit(solution)/shard_map/ppermute | solution.py:440
  179.5 8.8 %collective-permute-done.16 = bf16[8,24,1792]{2,1,0:T(8,128)(2,1)S(1)} collective-permute-done((bf16[8,24,1792]{2,1,0:T(8,128)(2,1)S(1)}, bf16[8,24,1792]{2,1,0:T(8,128)(2,1)S(1)}, u32[]{:S(2)}, u32[]{:S(2)}) %collective-permute-start.16) | collective-permute-done | bytes 688160 | tf_op jit(solution)/shard_map/ppermute | solution.py:440
  190.1 5.8 %collective-permute-done.11 = bf16[2,24,640]{2,1,0:T(8,128)(2,1)S(1)} collective-permute-done((bf16[2,24,640]{2,1,0:T(8,128)(2,1)S(1)}, bf16[2,24,640]{2,1,0:T(8,128)(2,1)S(1)}, u32[]{:S(2)}, u32[]{:S(2)}) %collective-permute-start.11) | collective-permute-done | bytes 61472 | tf_op jit(solution)/shard_map/ppermute | solution.py:440
  195.9 2.1 collective-permute-done.17
  198.3 5.1 %collective-permute-start.12 = (bf16[1,24,640]{2,1,0:T(8,128)(2,1)S(1)}, bf16[1,24,640]{2,1,0:T(8,128)(2,1)S(1)}, u32[]{:S(2)}, u32[]{:S(2)}) collective-permute-start(bf16[1,24,640]{2,1,0:T(8,128)(2,1)S(1)} %broadcast_select_fusion.7), channel_id=1, source_target_pairs={{0,8},{4,12},{8,0},{12,4},{16,24},{20,28},{24,16},{28,20},{1,9},{5... | collective-permute-start | bytes 92168 | tf_op jit(solution)/shard_map/ppermute | solution.py:440
  203.4 4.8 %collective-permute-done.18 = bf16[2,24,1792]{2,1,0:T(8,128)(2,1)S(1)} collective-permute-done((bf16[2,24,1792]{2,1,0:T(8,128)(2,1)S(1)}, bf16[2,24,1792]{2,1,0:T(8,128)(2,1)S(1)}, u32[]{:S(2)}, u32[]{:S(2)}) %collective-permute-start.18) | collective-permute-done | bytes 172064 | tf_op jit(solution)/shard_map/ppermute | solution.py:440
  210.1 2.8 %collective-permute-done.19 = bf16[1,24,1792]{2,1,0:T(8,128)(2,1)S(1)} collective-permute-done((bf16[1,24,1792]{2,1,0:T(8,128)(2,1)S(1)}, bf16[1,24,1792]{2,1,0:T(8,128)(2,1)S(1)}, u32[]{:S(2)}, u32[]{:S(2)}) %collective-permute-start.19) | collective-permute-done | bytes 86048 | tf_op jit(solution)/shard_map/ppermute | solution.py:440
  214.7 2.8 %collective-permute-done.20 = bf16[24,1792]{1,0:T(8,128)(2,1)S(1)} collective-permute-done((bf16[24,1792]{1,0:T(8,128)(2,1)S(1)}, bf16[24,1792]{1,0:T(8,128)(2,1)S(1)}, u32[]{:S(2)}, u32[]{:S(2)}) %collective-permute-start.20) | collective-permute-done | bytes 86048 | tf_op jit(solution)/shard_map/ppermute | solution.py:440
  (129 shorter events, 32.9 us)
Async XLA Ops:
  7.7 11.7 %copy-start.2 = (s32[256]{0:T(256)S(1)}, s32[256]{0:T(256)}, u32[]{:S(2)}) copy-start(s32[256]{0:T(256)} %param.20) | copy-start | bytes 3076
  8.5 8.1 %collective-permute-start.4 = (bf16[1,48,1792]{2,1,0:T(8,128)(2,1)S(1)}, bf16[1,48,1792]{2,1,0:T(8,128)(2,1)S(1)}, u32[]{:S(2)}, u32[]{:S(2)}) collective-permute-start(bf16[1,48,1792]{2,1,0:T(8,128)(2,1)S(1)} %fusion.4), channel_id=1, source_target_pairs={{0,8},{4,12},{8,0},{12,4},{16,24},{20,28},{24,16},{28,20},{1,9},{5... | collective-permute-start | bytes 516104 | tf_op jit(solution)/shard_map/ppermute | solution.py:440
  12.3 22.8 %collective-permute-start = (bf16[1,48,640]{2,1,0:T(8,128)(2,1)S(1)}, bf16[1,48,640]{2,1,0:T(8,128)(2,1)S(1)}, u32[]{:S(2)}, u32[]{:S(2)}) collective-permute-start(bf16[1,48,640]{2,1,0:T(8,128)(2,1)S(1)} %fusion.9), channel_id=1, source_target_pairs={{0,8},{4,12},{8,0},{12,4},{16,24},{20,28},{24,16},{28,20},{1,9},{5... | collective-permute-start | bytes 184328 | tf_op jit(solution)/shard_map/ppermute | solution.py:440
  16.6 16.9 %collective-permute-start.5 = (bf16[2,48,1792]{2,1,0:T(8,128)(2,1)S(1)}, bf16[2,48,1792]{2,1,0:T(8,128)(2,1)S(1)}, u32[]{:S(2)}, u32[]{:S(2)}) collective-permute-start(bf16[2,48,1792]{2,1,0:T(8,128)(2,1)S(1)} %maximum_select_fusion.6), channel_id=1, source_target_pairs={{0,16},{4,20},{8,24},{12,28},{16,0},{20,4},{24,8},{28,12},{1,17},{... | collective-permute-start | bytes 1032200 | tf_op jit(solution)/shard_map/ppermute | solution.py:440
  33.7 18.4 %collective-permute-start.6 = (bf16[4,48,1792]{2,1,0:T(8,128)(2,1)S(1)}, bf16[4,48,1792]{2,1,0:T(8,128)(2,1)S(1)}, u32[]{:S(2)}, u32[]{:S(2)}) collective-permute-start(bf16[4,48,1792]{2,1,0:T(8,128)(2,1)S(1)} %maximum_select_fusion.3), channel_id=1, source_target_pairs={{0,4},{4,0},{8,12},{12,8},{16,20},{20,16},{24,28},{28,24},{1,5},{5... | collective-permute-start | bytes 2064392 | tf_op jit(solution)/shard_map/ppermute | solution.py:440
  35.1 8.1 %collective-permute-start.1 = (bf16[2,48,640]{2,1,0:T(8,128)(2,1)S(1)}, bf16[2,48,640]{2,1,0:T(8,128)(2,1)S(1)}, u32[]{:S(2)}, u32[]{:S(2)}) collective-permute-start(bf16[2,48,640]{2,1,0:T(8,128)(2,1)S(1)} %maximum_select_fusion.11), channel_id=1, source_target_pairs={{0,16},{4,20},{8,24},{12,28},{16,0},{20,4},{24,8},{28,12},{1,17},{... | collective-permute-start | bytes 368648 | tf_op jit(solution)/shard_map/ppermute | solution.py:440
  43.3 12.2 %collective-permute-start.2 = (bf16[4,48,640]{2,1,0:T(8,128)(2,1)S(1)}, bf16[4,48,640]{2,1,0:T(8,128)(2,1)S(1)}, u32[]{:S(2)}, u32[]{:S(2)}) collective-permute-start(bf16[4,48,640]{2,1,0:T(8,128)(2,1)S(1)} %maximum_select_fusion.8), channel_id=1, source_target_pairs={{0,4},{4,0},{8,12},{12,8},{16,20},{20,16},{24,28},{28,24},{1,5},{5... | collective-permute-start | bytes 737288 | tf_op jit(solution)/shard_map/ppermute | solution.py:440
  52.5 24.2 %collective-permute-start.7 = (bf16[384,1792]{1,0:T(8,128)(2,1)S(1)}, bf16[384,1792]{1,0:T(8,128)(2,1)S(1)}, u32[]{:S(2)}, u32[]{:S(2)}) collective-permute-start(bf16[384,1792]{1,0:T(8,128)(2,1)S(1)} %bitcast.86), channel_id=1, source_target_pairs={{0,1},{1,0},{2,3},{3,2},{4,5},{5,4},{6,7},{7,6},{8,9},{9,8},{10,11... | collective-permute-start | bytes 4128776 | tf_op jit(solution)/shard_map/ppermute | solution.py:440
  55.5 2.0 collective-permute-start.3
  128.5 38.1 %collective-permute-start.15 = (bf16[384,1792]{1,0:T(8,128)(2,1)}, bf16[384,1792]{1,0:T(8,128)(2,1)}, u32[]{:S(2)}, u32[]{:S(2)}) collective-permute-start(bf16[384,1792]{1,0:T(8,128)(2,1)} %broadcast_select_fusion), channel_id=1, source_target_pairs={{0,1},{1,0},{2,3},{3,2},{4,5},{5,4},{6,7},{7,6},{8,9},{9,8},{10,11... | collective-permute-start | bytes 4128776 | tf_op jit(solution)/shard_map/ppermute | solution.py:440
  159.9 6.7 %copy-start = (bf16[384,3584]{1,0:T(8,128)(2,1)S(1)}, bf16[384,3584]{1,0:T(8,128)(2,1)}, u32[]{:S(2)}) copy-start(bf16[384,3584]{1,0:T(8,128)(2,1)} %get-tuple-element.34) | copy-start | bytes 8257540
  162.0 2.1 collective-permute-start.8
  165.5 8.9 %collective-permute-start.9 = (bf16[8,24,640]{2,1,0:T(8,128)(2,1)S(1)}, bf16[8,24,640]{2,1,0:T(8,128)(2,1)S(1)}, u32[]{:S(2)}, u32[]{:S(2)}) collective-permute-start(bf16[8,24,640]{2,1,0:T(8,128)(2,1)S(1)} %broadcast_select_fusion.4), channel_id=1, source_target_pairs={{0,2},{1,3},{2,0},{3,1},{4,6},{5,7},{6,4},{7,5},{8,10},{9,11},{10,... | collective-permute-start | bytes 737288 | tf_op jit(solution)/shard_map/ppermute | solution.py:440
  168.5 19.8 %collective-permute-start.16 = (bf16[8,24,1792]{2,1,0:T(8,128)(2,1)S(1)}, bf16[8,24,1792]{2,1,0:T(8,128)(2,1)S(1)}, u32[]{:S(2)}, u32[]{:S(2)}) collective-permute-start(bf16[8,24,1792]{2,1,0:T(8,128)(2,1)S(1)} %broadcast_select_fusion.1), channel_id=1, source_target_pairs={{0,2},{1,3},{2,0},{3,1},{4,6},{5,7},{6,4},{7,5},{8,10},{9,11},{10,... | collective-permute-start | bytes 2064392 | tf_op jit(solution)/shard_map/ppermute | solution.py:440
  174.5 4.9 %collective-permute-start.10 = (bf16[4,1,24,640]{3,2,1,0:T(8,128)(2,1)S(1)}, bf16[4,1,24,640]{3,2,1,0:T(8,128)(2,1)S(1)}, u32[]{:S(2)}, u32[]{:S(2)}) collective-permute-start(bf16[4,1,24,640]{3,2,1,0:T(8,128)(2,1)S(1)} %broadcast_select_fusion.5), channel_id=1, source_target_pairs={{0,4},{4,0},{8,12},{12,8},{16,20},{20,16},{24,28},{28,24},{1,5},{5... | collective-permute-start | bytes 368648 | tf_op jit(solution)/shard_map/ppermute | solution.py:440
  188.6 9.4 %collective-permute-start.17 = (bf16[4,1,24,1792]{3,2,1,0:T(8,128)(2,1)S(1)}, bf16[4,1,24,1792]{3,2,1,0:T(8,128)(2,1)S(1)}, u32[]{:S(2)}, u32[]{:S(2)}) collective-permute-start(bf16[4,1,24,1792]{3,2,1,0:T(8,128)(2,1)S(1)} %broadcast_select_fusion.3), channel_id=1, source_target_pairs={{0,4},{4,0},{8,12},{12,8},{16,20},{20,16},{24,28},{28,24},{1,5},{5... | collective-permute-start | bytes 1032200 | tf_op jit(solution)/shard_map/ppermute | solution.py:440
  190.0 5.8 %collective-permute-start.11 = (bf16[2,24,640]{2,1,0:T(8,128)(2,1)S(1)}, bf16[2,24,640]{2,1,0:T(8,128)(2,1)S(1)}, u32[]{:S(2)}, u32[]{:S(2)}) collective-permute-start(bf16[2,24,640]{2,1,0:T(8,128)(2,1)S(1)} %fusion.8), channel_id=1, source_target_pairs={{0,16},{4,20},{8,24},{12,28},{16,0},{20,4},{24,8},{28,12},{1,17},{... | collective-permute-start | bytes 184328 | tf_op jit(solution)/shard_map/ppermute | solution.py:440
  198.2 10.1 %collective-permute-start.18 = (bf16[2,24,1792]{2,1,0:T(8,128)(2,1)S(1)}, bf16[2,24,1792]{2,1,0:T(8,128)(2,1)S(1)}, u32[]{:S(2)}, u32[]{:S(2)}) collective-permute-start(bf16[2,24,1792]{2,1,0:T(8,128)(2,1)S(1)} %fusion.2), channel_id=1, source_target_pairs={{0,16},{4,20},{8,24},{12,28},{16,0},{20,4},{24,8},{28,12},{1,17},{... | collective-permute-start | bytes 516104 | tf_op jit(solution)/shard_map/ppermute | solution.py:440
  198.3 10.4 %collective-permute-start.12 = (bf16[1,24,640]{2,1,0:T(8,128)(2,1)S(1)}, bf16[1,24,640]{2,1,0:T(8,128)(2,1)S(1)}, u32[]{:S(2)}, u32[]{:S(2)}) collective-permute-start(bf16[1,24,640]{2,1,0:T(8,128)(2,1)S(1)} %broadcast_select_fusion.7), channel_id=1, source_target_pairs={{0,8},{4,12},{8,0},{12,4},{16,24},{20,28},{24,16},{28,20},{1,9},{5... | collective-permute-start | bytes 92168 | tf_op jit(solution)/shard_map/ppermute | solution.py:440
  208.4 4.6 %collective-permute-start.19 = (bf16[1,24,1792]{2,1,0:T(8,128)(2,1)S(1)}, bf16[1,24,1792]{2,1,0:T(8,128)(2,1)S(1)}, u32[]{:S(2)}, u32[]{:S(2)}) collective-permute-start(bf16[1,24,1792]{2,1,0:T(8,128)(2,1)S(1)} %broadcast_select_fusion.6), channel_id=1, source_target_pairs={{0,8},{4,12},{8,0},{12,4},{16,24},{20,28},{24,16},{28,20},{1,9},{5... | collective-permute-start | bytes 258056 | tf_op jit(solution)/shard_map/ppermute | solution.py:440
  208.7 5.9 %collective-permute-start.13 = (bf16[24,640]{1,0:T(8,128)(2,1)S(1)}, bf16[24,640]{1,0:T(8,128)(2,1)S(1)}, u32[]{:S(2)}, u32[]{:S(2)}) collective-permute-start(bf16[24,640]{1,0:T(8,128)(2,1)S(1)} %fusion.10), channel_id=1, source_target_pairs={{0,2},{1,3},{2,0},{3,1},{4,6},{5,7},{6,4},{7,5},{8,10},{9,11},{10,... | collective-permute-start | bytes 92168 | tf_op jit(solution)/shard_map/ppermute | solution.py:440
  212.9 4.6 %collective-permute-start.20 = (bf16[24,1792]{1,0:T(8,128)(2,1)S(1)}, bf16[24,1792]{1,0:T(8,128)(2,1)S(1)}, u32[]{:S(2)}, u32[]{:S(2)}) collective-permute-start(bf16[24,1792]{1,0:T(8,128)(2,1)S(1)} %fusion.7), channel_id=1, source_target_pairs={{0,2},{1,3},{2,0},{3,1},{4,6},{5,7},{6,4},{7,5},{8,10},{9,11},{10,... | collective-permute-start | bytes 258056 | tf_op jit(solution)/shard_map/ppermute | solution.py:440
  214.6 3.0 %collective-permute-start.14 = (bf16[48,640]{1,0:T(8,128)(2,1)S(1)}, bf16[48,640]{1,0:T(8,128)(2,1)S(1)}, u32[]{:S(2)}, u32[]{:S(2)}) collective-permute-start(bf16[48,640]{1,0:T(8,128)(2,1)S(1)} %maximum_select_fusion.13), channel_id=1, source_target_pairs={{0,1},{1,0},{2,3},{3,2},{4,5},{5,4},{6,7},{7,6},{8,9},{9,8},{10,11... | collective-permute-start | bytes 184328 | tf_op jit(solution)/shard_map/ppermute | solution.py:440
  217.5 1.6 collective-permute-start.21
  (6 other events, 28.0 us)

commit v2 on v1

v2 whole, which is shorter than its diff:
```python
from functools import partial
import math

import jax
import jax.numpy as jnp
from jax import lax
from jax.experimental import pallas as pl
from jax.experimental.pallas import tpu as pltpu
from jax.sharding import PartitionSpec as P

HEAD_DIM = 96
HEAD_PAD = 128
LENS = (196, 256, 400)
SLOT = 400
ROW_PAD = 32
PAIR = 2
PAIR_DIM = PAIR * HEAD_DIM
PAIR_PAD = PAIR * HEAD_PAD
QUARTERS = 4
VEC = 128
VEC_PAIR = 64
SCALE = 1.0 / math.sqrt(HEAD_DIM)
EXP_SCALE = SCALE * math.log2(math.e)
MIB = 1024 * 1024
VMEM = {"attn_fwd": 12, "mlp": 21, "attn_bwd": 8, "layer_out": 8, "input_grad": 10}
F32 = jnp.float32
BF16 = jnp.bfloat16


def dot_nn(a, b):
    return lax.dot_general(a, b, (((1,), (0,)), ((), ())), preferred_element_type=F32)


def dot_nt(a, b):
    return lax.dot_general(a, b, (((1,), (1,)), ((), ())), preferred_element_type=F32)


def dot_tn(a, b):
    return lax.dot_general(a, b, (((0,), (0,)), ((), ())), preferred_element_type=F32)


def pad_heads(values):
    rows, cols = values.shape
    gap = jnp.zeros((rows, HEAD_PAD - HEAD_DIM), values.dtype)
    parts = []
    for h in range(cols // HEAD_DIM):
        parts += [values[:, h * HEAD_DIM : (h + 1) * HEAD_DIM], gap]
    return jnp.concatenate(parts, axis=1)


def unpad_heads(values):
    rows, cols = values.shape
    return jnp.concatenate(
        [values[:, h * HEAD_PAD : h * HEAD_PAD + HEAD_DIM] for h in range(cols // HEAD_PAD)], axis=1
    )


def row_norm(x):
    center = x - jnp.mean(x, axis=-1, keepdims=True)
    inverse = lax.rsqrt(jnp.mean(center * center, axis=-1, keepdims=True) + 1e-6)
    return center * inverse, inverse


def row_norm_back(e, xhat, inverse):
    return inverse * (
        e - jnp.mean(e, axis=-1, keepdims=True) - xhat * jnp.mean(e * xhat, axis=-1, keepdims=True)
    )


def load_rows(ref, start, count):
    base = pl.multiple_of((start // 8) * 8, 8)
    window = ref[pl.ds(base, count + 8), :]
    moved = pltpu.roll(window, count + 4, 0)
    return jnp.where(start % 8 == 0, window, moved)[:count]


def store_rows(ref, start, length, values, cols):
    count = -(-length // 8) * 8
    base = pl.multiple_of((start // 8) * 8, 8)
    window = jnp.concatenate([values[:count], jnp.zeros((8, values.shape[1]), values.dtype)], axis=0)
    window = jnp.where(start % 8 == 0, window, pltpu.roll(window, 4, 0))
    row = lax.broadcasted_iota(jnp.int32, window.shape, 0) - start % 8
    held = ref[pl.ds(base, count + 8), cols]
    ref[pl.ds(base, count + 8), cols] = jnp.where((row >= 0) & (row < length), window, held)


def by_group(group, work):
    for g, length in enumerate(LENS):
        pl.when(group == g)(partial(work, length, -(-length // 16) * 16))


def gelu_pair(u):
    cdf = 0.5 + 0.5 * lax.erf(u * (1.0 / math.sqrt(2.0)))
    bell = jnp.exp2((u * u) * (-0.5 * math.log2(math.e)))
    return u * cdf, cdf + u * (bell * (1.0 / math.sqrt(2.0 * math.pi)))


def whole(array):
    at = (0,) * len(array.shape)
    return pl.BlockSpec(array.shape, lambda i, m: at, pipeline_mode=pl.Buffered(1))


def slot_block(cols):
    return pl.BlockSpec((1, SLOT, cols), lambda i, m: (i, 0, 0))


def call(kernel, name, grid, in_specs, out_specs, out_shape, scratch, args, waits=(), carry=(), far=()):
    given, made, passed = len(in_specs) + 1, len(out_shape), len(waits) + len(carry)

    def ordered(*refs):
        kernel(*refs[:given], *refs[given + passed : given + passed + made], *refs[given + passed + made + len(carry) :])

    args = [
        pltpu.with_memory_space_constraint(t, pltpu.HBM) if at in far else t for at, t in enumerate(args)
    ]
    anywhere = pl.BlockSpec(memory_space=pl.ANY)
    outs = pl.pallas_call(
        ordered,
        grid_spec=pltpu.PrefetchScalarGridSpec(
            num_scalar_prefetch=1,
            grid=(grid,),
            in_specs=list(in_specs) + [anywhere] * passed,
            out_specs=list(out_specs) + [anywhere] * len(carry),
            scratch_shapes=scratch,
        ),
        out_shape=list(out_shape) + [jax.ShapeDtypeStruct(t.shape, t.dtype) for t in carry],
        input_output_aliases={given + len(waits) + n: made + n for n in range(len(carry))},
        compiler_params=pltpu.CompilerParams(vmem_limit_bytes=VMEM[name] * MIB),
        name=name,
    )(*args, *waits, *carry)
    return outs


def groups_at(meta):
    return (meta.shape[0] - 2) // 2


def rows_used(meta):
    return meta[meta.shape[0] - 2]


def device_of(meta):
    return meta[meta.shape[0] - 1]


def core_of(meta):
    return device_of(meta) % 2


def attn_fwd_kernel(meta, tok, wf0, wf1, attn0, attn1, qkv0, qkv1, xhat_out, lse0, lse1, wpad0, wpad1,
                    tok32, out32, bias):
    i = pl.program_id(0)
    rows, width = tok.shape
    cols = 3 * PAIR_PAD
    sides = ((wf0, qkv0, lse0, wpad0), (wf1, qkv1, lse1, wpad1))

    @pl.when(i == 0)
    def _():
        tok32[:rows] = tok[...].astype(F32)
        tok32[rows:] = jnp.zeros((tok32.shape[0] - rows, width), F32)
        vec = wf0[:, 3 * PAIR_DIM :].astype(F32).T
        bias[0:2, :width] = vec[0:2]
        for c in range(2):

            @pl.when(core_of(meta) == c)
            def _():
                for p in range(2):
                    at = (p ^ c) * PAIR_DIM
                    parts = [pad_heads(vec[r : r + 1, at : at + PAIR_DIM]) for r in (2, 3)]
                    bias[2 + p : 3 + p, :] = jnp.concatenate(
                        [parts[0], jnp.zeros((1, PAIR_PAD), F32), parts[1]], axis=1
                    )

        for wf, _, _, wpad in sides:
            wpad[...] = pad_heads(wf[:, : 3 * PAIR_DIM].astype(F32)).astype(BF16)

    start = meta[i]

    def work(length, padded):
        xhat, _ = row_norm(load_rows(tok32, start, padded))
        normed = (xhat * bias[0:1, :width] + bias[1:2, :width]).astype(BF16)
        xhat_out[0, :padded, :] = xhat.astype(BF16)
        outs = []
        for p, (_, qkv, lse, wpad) in enumerate(sides):
            qkv[0, :padded, :] = (dot_nn(normed, wpad[...]) + bias[2 + p : 3 + p, :]).astype(BF16)
            for h in range(PAIR):
                at = h * HEAD_PAD
                q = qkv[0, :padded, at : at + HEAD_PAD]
                k = qkv[0, :padded, PAIR_PAD + at : PAIR_PAD + at + HEAD_PAD]
                v = qkv[0, :padded, 2 * PAIR_PAD + at : 2 * PAIR_PAD + at + HEAD_PAD]
                s = dot_nt(k, q)
                if length < padded:
                    key = lax.broadcasted_iota(jnp.int32, s.shape, 0)
                    s = jnp.where(key < length, s, -1e30)
                top = jnp.max(s, axis=0, keepdims=True)
                e = jnp.exp2((s - top) * EXP_SCALE)
                total = jnp.sum(e, axis=0, keepdims=True)
                probs = (e * (1.0 / total)).astype(BF16)
                lse[0, h : h + 1, :padded] = top * EXP_SCALE + jnp.log2(total)
                outs.append(dot_tn(probs, v))
        store_rows(out32, start, length, jnp.concatenate(outs, axis=1), slice(None))

    by_group(meta[groups_at(meta) + i], work)

    @pl.when(i == pl.num_programs(0) - 1)
    def _():
        row = lax.broadcasted_iota(jnp.int32, (rows, 1), 0)
        mixed = jnp.where(row < rows_used(meta), out32[:rows], 0.0).astype(BF16)
        attn0[...] = mixed[:, :PAIR_PAD]
        attn1[...] = mixed[:, PAIR_PAD:]


def attn_fwd(meta, tokens, wf, waits, carry):
    rows, width = tokens.shape
    slots = groups_at(meta)
    cols = 3 * PAIR_PAD
    out_shape = [jax.ShapeDtypeStruct((rows, PAIR_PAD), BF16)] * 2
    out_shape += [jax.ShapeDtypeStruct((slots, SLOT, cols), BF16)] * 2
    out_shape += [jax.ShapeDtypeStruct((slots, SLOT, width), BF16)]
    out_shape += [jax.ShapeDtypeStruct((slots, 8, 512), F32)] * 2
    out_shape += [jax.ShapeDtypeStruct((width, cols), BF16)] * 2
    stats = pl.BlockSpec((1, 8, 512), lambda i, m: (i, 0, 0))
    out_specs = [whole(out_shape[0])] * 2 + [slot_block(cols)] * 2 + [slot_block(width)]
    out_specs += [stats] * 2 + [whole(out_shape[-1])] * 2
    scratch = [
        pltpu.VMEM((rows + ROW_PAD, width), F32),
        pltpu.VMEM((rows + ROW_PAD, 2 * PAIR_PAD), F32),
        pltpu.VMEM((8, cols), F32),
    ]
    in_specs = [whole(tokens), whole(wf[0]), whole(wf[1])]
    args = (meta, tokens, *wf)
    return call(attn_fwd_kernel, "attn_fwd", slots, in_specs, out_specs, out_shape, scratch, args, waits, carry)


def put_blocks(to, value, col, shards, parity=None):
    rows, cols = value.shape
    size = rows // shards
    half = rows // 2
    if size % 16:
        if parity is not None:
            value = value[parity * half : (parity + 1) * half]
        to[:, col : col + cols] = value
        return
    for n, place in enumerate(turned(shards)):
        at = place * size
        if parity is not None:
            if n % 2 != parity:
                continue
            at -= parity * half
        to[at : at + size, col : col + cols] = value[n * size : (n + 1) * size]


def mlp_kernel(meta, tok, cot, attn0, attn1, w0, w1, x1o, acto, dx1, da0, da1,
               keep_a, send_a, keep_b, send_b, wproj, rowvec, gd, gu, gp, gsum, *, shards):
    i = pl.program_id(0)
    rows, width = tok.shape
    parts = (w0, w1)

    def in_order(first, second, use):
        for c in range(2):
            pl.when(core_of(meta) == c)(partial(use, c, *((first, second) if c == 0 else (second, first))))

    @pl.when(i == 0)
    def _():
        def use(c, low, high):
            flat = [ref[x][:, width : width + VEC] for ref in (low, high) for x in range(2)]
            proj = jnp.concatenate(flat[: width // VEC], axis=1)
            wproj[...] = jnp.zeros(wproj.shape, BF16)
            for h in range(2 * PAIR):
                at = (h ^ (PAIR * c)) * HEAD_PAD
                wproj[at : at + HEAD_DIM] = proj[h * HEAD_DIM : (h + 1) * HEAD_DIM]
            vec = flat[-1].astype(F32).T
            for r in range(4):
                rowvec[r : r + 1, :width] = vec[r : r + 1]
                at = (r ^ (2 * c)) * width
                rowvec[4:5, at : at + width] = vec[4 + r : 5 + r]

        in_order(w0, w1, use)
        gd[...] = jnp.zeros(gd.shape, F32)
        gu[...] = jnp.zeros(gu.shape, F32)
        gp[...] = jnp.zeros(gp.shape, F32)
        gsum[...] = jnp.zeros(gsum.shape, F32)

    proj_bias, gain, shift, down_bias = [rowvec[r : r + 1, :width] for r in range(4)]
    row = lax.broadcasted_iota(jnp.int32, (rows, 1), 0) + i * rows
    valid = (row < rows_used(meta)).astype(F32)
    mixed0, mixed1 = attn0[...], attn1[...]
    x1 = tok[...].astype(F32) + dot_nn(mixed0, wproj[:PAIR_PAD]) + dot_nn(mixed1, wproj[PAIR_PAD:])
    x1 = x1 + proj_bias
    x1o[...] = (x1 + down_bias) * valid
    xhat, inverse = row_norm(x1)
    normed = (xhat * gain + shift).astype(BF16)
    dy = cot[...].astype(F32) * valid
    dyb = dy.astype(BF16)
    dn = jnp.zeros((rows, width), F32)
    chunk = 2 * width
    for c in range(2):
        at = c * chunk
        up = jnp.concatenate([parts[c][0][:, :width], parts[c][1][:, :width]], axis=1)
        down = jnp.concatenate([parts[c][x][:, width + VEC :] for x in range(2)], axis=0)
        pre = dot_nn(normed, up) + rowvec[4:5, at : at + chunk]
        act, slope = gelu_pair(pre)
        actb = act.astype(BF16)
        acto[:, at : at + chunk] = actb
        dpre = dot_nt(dyb, down) * slope
        dpreb = dpre.astype(BF16)
        gd[:, at : at + chunk] += dot_tn(dyb, actb)
        gu[:, at : at + chunk] += dot_tn(normed, dpreb)
        gsum[4:5, at : at + chunk] += jnp.sum(dpre, axis=0, keepdims=True)
        dn = dn + dot_nt(dpreb, up)
    dx = dy + row_norm_back(dn * gain, xhat, inverse)
    dx1[...] = dx
    dxb = dx.astype(BF16)
    gp[:, :PAIR_PAD] += dot_tn(dxb, mixed0)
    gp[:, PAIR_PAD:] += dot_tn(dxb, mixed1)
    da0[...] = dot_nt(dxb, wproj[:PAIR_PAD]).astype(BF16)
    da1[...] = dot_nt(dxb, wproj[PAIR_PAD:]).astype(BF16)
    gsum[0:1, :width] += jnp.sum(dx, axis=0, keepdims=True)
    gsum[1:2, :width] += jnp.sum(dn * xhat, axis=0, keepdims=True)
    gsum[2:3, :width] += jnp.sum(dn, axis=0, keepdims=True)
    gsum[3:4, :width] += jnp.sum(dy, axis=0, keepdims=True)

    @pl.when(i == pl.num_programs(0) - 1)
    def _():
        for half, (to_a, to_b) in enumerate(((keep_a, keep_b), (send_a, send_b))):
            for x in range(2):
                at = (2 * half + x) * width
                put_blocks(to_a.at[x], gu[:, at : at + width].astype(BF16), 0, shards)
                part = gd[:, at : at + width].T.astype(BF16)
                for y in range(2):
                    put_blocks(to_b.at[y, x], part, 0, shards, y)

        def use(c, low, high):
            rows_of = [gsum[r : r + 1, :width] for r in range(4)]
            for r in range(4):
                at = (r ^ (2 * c)) * width
                rows_of.append(gsum[4:5, at : at + width])
            vec = jnp.concatenate(rows_of + [jnp.zeros((VEC - 8, width), F32)], axis=0).T
            grad = unpad_heads(gp[...]).T
            first, second = grad[:PAIR_DIM], grad[PAIR_DIM:]
            proj = jnp.concatenate([second, first] if c else [first, second], axis=0)
            flat = jnp.concatenate([proj, vec], axis=1).astype(BF16)
            for k in range(QUARTERS):
                to = (low, high)[k // 2].at[k % 2]
                put_blocks(to, flat[:, k * VEC : (k + 1) * VEC], width, shards)

        in_order(keep_a, send_a, use)


def mlp(meta, tokens, cotangent, attn, w, shards, block=512):
    rows, width = tokens.shape
    hidden = QUARTERS * width
    by_row = lambda cols: pl.BlockSpec((block, cols), lambda i, m: (i, 0))
    out_shape = [
        pltpu.HBM((rows, width), F32),
        pltpu.HBM((rows, hidden), BF16),
        pltpu.HBM((rows, width), F32),
        jax.ShapeDtypeStruct((rows, PAIR_PAD), BF16),
        jax.ShapeDtypeStruct((rows, PAIR_PAD), BF16),
    ]
    out_shape += [jax.ShapeDtypeStruct((2, width, width + VEC), BF16)] * 2
    out_shape += [jax.ShapeDtypeStruct((2, 2, width // 2, width), BF16)] * 2
    out_specs = [by_row(s.shape[1]) for s in out_shape[:5]] + [whole(s) for s in out_shape[5:]]
    in_specs = [by_row(width)] * 2 + [by_row(PAIR_PAD)] * 2 + [whole(t) for t in w]
    scratch = [
        pltpu.VMEM((2 * PAIR_PAD, width), BF16),
        pltpu.VMEM((8, hidden), F32),
        pltpu.VMEM((width, hidden), F32),
        pltpu.VMEM((width, hidden), F32),
        pltpu.VMEM((width, 2 * PAIR_PAD), F32),
        pltpu.VMEM((8, hidden), F32),
    ]
    args = (meta, tokens, cotangent, *attn, *w)
    kernel = partial(mlp_kernel, shards=shards)
    return call(kernel, "mlp", rows // block, in_specs, out_specs, out_shape, scratch, args)


def layer_out_kernel(meta, x1, act, w0, w1, out):
    rows, width = x1.shape
    row = lax.broadcasted_iota(jnp.int32, (rows, 1), 0) + pl.program_id(0) * rows
    valid = (row < rows_used(meta)).astype(F32)
    y = x1[...]
    for c, ref in enumerate((w0, w1)):
        down = jnp.concatenate([ref[x][:, width + VEC :] for x in range(2)], axis=0)
        y = y + dot_nn(act[:, 2 * c * width : 2 * (c + 1) * width], down) * valid
    out[...] = y.astype(BF16)


def layer_output(meta, x1, act, w, waits, carry, block=512):
    rows, width = x1.shape
    by_row = lambda cols: pl.BlockSpec((block, cols), lambda i, m: (i, 0))
    return call(
        layer_out_kernel,
        "layer_out",
        rows // block,
        [by_row(width), by_row(act.shape[1]), whole(w[0]), whole(w[1])],
        [by_row(width)],
        [jax.ShapeDtypeStruct((rows, width), BF16)],
        [],
        (meta, x1, act, *w),
        waits,
        carry,
        (1, 2),
    )


def attn_bwd_kernel(meta, qkv, xhat, lse, dattn, wpad, wf, dqkv, grads, da32, gw, gsum, *, own, shards):
    i = pl.program_id(0)
    rows = dattn.shape[0]
    width = wf.shape[0]

    @pl.when(i == 0)
    def _():
        da32[:rows] = dattn[...].astype(F32)
        da32[rows:] = jnp.zeros((da32.shape[0] - rows, PAIR_PAD), F32)
        gw[...] = jnp.zeros(gw.shape, F32)
        gsum[...] = jnp.zeros(gsum.shape, F32)

    start = meta[i]

    def work(length, padded):
        da = load_rows(da32, start, padded)
        if length < padded:
            keep = lax.broadcasted_iota(jnp.int32, (padded, 1), 0) < length
            da = jnp.where(keep, da, 0.0)
        da = da.astype(BF16)
        for h in range(PAIR):
            at = h * HEAD_PAD
            q = qkv[0, :padded, at : at + HEAD_PAD]
            k = qkv[0, :padded, PAIR_PAD + at : PAIR_PAD + at + HEAD_PAD]
            v = qkv[0, :padded, 2 * PAIR_PAD + at : 2 * PAIR_PAD + at + HEAD_PAD]
            dah = da[:, at : at + HEAD_PAD]
            s = dot_nt(k, q)
            p = jnp.exp2(s * EXP_SCALE - lse[0, h : h + 1, :padded])
            if length < padded:
                key = lax.broadcasted_iota(jnp.int32, s.shape, 0)
                p = jnp.where(key < length, p, 0.0)
            dp = dot_nt(v, dah)
            mean = jnp.sum(p * dp, axis=0, keepdims=True)
            ds = (p * (dp - mean)).astype(BF16)
            dv = dot_nn(p.astype(BF16), dah)
            dk = dot_nn(ds, q) * SCALE
            dq = dot_tn(ds, k) * SCALE
            gsum[0:1, at : at + HEAD_PAD] += jnp.sum(dq, axis=0, keepdims=True)
            gsum[0:1, 2 * PAIR_PAD + at : 2 * PAIR_PAD + at + HEAD_PAD] += jnp.sum(dv, axis=0, keepdims=True)
            dqkv[0, :padded, at : at + HEAD_PAD] = dq.astype(BF16)
            dqkv[0, :padded, PAIR_PAD + at : PAIR_PAD + at + HEAD_PAD] = dk.astype(BF16)
            dqkv[0, :padded, 2 * PAIR_PAD + at : 2 * PAIR_PAD + at + HEAD_PAD] = dv.astype(BF16)
        d = dqkv[0, :padded, :]
        gw[...] += dot_tn(xhat[0, :padded, :], d)
        gsum[1:2, :] += jnp.sum(d.astype(F32), axis=0, keepdims=True)

    by_group(meta[groups_at(meta) + i], work)

    @pl.when(i == pl.num_programs(0) - 1)
    def _():
        w = wpad[...].astype(F32)
        raw = gw[...]
        col = gsum[1:2, :]
        gain_term = jnp.sum(raw * w, axis=1, keepdims=True)
        bias_term = jnp.sum(col * w, axis=1, keepdims=True)
        vec = wf[:, 3 * PAIR_DIM :].astype(F32)
        main = unpad_heads(raw * vec[:, 0:1] + vec[:, 1:2] * col).astype(BF16)
        put_blocks(grads, main, 0, shards)
        q_sum = unpad_heads(gsum[0:1, :PAIR_PAD])
        v_sum = unpad_heads(gsum[0:1, 2 * PAIR_PAD :])
        gap = jnp.zeros((1, width - PAIR_DIM), F32)
        for c in range(2):

            @pl.when(core_of(meta) == (c if own else 1 - c))
            def _():
                rows_of = [jnp.concatenate([gap, t] if c else [t, gap], axis=1) for t in (q_sum, v_sum)]
                rows_of = [jnp.zeros((2, width), F32)] + rows_of + [jnp.zeros((VEC - 4, width), F32)]
                sums = jnp.concatenate(rows_of, axis=0).T
                lane = lax.broadcasted_iota(jnp.int32, sums.shape, 1)
                tail = jnp.where(lane == 0, gain_term, jnp.where(lane == 1, bias_term, sums))
                put_blocks(grads, tail[:, :VEC_PAIR].astype(BF16), 3 * PAIR_DIM, shards)


def attn_bwd(meta, qkv, xhat, lse, dattn, wpad, wf, own, shards, waits, carry):
    rows = dattn.shape[0]
    width = wf.shape[0]
    cols = 3 * PAIR_PAD
    out_shape = [jax.ShapeDtypeStruct(qkv.shape, BF16), jax.ShapeDtypeStruct(wf.shape, BF16)]
    in_specs = [slot_block(cols), slot_block(width), pl.BlockSpec((1, 8, 512), lambda i, m: (i, 0, 0))]
    in_specs += [whole(dattn), whole(wpad), whole(wf)]
    scratch = [
        pltpu.VMEM((rows + ROW_PAD, PAIR_PAD), F32),
        pltpu.VMEM((width, cols), F32),
        pltpu.VMEM((8, cols), F32),
    ]
    args = (meta, qkv, xhat, lse, dattn, wpad, wf)
    kernel = partial(attn_bwd_kernel, own=own, shards=shards)
    out_specs = [slot_block(cols), whole(wf)]
    grid = groups_at(meta)
    return call(kernel, "attn_bwd", grid, in_specs, out_specs, out_shape, scratch, args, waits, carry)


def input_grad_kernel(meta, tok, d0, d1, w0, w1, wf, dx1, out, tok32, bias):
    i = pl.program_id(0)
    rows, width = tok.shape

    @pl.when(i == 0)
    def _():
        tok32[:rows] = tok[...].astype(F32)
        tok32[rows:] = jnp.zeros((tok32.shape[0] - rows, width), F32)
        bias[...] = wf[:, 3 * PAIR_DIM :].astype(F32).T[0:8]

    start = meta[i]

    def work(length, padded):
        dn = dot_nt(d0[0, :padded, :], w0[...]) + dot_nt(d1[0, :padded, :], w1[...])
        xhat, inverse = row_norm(load_rows(tok32, start, padded))
        dx = row_norm_back(dn * bias[0:1, :], xhat, inverse)
        store_rows(tok32, start, length, dx, slice(None))

    by_group(meta[groups_at(meta) + i], work)

    @pl.when(i == pl.num_programs(0) - 1)
    def _():
        row = lax.broadcasted_iota(jnp.int32, (rows, 1), 0)
        total = dx1[...] + tok32[:rows]
        out[...] = jnp.where(row < rows_used(meta), total, 0.0).astype(BF16)


def input_grad(meta, tokens, d, w, wf, dx1, waits, carry):
    rows, width = tokens.shape
    slot = slot_block(d[0].shape[2])
    in_specs = [whole(tokens), slot, slot] + [whole(t) for t in (*w, wf, dx1)]
    scratch = [pltpu.VMEM((rows + ROW_PAD, width), F32), pltpu.VMEM((8, width), F32)]
    out_shape = [jax.ShapeDtypeStruct((rows, width), BF16)]
    args = (meta, tokens, *d, *w, wf, dx1)
    grid, out_specs = groups_at(meta), [whole(tokens)]
    return call(
        input_grad_kernel, "input_grad", grid, in_specs, out_specs, out_shape, scratch, args, waits, carry
    )


def turned(shards):
    count = shards.bit_length() - 1
    return [sum(((n >> b) & 1) << (count - 1 - b) for b in range(count)) for n in range(shards)]


def image_table(size_group, assignment, device, slots):
    owned = assignment == device
    rank = jnp.cumsum(owned.astype(jnp.int32)) - 1
    slot = jnp.arange(slots, dtype=jnp.int32)
    here = owned[None, :] & (rank[None, :] == slot[:, None])
    groups = jnp.sum(jnp.where(here, size_group[None, :], 0), axis=1)
    lengths = jnp.where(groups == 0, LENS[0], jnp.where(groups == 1, LENS[1], LENS[2]))
    ends = jnp.sum(jnp.where(slot[None, :] <= slot[:, None], lengths[None, :], 0), axis=1)
    return jnp.concatenate([ends - lengths, groups, ends[-1:], device[None]]).astype(jnp.int32)


def swap(value, axis, bit):
    size = lax.axis_size(axis)
    return lax.ppermute(value, axis, [(i, i ^ bit) for i in range(size)])


def sides_of(bits):
    table = {}
    for axis, those in bits.items():
        for bit in those:
            mine = (lax.axis_index(axis) & bit) // bit
            table[axis, bit] = (mine.astype(jnp.uint32), (1 - mine).astype(jnp.uint32), mine == 1)
    return table


def pick(sides, value, axis, bit, dim):
    mine, theirs, _ = sides[axis, bit]
    keep = lax.dynamic_index_in_dim(value, mine, dim, keepdims=False)
    send = lax.dynamic_index_in_dim(value, theirs, dim, keepdims=False)
    return keep, send


def join(upper, own, other, dim):
    return jnp.where(upper, jnp.stack([other, own], axis=dim), jnp.stack([own, other], axis=dim))


def added(keep, got):
    return (keep.astype(F32) + got.astype(F32)).astype(BF16)


def after(value, *others):
    return lax.optimization_barrier((value, *others))[0]


class Gather:
    def __init__(self, sides, part, keys):
        self.sides, self.part, self.keys, self.have = sides, part, keys, []

    def grow(self, axis, bit, *others, upper=None):
        if others:
            self.part = after(self.part, *others)
        upper = self.sides[axis, bit][2] if upper is None else upper
        dim = sum(self.keys.index(k) < self.keys.index((axis, bit)) for k in self.have)
        self.part = join(upper, self.part, swap(self.part, axis, bit), dim)
        self.have.append((axis, bit))
        return self


def body(
    tokens,
    cotangent,
    size_group,
    assignment,
    ln1_gain,
    ln1_bias,
    w_qkv,
    q_bias,
    v_bias,
    w_proj,
    proj_bias,
    ln2_gain,
    ln2_bias,
    w_up,
    up_bias,
    w_down,
    down_bias,
):
    rows, width = tokens.shape
    shards = lax.axis_size("fsdp")
    size = width // shards
    devices = shards * lax.axis_size("dp")
    device = lax.axis_index("fsdp") * lax.axis_size("dp") + lax.axis_index("dp")
    table = image_table(size_group, assignment, device, size_group.shape[0] // devices)

    bits = [1 << b for b in range(shards.bit_length() - 1)]
    far, near, y = bits[2:], bits[1:2], bits[0]
    tail_keys = [("fsdp", b) for b in reversed(bits)]
    sides = sides_of({"dp": (1, 2), "fsdp": bits})
    core, column = sides["dp", 1][0], sides["dp", 2][0]

    vectors = jnp.stack([ln1_gain, ln1_bias, q_bias, v_bias]).T
    pair = w_qkv.reshape(size, 3, 2, PAIR_DIM)
    pair = lax.dynamic_index_in_dim(pair, core, 2, keepdims=False).reshape(size, 3 * PAIR_DIM)
    pair = jnp.concatenate([pair, vectors, jnp.zeros((size, VEC_PAIR - 4), BF16)], axis=1)
    quarter = 2 * core + column
    vectors = jnp.stack([proj_bias, ln2_gain, ln2_bias, down_bias]).T
    extra = jnp.concatenate(
        [
            w_proj.reshape(size, width),
            vectors,
            up_bias.reshape(QUARTERS, size).T,
            jnp.zeros((size, VEC - 4 - QUARTERS), BF16),
        ],
        axis=1,
    )
    up = lax.dynamic_index_in_dim(w_up.reshape(size, shards, QUARTERS, size), quarter, 2, False)
    part_a = jnp.concatenate(
        [up.reshape(size, width), lax.dynamic_slice_in_dim(extra, quarter * VEC, VEC, 1)], axis=1
    )
    part_b = lax.dynamic_index_in_dim(w_down.reshape(QUARTERS, size, width), quarter, 0, False)

    f = Gather(sides, pair, tail_keys)
    ab = Gather(sides, jnp.concatenate([part_a, part_b], axis=1), [("dp", 2)] + tail_keys)
    for bit in far:
        ab.grow("fsdp", bit)
    for bit in near:
        f.grow("fsdp", bit)
    ab.grow("dp", 2, f.part)
    for bit in far:
        f.grow("fsdp", bit)
    for bit in near:
        ab.grow("fsdp", bit, f.part)
    f.grow("fsdp", y)
    own = f.part.reshape(width, -1)
    ab.part = after(ab.part, own)
    wf = (own, swap(own, "dp", 1))

    upper = jnp.broadcast_to(sides["fsdp", y][2], (8, ab.part.shape[-1])).astype(jnp.int32)
    table, sides, upper = lax.optimization_barrier((table, sides, upper))
    attn0, attn1, qkv0, qkv1, xhat, lse0, lse1, wpad0, wpad1, upper = attn_fwd(
        table, tokens, wf, (ab.part,), (upper,)
    )
    ab.grow("fsdp", y, upper=upper[0] != 0)
    w = ab.part.reshape(2, width, -1)
    w = (w, swap(w, "dp", 1))
    x1, act, dx1, dattn0, dattn1, keep_a, send_a, keep_b, send_b = mlp(
        table, tokens, cotangent, (attn0, attn1), w, shards
    )

    def by_bits(value, lead):
        if size % 16:
            value = value.reshape(value.shape[:lead] + (2,) * len(bits) + (size, value.shape[-1]))
            order = [lead + b for b in reversed(range(len(bits)))]
            return value.transpose(*range(lead), *order, *range(lead + len(bits), value.ndim))
        return value.reshape(value.shape[:lead] + (2,) * len(bits) + (size, value.shape[-1]))

    def halves_of_b(value):
        if size % 16:
            value = value.swapaxes(0, 1).reshape(2, width, width)
            return by_bits(value, 1).swapaxes(0, 1)
        return value.reshape((2, 2) + (2,) * (len(bits) - 1) + (size, width))

    got_a, got_b = swap(send_a, "dp", 1), swap(send_b, "dp", 1)
    d1, send_g, keep_a, keep_b = attn_bwd(
        table, qkv1, xhat, lse1, dattn1, wpad1, wf[1], False, shards, (send_a, send_b), (keep_a, keep_b)
    )
    got_g = swap(send_g, "dp", 1)
    keep_a, send_a = pick(sides, by_bits(added(keep_a, got_a), 1), "dp", 2, 0)
    keep_b, send_b = pick(sides, halves_of_b(added(keep_b, got_b)), "fsdp", y, 0)
    got_a, got_b = swap(send_a, "dp", 2), swap(send_b, "fsdp", y)
    d0, keep_g, keep_a, keep_b = attn_bwd(
        table, qkv0, xhat, lse0, dattn0, wpad0, wf[0], True, shards, (send_a, send_b, send_g), (keep_a, keep_b)
    )
    keep_g, send_g = pick(sides, by_bits(added(keep_g, got_g), 0), "fsdp", y, 0)
    keep_a, send_a = pick(sides, added(keep_a, got_a), "fsdp", y, 0)
    keep_b, send_b = pick(sides, added(keep_b, got_b), "dp", 2, 0)
    got_g = swap(send_g, "fsdp", y)
    got_a, got_b = swap(send_a, "fsdp", y), swap(send_b, "dp", 2)
    layer_out, keep_g, keep_a, keep_b = layer_output(
        table, x1, act, w, (send_g, send_a, send_b), (keep_g, keep_a, keep_b)
    )
    part_g = added(keep_g, got_g)
    part = jnp.concatenate([added(keep_a, got_a), added(keep_b, got_b)], axis=-1)
    for count, bit in enumerate(bits[1:]):
        keep_g, send_g = pick(sides, part_g, "fsdp", bit, 0)
        keep, send = pick(sides, part, "fsdp", bit, 0)
        got_g, got = swap(send_g, "fsdp", bit), swap(send, "fsdp", bit)
        if count == 0:
            grad_input, keep_g, keep = input_grad(
                table, tokens, (d0, d1), (wpad0, wpad1), wf[0], dx1, (send_g, send), (keep_g, keep)
            )
        part_g, part = added(keep_g, got_g), added(keep, got)
    part_g = added(part_g, swap(part_g, "dp", 2))
    part = join(sides["dp", 2][2], part, swap(part, "dp", 2), 0)
    part_g = join(sides["dp", 1][2], part_g, swap(part_g, "dp", 1), 0).astype(F32)
    part = join(sides["dp", 1][2], part, swap(part, "dp", 1), 0).astype(F32)

    grad_qkv = part_g[:, :, : 3 * PAIR_DIM].reshape(2, size, 3, PAIR_DIM).transpose(1, 2, 0, 3)
    ends = (part_g[0, :, 3 * PAIR_DIM : 3 * PAIR_DIM + 4] + part_g[1, :, 3 * PAIR_DIM : 3 * PAIR_DIM + 4]).T
    part = part.reshape(QUARTERS, size, -1)
    grad_up = part[:, :, :width].reshape(QUARTERS, size, shards, size).transpose(1, 2, 0, 3)
    extra = part[:, :, width : width + VEC].transpose(1, 0, 2).reshape(size, QUARTERS * VEC)
    more = extra[:, width : width + 4 + QUARTERS].T
    return (
        layer_out,
        grad_input,
        ends[0],
        ends[1],
        grad_qkv.reshape(-1),
        ends[2],
        ends[3],
        extra[:, :width].reshape(-1),
        more[0],
        more[1],
        more[2],
        grad_up.reshape(-1),
        more[4:].reshape(-1),
        part[:, :, width + VEC :].reshape(-1),
        more[3],
    )


def solution(mesh):
    rows = P(("fsdp", "dp"), None)
    flat = P("fsdp")
    return jax.shard_map(
        body,
        mesh=mesh,
        in_specs=(rows, rows, P(), P()) + (flat,) * 13,
        out_specs=(rows, rows) + (flat,) * 13,
        check_vma=False,
    )
```

time: 225 us -> 167 us (0.74)
  waiting for transfers between devices: 74 us -> 36.6 us
  Pallas kernels: 96.3 us -> 86.2 us
  other arithmetic: 15.1 us -> 6.16 us
    ppermute x22 -> x25, waiting for transfers between devices: 74 us -> 36.6 us  [swap(): return lax.ppermute(value, axis, [(i, i ^ bit) for i in range(size)])]
    pallas_call x3 -> x6, Pallas kernels: 96.3 us -> 86.2 us  [call(): pl.pallas_call(ordered, grid_spec=pltpu.PrefetchScalarGridSpec(num_scalar...]
    select_n x22 -> x12, other arithmetic: 9.09 us -> 0.84 us  [join(): jnp.where(upper, jnp.stack([other, own], axis=dim), jnp.stack([own, other...]
    another operation x9 -> x5, local copies, waits for them, and re-layouts: 3.57 us -> 0.56 us  [the longest x8 3.45 us: column(): return vector.reshape(-1, size).T]
    convert_element_type x10 -> x15, other arithmetic: 3.95 us -> 1.09 us  [the longest x13 0.99 us: added(): return (keep.astype(F32) + got.astype(F32)).astype(BF16)]
    another operation x3 -> x9, other arithmetic: 0.35 us -> 2.87 us  [the longest x4 1.79 us: join(): jnp.stack([other, own], axis=dim)]
    ppermute x22 -> x25, starting transfers between devices: 21.6 us -> 22.7 us  [swap(): return lax.ppermute(value, axis, [(i, i ^ bit) for i in range(size)])]
    reshape x13 -> x14, local copies, waits for them, and re-layouts: 7.48 us -> 8.26 us  [the longest x1 1.34 us: body(): grad_up.reshape(-1)]
  transfers between devices with their start and end apart: 22 -> 25, of which waited for: 14 -> 11; matrix products, arithmetic and copies ran while one was open for 6% -> 4% of each run, Pallas kernels for 22% -> 35%
where the time goes in v2:
time: 167 us
  Pallas kernels  86.2 us (52%)
  waiting for transfers between devices  36.6 us (22%)
  starting transfers between devices  22.7 us (14%)
  local copies, waits for them, and re-layouts  14.3 us (9%)
  other arithmetic  6.16 us (4%)
    pallas_call x6, Pallas kernels, call(): pl.pallas_call(ordered, grid_spec=pltpu.PrefetchScalarGridSpec(num_scalar...  86.2 us
    ppermute x25, waiting for transfers between devices, swap(): return lax.ppermute(value, axis, [(i, i ^ bit) for i in range(size)])  36.6 us
    ppermute x25, starting transfers between devices, swap(): return lax.ppermute(value, axis, [(i, i ^ bit) for i in range(size)])  22.7 us
  transfers between devices with their start and end apart: 25, of which 11 were waited for; matrix products, arithmetic and copies ran while one was open for 4% of the time, Pallas kernels for 35%

profile of v2, /device:TPU:0, one launch (start us, length us, event | category | flops | bytes accessed | tf_op | source)
XLA Modules:
  0.0 167.3 jit_solution(17394683864847905581)
XLA Ops:
  6.5 4.1 %collective-permute-start.4 = (bf16[48,896]{1,0:T(8,128)(2,1)S(1)}, bf16[48,896]{1,0:T(8,128)(2,1)S(1)}, u32[]{:S(2)}, u32[]{:S(2)}) collective-permute-start(bf16[48,896]{1,0:T(8,128)(2,1)S(1)} %get-tuple-element.137), channel_id=1, source_target_pairs={{0,16},{4,20},{8,24},{12,28},{16,0},{20,4},{24,8},{28,12},{1,17},{... | collective-permute-start | bytes 258056 | tf_op jit(solution)/shard_map/ppermute | solution.py:557
  11.7 1.6 collective-permute-start
  14.2 1.7 %collective-permute-done = bf16[48,640]{1,0:T(8,128)(2,1)S(1)} collective-permute-done((bf16[48,640]{1,0:T(8,128)(2,1)S(1)}, bf16[48,640]{1,0:T(8,128)(2,1)S(1)}, u32[]{:S(2)}, u32[]{:S(2)}) %collective-permute-start) | collective-permute-done | bytes 61472 | tf_op jit(solution)/shard_map/ppermute | solution.py:557
  17.2 1.6 collective-permute-start.5
  18.7 5.0 %collective-permute-done.1 = bf16[2,48,640]{2,1,0:T(8,128)(2,1)S(1)} collective-permute-done((bf16[2,48,640]{2,1,0:T(8,128)(2,1)S(1)}, bf16[2,48,640]{2,1,0:T(8,128)(2,1)S(1)}, u32[]{:S(2)}, u32[]{:S(2)}) %collective-permute-start.1) | collective-permute-done | bytes 122912 | tf_op jit(solution)/shard_map/ppermute | solution.py:557
  23.7 1.9 %collective-permute-start.2 = (bf16[2,2,48,640]{3,2,1,0:T(8,128)(2,1)S(1)}, bf16[2,2,48,640]{3,2,1,0:T(8,128)(2,1)S(1)}, u32[]{:S(2)}, u32[]{:S(2)}) collective-permute-start(bf16[2,2,48,640]{3,2,1,0:T(8,128)(2,1)S(1)} %maximum_select_fusion.4), channel_id=1, source_target_pairs={{0,4},{4,0},{8,12},{12,8},{16,20},{20,16},{24,28},{28,24},{1,5},{5... | collective-permute-start | bytes 737288 | tf_op jit(solution)/shard_map/ppermute | solution.py:557
  25.9 5.5 %collective-permute-done.2 = bf16[2,2,48,640]{3,2,1,0:T(8,128)(2,1)S(1)} collective-permute-done((bf16[2,2,48,640]{3,2,1,0:T(8,128)(2,1)S(1)}, bf16[2,2,48,640]{3,2,1,0:T(8,128)(2,1)S(1)}, u32[]{:S(2)}, u32[]{:S(2)}) %collective-permute-start.2) | collective-permute-done | bytes 245792 | tf_op jit(solution)/shard_map/ppermute | solution.py:557
  31.6 3.5 %collective-permute-done.6 = bf16[2,2,48,896]{3,2,1,0:T(8,128)(2,1)S(1)} collective-permute-done((bf16[2,2,48,896]{3,2,1,0:T(8,128)(2,1)S(1)}, bf16[2,2,48,896]{3,2,1,0:T(8,128)(2,1)S(1)}, u32[]{:S(2)}, u32[]{:S(2)}) %collective-permute-start.6) | collective-permute-done | bytes 344096 | tf_op jit(solution)/shard_map/ppermute | solution.py:557
  37.0 17.1 %attn_fwd.1 = (bf16[2048,256]{1,0:T(8,128)(2,1)S(1)}, bf16[2048,256]{1,0:T(8,128)(2,1)S(1)}, bf16[8,400,768]{2,1,0:T(8,128)(2,1)S(1)}, bf16[8,400,768]{2,1,0:T(8...) custom-call(s32[18]{0:T(128)S(1)} %pad_add_fusion.refs_0_, ...), custom_call_target="tpu_custom_call", output_to_operand_aliasing={{9}: (5, {})} | custom-call | tf_op jit(solution)/shard_map/attn_fwd/pallas_call | solution.py:117
  54.2 1.6 pad_maximum_fusion
  56.5 3.1 %collective-permute-done.8.refs_6_.refs_4_ = bf16[2,384,896]{2,1,0:T(8,128)(2,1)S(1)} collective-permute-done((bf16[2,384,896]{2,1,0:T(8,128)(2,1)S(1)}, bf16[2,384,896]{2,1,0:T(8,128)(2,1)S(1)}, u32[]{:S(2)}, u32[]{:S(2)}) %collective-permute-start.8) | collective-permute-done | bytes 1376288 | tf_op jit(solution)/shard_map/ppermute | solution.py:557
  59.6 27.8 %mlp.1 = (f32[2048,384]{1,0:T(8,128)}, bf16[2048,1536]{1,0:T(8,128)(2,1)}, f32[2048,384]{1,0:T(8,128)}, bf16[2048,256]{1,0:T(8,128)(2,1)S(1)}, bf16[2048,256]{1,...) custom-call(s32[18]{0:T(128)S(1)} %pad_add_fusion.refs_0_, ...), custom_call_target="tpu_custom_call" | custom-call | tf_op jit(solution)/shard_map/mlp/pallas_call | solution.py:117
  87.9 12.3 %attn_bwd.2 = (bf16[8,400,768]{2,1,0:T(8,128)(2,1)S(1)}, bf16[384,640]{1,0:T(8,128)(2,1)S(1)}, bf16[2,384,512]{2,1,0:T(8,128)(2,1)S(1)}, bf16[2,2,192,384]{3,2,1,0:T(8,128)(2,1)S(1)}) custom-call(s32[18]{0:T(128)S(1)} %pad_add_fusion.refs_0_, bf16[8,400,768]{2,1,0:T(8,128)(2,1)S(1)} %get-tuple-element.79.refs_1_, ...), custom_call_target="tpu_custom_call", output_to_operand_aliasing={{2}: (9, {}), {3}: (10, {})} | custom-call | tf_op jit(solution)/shard_map/attn_bwd/pallas_call | solution.py:117
  100.9 3.3 %collective-permute-start.12 = (bf16[2,2,2,48,512]{4,3,2,1,0:T(8,128)(2,1)S(1)}, bf16[2,2,2,48,512]{4,3,2,1,0:T(8,128)(2,1)S(1)}, u32[]{:S(2)}, u32[]{:S(2)}) collective-permute-start(bf16[2,2,2,48,512]{4,3,2,1,0:T(8,128)(2,1)S(1)} %get-tuple-element.122.refs_7_), channel_id=1, source_target_pairs={{0,2},{1,3},{2,0},{3,1},{4,6},{5,7},{6,4},{7,5},{8,10},{9,11},{10,... | collective-permute-start | bytes 1179656 | tf_op jit(solution)/shard_map/ppermute | solution.py:557
  104.2 12.1 %attn_bwd.3 = (bf16[8,400,768]{2,1,0:T(8,128)(2,1)S(1)}, bf16[384,640]{1,0:T(8,128)(2,1)S(1)}, bf16[2,2,2,48,512]{4,3,2,1,0:T(8,128)(2,1)S(1)}, bf16[2,2,2,48,384]{4,3,2,1,0:T(8,128)(2,1)S(1)}) custom-call(s32[18]{0:T(128)S(1)} %pad_add_fusion.refs_0_, ...), custom_call_target="tpu_custom_call", output_to_operand_aliasing={{2}: (10, {}), {3}: (11, {})} | custom-call | tf_op jit(solution)/shard_map/attn_bwd/pallas_call | solution.py:117
  119.0 8.2 %layer_out.1 = (bf16[2048,384]{1,0:T(8,128)(2,1)}, bf16[2,2,48,640]{3,2,1,0:T(8,128)(2,1)S(1)}, bf16[2,2,48,512]{3,2,1,0:T(8,128)(2,1)S(1)}, bf16[2,2,48,384]{3,2,1,0:T(8,128)(2,1)S(1)}) custom-call(s32[18]{0:T(128)S(1)} %pad_add_fusion.refs_0_, f32[2048,384]{1,0:T(8,128)} %get-tuple-element.72.refs_1_, ...), custom_call_target="tpu_custom_call", output_to_operand_aliasing={{1}: (8, {}), {2}: (9, {}), {3}: (10, {})} | custom-call | tf_op jit(solution)/shard_map/layer_out/pallas_call | solution.py:117
  128.3 8.8 %input_grad.1 = (bf16[2048,384]{1,0:T(8,128)(2,1)}, bf16[2,48,640]{2,1,0:T(8,128)(2,1)S(1)}, bf16[2,48,896]{2,1,0:T(8,128)(2,1)S(1)}) custom-call(s32[18]{0:T(128)S(1)} %pad_add_fusion.refs_0_, bf16[2048,384]{1,0:T(8,128)(2,1)S(1)} %copy-done, bf16[8,400,768]{2,1,0:T(8,128)(2,1)S(1)} %get-tuple-element.98.refs_2_, ...), custom_call_target="tpu_custom_call", output_to_operand_aliasing={{1}: (10, {}), {2}: (11, {})} | custom-call | tf_op jit(solution)/shard_map/input_grad/pallas_call | solution.py:117
  137.2 5.8 %collective-permute-done.18 = bf16[48,640]{1,0:T(8,128)(2,1)S(1)} collective-permute-done((bf16[48,640]{1,0:T(8,128)(2,1)S(1)}, bf16[48,640]{1,0:T(8,128)(2,1)S(1)}, u32[]{:S(2)}, u32[]{:S(2)}) %collective-permute-start.18) | collective-permute-done | bytes 61472 | tf_op jit(solution)/shard_map/ppermute | solution.py:557
  143.7 2.5 %collective-permute-start.21 = (bf16[2,48,896]{2,1,0:T(8,128)(2,1)S(1)}, bf16[2,48,896]{2,1,0:T(8,128)(2,1)S(1)}, u32[]{:S(2)}, u32[]{:S(2)}) collective-permute-start(bf16[2,48,896]{2,1,0:T(8,128)(2,1)S(1)} %get-tuple-element.132.refs_9_), channel_id=1, source_target_pairs={{0,8},{4,12},{8,0},{12,4},{16,24},{20,28},{24,16},{28,20},{1,9},{5... | collective-permute-start | bytes 516104 | tf_op jit(solution)/shard_map/ppermute | solution.py:557
  147.4 2.3 %collective-permute-done.21 = bf16[2,48,896]{2,1,0:T(8,128)(2,1)S(1)} collective-permute-done((bf16[2,48,896]{2,1,0:T(8,128)(2,1)S(1)}, bf16[2,48,896]{2,1,0:T(8,128)(2,1)S(1)}, u32[]{:S(2)}, u32[]{:S(2)}) %collective-permute-start.21) | collective-permute-done | bytes 172064 | tf_op jit(solution)/shard_map/ppermute | solution.py:557
  149.9 5.3 %collective-permute-done.22 = bf16[48,896]{1,0:T(8,128)(2,1)S(1)} collective-permute-done((bf16[48,896]{1,0:T(8,128)(2,1)S(1)}, bf16[48,896]{1,0:T(8,128)(2,1)S(1)}, u32[]{:S(2)}, u32[]{:S(2)}) %collective-permute-start.22) | collective-permute-done | bytes 86048 | tf_op jit(solution)/shard_map/ppermute | solution.py:557
  155.3 1.8 %collective-permute-start.23 = (bf16[48,896]{1,0:T(8,128)(2,1)S(1)}, bf16[48,896]{1,0:T(8,128)(2,1)S(1)}, u32[]{:S(2)}, u32[]{:S(2)}) collective-permute-start(bf16[48,896]{1,0:T(8,128)(2,1)S(1)} %fusion.4), channel_id=1, source_target_pairs={{0,2},{1,3},{2,0},{3,1},{4,6},{5,7},{6,4},{7,5},{8,10},{9,11},{10,... | collective-permute-start | bytes 258056 | tf_op jit(solution)/shard_map/ppermute | solution.py:557
  157.1 2.7 %collective-permute-done.23 = bf16[48,896]{1,0:T(8,128)(2,1)S(1)} collective-permute-done((bf16[48,896]{1,0:T(8,128)(2,1)S(1)}, bf16[48,896]{1,0:T(8,128)(2,1)S(1)}, u32[]{:S(2)}, u32[]{:S(2)}) %collective-permute-start.23) | collective-permute-done | bytes 86048 | tf_op jit(solution)/shard_map/ppermute | solution.py:557
  163.8 1.3 reshape.395
  (150 shorter events, 25.1 us)
Async XLA Ops:
  6.5 10.6 %collective-permute-start.4 = (bf16[48,896]{1,0:T(8,128)(2,1)S(1)}, bf16[48,896]{1,0:T(8,128)(2,1)S(1)}, u32[]{:S(2)}, u32[]{:S(2)}) collective-permute-start(bf16[48,896]{1,0:T(8,128)(2,1)S(1)} %get-tuple-element.137), channel_id=1, source_target_pairs={{0,16},{4,20},{8,24},{12,28},{16,0},{20,4},{24,8},{28,12},{1,17},{... | collective-permute-start | bytes 258056 | tf_op jit(solution)/shard_map/ppermute | solution.py:557
  11.7 4.2 %collective-permute-start = (bf16[48,640]{1,0:T(8,128)(2,1)S(1)}, bf16[48,640]{1,0:T(8,128)(2,1)S(1)}, u32[]{:S(2)}, u32[]{:S(2)}) collective-permute-start(bf16[48,640]{1,0:T(8,128)(2,1)S(1)} %maximum_maximum_fusion), channel_id=1, source_target_pairs={{0,8},{4,12},{8,0},{12,4},{16,24},{20,28},{24,16},{28,20},{1,9},{5... | collective-permute-start | bytes 184328 | tf_op jit(solution)/shard_map/ppermute | solution.py:557
  16.0 7.7 %collective-permute-start.1 = (bf16[2,48,640]{2,1,0:T(8,128)(2,1)S(1)}, bf16[2,48,640]{2,1,0:T(8,128)(2,1)S(1)}, u32[]{:S(2)}, u32[]{:S(2)}) collective-permute-start(bf16[2,48,640]{2,1,0:T(8,128)(2,1)S(1)} %maximum_select_fusion.9), channel_id=1, source_target_pairs={{0,16},{4,20},{8,24},{12,28},{16,0},{20,4},{24,8},{28,12},{1,17},{... | collective-permute-start | bytes 368648 | tf_op jit(solution)/shard_map/ppermute | solution.py:557
  17.2 8.5 %collective-permute-start.5 = (bf16[2,48,896]{2,1,0:T(8,128)(2,1)S(1)}, bf16[2,48,896]{2,1,0:T(8,128)(2,1)S(1)}, u32[]{:S(2)}, u32[]{:S(2)}) collective-permute-start(bf16[2,48,896]{2,1,0:T(8,128)(2,1)S(1)} %maximum_select_fusion.6), channel_id=1, source_target_pairs={{0,2},{1,3},{2,0},{3,1},{4,6},{5,7},{6,4},{7,5},{8,10},{9,11},{10,... | collective-permute-start | bytes 516104 | tf_op jit(solution)/shard_map/ppermute | solution.py:557
  23.7 7.7 %collective-permute-start.2 = (bf16[2,2,48,640]{3,2,1,0:T(8,128)(2,1)S(1)}, bf16[2,2,48,640]{3,2,1,0:T(8,128)(2,1)S(1)}, u32[]{:S(2)}, u32[]{:S(2)}) collective-permute-start(bf16[2,2,48,640]{3,2,1,0:T(8,128)(2,1)S(1)} %maximum_select_fusion.4), channel_id=1, source_target_pairs={{0,4},{4,0},{8,12},{12,8},{16,20},{20,16},{24,28},{28,24},{1,5},{5... | collective-permute-start | bytes 737288 | tf_op jit(solution)/shard_map/ppermute | solution.py:557
  25.7 9.4 %collective-permute-start.6 = (bf16[2,2,48,896]{3,2,1,0:T(8,128)(2,1)S(1)}, bf16[2,2,48,896]{3,2,1,0:T(8,128)(2,1)S(1)}, u32[]{:S(2)}, u32[]{:S(2)}) collective-permute-start(bf16[2,2,48,896]{3,2,1,0:T(8,128)(2,1)S(1)} %maximum_select_fusion.2), channel_id=1, source_target_pairs={{0,8},{4,12},{8,0},{12,4},{16,24},{20,28},{24,16},{28,20},{1,9},{5... | collective-permute-start | bytes 1032200 | tf_op jit(solution)/shard_map/ppermute | solution.py:557
  31.6 5.5 %collective-permute-start.3 = (bf16[384,640]{1,0:T(8,128)(2,1)S(1)}, bf16[384,640]{1,0:T(8,128)(2,1)S(1)}, u32[]{:S(2)}, u32[]{:S(2)}) collective-permute-start(bf16[384,640]{1,0:T(8,128)(2,1)S(1)} %bitcast.114), channel_id=1, source_target_pairs={{0,1},{1,0},{2,3},{3,2},{4,5},{5,4},{6,7},{7,6},{8,9},{9,8},{10,11... | collective-permute-start | bytes 1474568 | tf_op jit(solution)/shard_map/ppermute | solution.py:557
  35.2 18.9 %collective-permute-start.7 = (bf16[2,2,2,48,896]{4,3,2,1,0:T(8,128)(2,1)S(1)}, bf16[2,2,2,48,896]{4,3,2,1,0:T(8,128)(2,1)}, u32[]{:S(2)}, u32[]{:S(2)}) collective-permute-start(bf16[2,2,2,48,896]{4,3,2,1,0:T(8,128)(2,1)S(1)} %maximum_select_fusion.refs_4_), channel_id=1, source_target_pairs={{0,4},{4,0},{8,12},{12,8},{16,20},{20,16},{24,28},{28,24},{1,5},{5... | collective-permute-start | bytes 2064392 | tf_op jit(solution)/shard_map/ppermute | solution.py:557
  56.4 3.2 %collective-permute-start.8 = (bf16[2,384,896]{2,1,0:T(8,128)(2,1)S(1)}, bf16[2,384,896]{2,1,0:T(8,128)(2,1)S(1)}, u32[]{:S(2)}, u32[]{:S(2)}) collective-permute-start(bf16[2,384,896]{2,1,0:T(8,128)(2,1)S(1)} %bitcast_select_fusion.refs_5_.refs_3_), channel_id=1, source_target_pairs={{0,1},{1,0},{2,3},{3,2},{4,5},{5,4},{6,7},{7,6},{8,9},{9,8},{10,11... | collective-permute-start | bytes 4128776 | tf_op jit(solution)/shard_map/ppermute | solution.py:557
  87.4 12.9 %collective-permute-start.10 = (bf16[2,2,192,384]{3,2,1,0:T(8,128)(2,1)S(1)}, bf16[2,2,192,384]{3,2,1,0:T(8,128)(2,1)S(1)}, u32[]{:S(2)}, u32[]{:S(2)}) collective-permute-start(bf16[2,2,192,384]{3,2,1,0:T(8,128)(2,1)S(1)} %get-tuple-element.84.refs_8_), channel_id=1, source_target_pairs={{0,1},{1,0},{2,3},{3,2},{4,5},{5,4},{6,7},{7,6},{8,9},{9,8},{10,11... | collective-permute-start | bytes 1769480 | tf_op jit(solution)/shard_map/ppermute | solution.py:557
  87.5 13.1 %collective-permute-start.9 = (bf16[2,384,512]{2,1,0:T(8,128)(2,1)S(1)}, bf16[2,384,512]{2,1,0:T(8,128)(2,1)S(1)}, u32[]{:S(2)}, u32[]{:S(2)}) collective-permute-start(bf16[2,384,512]{2,1,0:T(8,128)(2,1)S(1)} %get-tuple-element.83.refs_7_), channel_id=1, source_target_pairs={{0,1},{1,0},{2,3},{3,2},{4,5},{5,4},{6,7},{7,6},{8,9},{9,8},{10,11... | collective-permute-start | bytes 2359304 | tf_op jit(solution)/shard_map/ppermute | solution.py:557
  100.2 16.1 %collective-permute-start.11 = (bf16[384,640]{1,0:T(8,128)(2,1)S(1)}, bf16[384,640]{1,0:T(8,128)(2,1)S(1)}, u32[]{:S(2)}, u32[]{:S(2)}) collective-permute-start(bf16[384,640]{1,0:T(8,128)(2,1)S(1)} %get-tuple-element.91.refs_9_), channel_id=1, source_target_pairs={{0,1},{1,0},{2,3},{3,2},{4,5},{5,4},{6,7},{7,6},{8,9},{9,8},{10,11... | collective-permute-start | bytes 1474568 | tf_op jit(solution)/shard_map/ppermute | solution.py:557
  100.6 16.0 %collective-permute-start.13 = (bf16[2,2,2,48,384]{4,3,2,1,0:T(8,128)(2,1)S(1)}, bf16[2,2,2,48,384]{4,3,2,1,0:T(8,128)(2,1)S(1)}, u32[]{:S(2)}, u32[]{:S(2)}) collective-permute-start(bf16[2,2,2,48,384]{4,3,2,1,0:T(8,128)(2,1)S(1)} %get-tuple-element.126.refs_8_), channel_id=1, source_target_pairs={{0,4},{4,0},{8,12},{12,8},{16,20},{20,16},{24,28},{28,24},{1,5},{5... | collective-permute-start | bytes 884744 | tf_op jit(solution)/shard_map/ppermute | solution.py:557
  100.9 16.6 %collective-permute-start.12 = (bf16[2,2,2,48,512]{4,3,2,1,0:T(8,128)(2,1)S(1)}, bf16[2,2,2,48,512]{4,3,2,1,0:T(8,128)(2,1)S(1)}, u32[]{:S(2)}, u32[]{:S(2)}) collective-permute-start(bf16[2,2,2,48,512]{4,3,2,1,0:T(8,128)(2,1)S(1)} %get-tuple-element.122.refs_7_), channel_id=1, source_target_pairs={{0,2},{1,3},{2,0},{3,1},{4,6},{5,7},{6,4},{7,5},{8,10},{9,11},{10,... | collective-permute-start | bytes 1179656 | tf_op jit(solution)/shard_map/ppermute | solution.py:557
  116.5 10.7 %collective-permute-start.14 = (bf16[2,2,48,640]{3,2,1,0:T(8,128)(2,1)S(1)}, bf16[2,2,48,640]{3,2,1,0:T(8,128)(2,1)S(1)}, u32[]{:S(2)}, u32[]{:S(2)}) collective-permute-start(bf16[2,2,48,640]{3,2,1,0:T(8,128)(2,1)S(1)} %get-tuple-element.128.refs_5_), channel_id=1, source_target_pairs={{0,4},{4,0},{8,12},{12,8},{16,20},{20,16},{24,28},{28,24},{1,5},{5... | collective-permute-start | bytes 737288 | tf_op jit(solution)/shard_map/ppermute | solution.py:557
  116.7 11.0 %collective-permute-start.16 = (bf16[2,2,48,384]{3,2,1,0:T(8,128)(2,1)S(1)}, bf16[2,2,48,384]{3,2,1,0:T(8,128)(2,1)S(1)}, u32[]{:S(2)}, u32[]{:S(2)}) collective-permute-start(bf16[2,2,48,384]{3,2,1,0:T(8,128)(2,1)S(1)} %get-tuple-element.134.refs_7_), channel_id=1, source_target_pairs={{0,2},{1,3},{2,0},{3,1},{4,6},{5,7},{6,4},{7,5},{8,10},{9,11},{10,... | collective-permute-start | bytes 442376 | tf_op jit(solution)/shard_map/ppermute | solution.py:557
  117.7 10.5 %collective-permute-start.15 = (bf16[2,2,48,512]{3,2,1,0:T(8,128)(2,1)S(1)}, bf16[2,2,48,512]{3,2,1,0:T(8,128)(2,1)S(1)}, u32[]{:S(2)}, u32[]{:S(2)}) collective-permute-start(bf16[2,2,48,512]{3,2,1,0:T(8,128)(2,1)S(1)} %get-tuple-element.130.refs_6_), channel_id=1, source_target_pairs={{0,4},{4,0},{8,12},{12,8},{16,20},{20,16},{24,28},{28,24},{1,5},{5... | collective-permute-start | bytes 589832 | tf_op jit(solution)/shard_map/ppermute | solution.py:557
  127.3 9.8 %collective-permute-start.17 = (bf16[2,48,640]{2,1,0:T(8,128)(2,1)S(1)}, bf16[2,48,640]{2,1,0:T(8,128)(2,1)S(1)}, u32[]{:S(2)}, u32[]{:S(2)}) collective-permute-start(bf16[2,48,640]{2,1,0:T(8,128)(2,1)S(1)} %get-tuple-element.136.refs_8_), channel_id=1, source_target_pairs={{0,8},{4,12},{8,0},{12,4},{16,24},{20,28},{24,16},{28,20},{1,9},{5... | collective-permute-start | bytes 368648 | tf_op jit(solution)/shard_map/ppermute | solution.py:557
  137.1 5.8 %collective-permute-start.18 = (bf16[48,640]{1,0:T(8,128)(2,1)S(1)}, bf16[48,640]{1,0:T(8,128)(2,1)S(1)}, u32[]{:S(2)}, u32[]{:S(2)}) collective-permute-start(bf16[48,640]{1,0:T(8,128)(2,1)S(1)} %dynamic-slice_bitcast_fusion.13), channel_id=1, source_target_pairs={{0,16},{4,20},{8,24},{12,28},{16,0},{20,4},{24,8},{28,12},{1,17},{... | collective-permute-start | bytes 184328 | tf_op jit(solution)/shard_map/ppermute | solution.py:557
  143.0 4.3 %collective-permute-start.19 = (bf16[48,640]{1,0:T(8,128)(2,1)S(1)}, bf16[48,640]{1,0:T(8,128)(2,1)S(1)}, u32[]{:S(2)}, u32[]{:S(2)}) collective-permute-start(bf16[48,640]{1,0:T(8,128)(2,1)S(1)} %fusion.6), channel_id=1, source_target_pairs={{0,2},{1,3},{2,0},{3,1},{4,6},{5,7},{6,4},{7,5},{8,10},{9,11},{10,... | collective-permute-start | bytes 184328 | tf_op jit(solution)/shard_map/ppermute | solution.py:557
  143.7 6.1 %collective-permute-start.21 = (bf16[2,48,896]{2,1,0:T(8,128)(2,1)S(1)}, bf16[2,48,896]{2,1,0:T(8,128)(2,1)S(1)}, u32[]{:S(2)}, u32[]{:S(2)}) collective-permute-start(bf16[2,48,896]{2,1,0:T(8,128)(2,1)S(1)} %get-tuple-element.132.refs_9_), channel_id=1, source_target_pairs={{0,8},{4,12},{8,0},{12,4},{16,24},{20,28},{24,16},{28,20},{1,9},{5... | collective-permute-start | bytes 516104 | tf_op jit(solution)/shard_map/ppermute | solution.py:557
  147.3 2.6 %collective-permute-start.20 = (bf16[48,640]{1,0:T(8,128)(2,1)S(1)}, bf16[48,640]{1,0:T(8,128)(2,1)S(1)}, u32[]{:S(2)}, u32[]{:S(2)}) collective-permute-start(bf16[48,640]{1,0:T(8,128)(2,1)S(1)} %add_convert_fusion.10), channel_id=1, source_target_pairs={{0,1},{1,0},{2,3},{3,2},{4,5},{5,4},{6,7},{7,6},{8,9},{9,8},{10,11... | collective-permute-start | bytes 184328 | tf_op jit(solution)/shard_map/ppermute | solution.py:557
  149.8 5.4 %collective-permute-start.22 = (bf16[48,896]{1,0:T(8,128)(2,1)S(1)}, bf16[48,896]{1,0:T(8,128)(2,1)S(1)}, u32[]{:S(2)}, u32[]{:S(2)}) collective-permute-start(bf16[48,896]{1,0:T(8,128)(2,1)S(1)} %dynamic-slice_bitcast_fusion.12), channel_id=1, source_target_pairs={{0,16},{4,20},{8,24},{12,28},{16,0},{20,4},{24,8},{28,12},{1,17},{... | collective-permute-start | bytes 258056 | tf_op jit(solution)/shard_map/ppermute | solution.py:557
  155.3 4.6 %collective-permute-start.23 = (bf16[48,896]{1,0:T(8,128)(2,1)S(1)}, bf16[48,896]{1,0:T(8,128)(2,1)S(1)}, u32[]{:S(2)}, u32[]{:S(2)}) collective-permute-start(bf16[48,896]{1,0:T(8,128)(2,1)S(1)} %fusion.4), channel_id=1, source_target_pairs={{0,2},{1,3},{2,0},{3,1},{4,6},{5,7},{6,4},{7,5},{8,10},{9,11},{10,... | collective-permute-start | bytes 258056 | tf_op jit(solution)/shard_map/ppermute | solution.py:557
  (11 other events, 94.6 us)

commit v3 on v2

--- a/solution.py
+++ b/solution.py
@@ -22,7 +22,7 @@
 SCALE = 1.0 / math.sqrt(HEAD_DIM)
 EXP_SCALE = SCALE * math.log2(math.e)
 MIB = 1024 * 1024
-VMEM = {"attn_fwd": 12, "mlp": 21, "attn_bwd": 8, "layer_out": 8, "input_grad": 10}
+VMEM = {"attn_fwd": 12, "mlp": 26, "attn_bwd": 8, "layer_out": 8, "input_grad": 10, "finish": 10}
 F32 = jnp.float32
 BF16 = jnp.bfloat16
 
@@ -180,24 +180,29 @@
         xhat, _ = row_norm(load_rows(tok32, start, padded))
         normed = (xhat * bias[0:1, :width] + bias[1:2, :width]).astype(BF16)
         xhat_out[0, :padded, :] = xhat.astype(BF16)
-        outs = []
         for p, (_, qkv, lse, wpad) in enumerate(sides):
             qkv[0, :padded, :] = (dot_nn(normed, wpad[...]) + bias[2 + p : 3 + p, :]).astype(BF16)
-            for h in range(PAIR):
-                at = h * HEAD_PAD
-                q = qkv[0, :padded, at : at + HEAD_PAD]
-                k = qkv[0, :padded, PAIR_PAD + at : PAIR_PAD + at + HEAD_PAD]
-                v = qkv[0, :padded, 2 * PAIR_PAD + at : 2 * PAIR_PAD + at + HEAD_PAD]
-                s = dot_nt(k, q)
-                if length < padded:
-                    key = lax.broadcasted_iota(jnp.int32, s.shape, 0)
-                    s = jnp.where(key < length, s, -1e30)
-                top = jnp.max(s, axis=0, keepdims=True)
-                e = jnp.exp2((s - top) * EXP_SCALE)
-                total = jnp.sum(e, axis=0, keepdims=True)
-                probs = (e * (1.0 / total)).astype(BF16)
-                lse[0, h : h + 1, :padded] = top * EXP_SCALE + jnp.log2(total)
-                outs.append(dot_tn(probs, v))
+        heads = [(p, h) for p in range(2) for h in range(PAIR)]
+        scores = []
+        for p, h in heads:
+            qkv, at = sides[p][1], h * HEAD_PAD
+            q = qkv[0, :padded, at : at + HEAD_PAD]
+            k = qkv[0, :padded, PAIR_PAD + at : PAIR_PAD + at + HEAD_PAD]
+            scores.append(dot_nt(k, q))
+        probs = []
+        for (p, h), s in zip(heads, scores):
+            if length < padded:
+                key = lax.broadcasted_iota(jnp.int32, s.shape, 0)
+                s = jnp.where(key < length, s, -1e30)
+            top = jnp.max(s, axis=0, keepdims=True)
+            e = jnp.exp2((s - top) * EXP_SCALE)
+            total = jnp.sum(e, axis=0, keepdims=True)
+            probs.append((e * (1.0 / total)).astype(BF16))
+            sides[p][2][0, h : h + 1, :padded] = top * EXP_SCALE + jnp.log2(total)
+        outs = []
+        for (p, h), prob in zip(heads, probs):
+            at = 2 * PAIR_PAD + h * HEAD_PAD
+            outs.append(dot_tn(prob, sides[p][1][0, :padded, at : at + HEAD_PAD]))
         store_rows(out32, start, length, jnp.concatenate(outs, axis=1), slice(None))
 
     by_group(meta[groups_at(meta) + i], work)
@@ -250,11 +255,12 @@
         to[at : at + size, col : col + cols] = value[n * size : (n + 1) * size]
 
 
-def mlp_kernel(meta, tok, cot, attn0, attn1, w0, w1, x1o, acto, dx1, da0, da1,
+def mlp_kernel(meta, tok, cot, attn0, attn1, w0, w1, b0, b1, x1o, acto, dx1, da0, da1,
                keep_a, send_a, keep_b, send_b, wproj, rowvec, gd, gu, gp, gsum, *, shards):
     i = pl.program_id(0)
     rows, width = tok.shape
     parts = (w0, w1)
+    lower = (b0, b1)
 
     def in_order(first, second, use):
         for c in range(2):
@@ -284,30 +290,35 @@
     proj_bias, gain, shift, down_bias = [rowvec[r : r + 1, :width] for r in range(4)]
     row = lax.broadcasted_iota(jnp.int32, (rows, 1), 0) + i * rows
     valid = (row < rows_used(meta)).astype(F32)
+    dy = cot[...].astype(F32) * valid
+    dyb = dy.astype(BF16)
+    chunk = 2 * width
+    ups = [jnp.concatenate([parts[c][0][:, :width], parts[c][1][:, :width]], axis=1) for c in range(2)]
+    downs = [jnp.concatenate([lower[c][x] for x in range(2)], axis=0) for c in range(2)]
+    dacts = [dot_nt(dyb, downs[c]) for c in range(2)]
     mixed0, mixed1 = attn0[...], attn1[...]
     x1 = tok[...].astype(F32) + dot_nn(mixed0, wproj[:PAIR_PAD]) + dot_nn(mixed1, wproj[PAIR_PAD:])
     x1 = x1 + proj_bias
     x1o[...] = (x1 + down_bias) * valid
     xhat, inverse = row_norm(x1)
     normed = (xhat * gain + shift).astype(BF16)
-    dy = cot[...].astype(F32) * valid
-    dyb = dy.astype(BF16)
     dn = jnp.zeros((rows, width), F32)
-    chunk = 2 * width
+    kept = []
     for c in range(2):
         at = c * chunk
-        up = jnp.concatenate([parts[c][0][:, :width], parts[c][1][:, :width]], axis=1)
-        down = jnp.concatenate([parts[c][x][:, width + VEC :] for x in range(2)], axis=0)
-        pre = dot_nn(normed, up) + rowvec[4:5, at : at + chunk]
+        pre = dot_nn(normed, ups[c]) + rowvec[4:5, at : at + chunk]
         act, slope = gelu_pair(pre)
         actb = act.astype(BF16)
         acto[:, at : at + chunk] = actb
-        dpre = dot_nt(dyb, down) * slope
+        dpre = dacts[c] * slope
         dpreb = dpre.astype(BF16)
-        gd[:, at : at + chunk] += dot_tn(dyb, actb)
-        gu[:, at : at + chunk] += dot_tn(normed, dpreb)
         gsum[4:5, at : at + chunk] += jnp.sum(dpre, axis=0, keepdims=True)
-        dn = dn + dot_nt(dpreb, up)
+        dn = dn + dot_nt(dpreb, ups[c])
+        kept.append(dpreb)
+    for c in range(2):
+        at = c * chunk
+        gd[:, at : at + chunk] += dot_tn(dyb, acto[:, at : at + chunk])
+        gu[:, at : at + chunk] += dot_tn(normed, kept[c])
     dx = dy + row_norm_back(dn * gain, xhat, inverse)
     dx1[...] = dx
     dxb = dx.astype(BF16)
@@ -375,13 +386,13 @@
     return call(kernel, "mlp", rows // block, in_specs, out_specs, out_shape, scratch, args)
 
 
-def layer_out_kernel(meta, x1, act, w0, w1, out):
+def layer_out_kernel(meta, x1, act, b0, b1, out):
     rows, width = x1.shape
     row = lax.broadcasted_iota(jnp.int32, (rows, 1), 0) + pl.program_id(0) * rows
     valid = (row < rows_used(meta)).astype(F32)
     y = x1[...]
-    for c, ref in enumerate((w0, w1)):
-        down = jnp.concatenate([ref[x][:, width + VEC :] for x in range(2)], axis=0)
+    for c, ref in enumerate((b0, b1)):
+        down = jnp.concatenate([ref[x] for x in range(2)], axis=0)
         y = y + dot_nn(act[:, 2 * c * width : 2 * (c + 1) * width], down) * valid
     out[...] = y.astype(BF16)
 
@@ -424,29 +435,35 @@
             keep = lax.broadcasted_iota(jnp.int32, (padded, 1), 0) < length
             da = jnp.where(keep, da, 0.0)
         da = da.astype(BF16)
-        for h in range(PAIR):
-            at = h * HEAD_PAD
-            q = qkv[0, :padded, at : at + HEAD_PAD]
-            k = qkv[0, :padded, PAIR_PAD + at : PAIR_PAD + at + HEAD_PAD]
-            v = qkv[0, :padded, 2 * PAIR_PAD + at : 2 * PAIR_PAD + at + HEAD_PAD]
-            dah = da[:, at : at + HEAD_PAD]
-            s = dot_nt(k, q)
-            p = jnp.exp2(s * EXP_SCALE - lse[0, h : h + 1, :padded])
+        def cut(ref, part, h):
+            at = part * PAIR_PAD + h * HEAD_PAD
+            return ref[0, :padded, at : at + HEAD_PAD]
+
+        heads = range(PAIR)
+        das = [da[:, h * HEAD_PAD : (h + 1) * HEAD_PAD] for h in heads]
+        scores = [dot_nt(cut(qkv, 1, h), cut(qkv, 0, h)) for h in heads]
+        dps = [dot_nt(cut(qkv, 2, h), das[h]) for h in heads]
+        ps, dss = [], []
+        for h in heads:
+            p = jnp.exp2(scores[h] * EXP_SCALE - lse[0, h : h + 1, :padded])
             if length < padded:
-                key = lax.broadcasted_iota(jnp.int32, s.shape, 0)
+                key = lax.broadcasted_iota(jnp.int32, p.shape, 0)
                 p = jnp.where(key < length, p, 0.0)
-            dp = dot_nt(v, dah)
-            mean = jnp.sum(p * dp, axis=0, keepdims=True)
-            ds = (p * (dp - mean)).astype(BF16)
-            dv = dot_nn(p.astype(BF16), dah)
-            dk = dot_nn(ds, q) * SCALE
-            dq = dot_tn(ds, k) * SCALE
-            gsum[0:1, at : at + HEAD_PAD] += jnp.sum(dq, axis=0, keepdims=True)
-            gsum[0:1, 2 * PAIR_PAD + at : 2 * PAIR_PAD + at + HEAD_PAD] += jnp.sum(dv, axis=0, keepdims=True)
-            dqkv[0, :padded, at : at + HEAD_PAD] = dq.astype(BF16)
-            dqkv[0, :padded, PAIR_PAD + at : PAIR_PAD + at + HEAD_PAD] = dk.astype(BF16)
-            dqkv[0, :padded, 2 * PAIR_PAD + at : 2 * PAIR_PAD + at + HEAD_PAD] = dv.astype(BF16)
-        d = dqkv[0, :padded, :]
+            mean = jnp.sum(p * dps[h], axis=0, keepdims=True)
+            dss.append((p * (dps[h] - mean)).astype(BF16))
+            ps.append(p.astype(BF16))
+        parts = [[dot_tn(dss[h], cut(qkv, 1, h)) * SCALE for h in heads]]
+        parts += [[dot_nn(dss[h], cut(qkv, 0, h)) * SCALE for h in heads]]
+        parts += [[dot_nn(ps[h], das[h]) for h in heads]]
+        d = []
+        for part in range(3):
+            value = jnp.concatenate(parts[part], axis=1)
+            at = part * PAIR_PAD
+            if part != 1:
+                gsum[0:1, at : at + PAIR_PAD] += jnp.sum(value, axis=0, keepdims=True)
+            d.append(value.astype(BF16))
+        d = jnp.concatenate(d, axis=1)
+        dqkv[0, :padded, :] = d
         gw[...] += dot_tn(xhat[0, :padded, :], d)
         gsum[1:2, :] += jnp.sum(d.astype(F32), axis=0, keepdims=True)
 
@@ -536,6 +553,58 @@
     )
 
 
+def final_parts(core, own, got, shards):
+    size = own.shape[0]
+    width = shards * size
+    cut = 3 * PAIR_DIM + VEC_PAIR
+    low, high = (got, own) if core else (own, got)
+    qkv = [t[:, part * PAIR_DIM : (part + 1) * PAIR_DIM] for part in range(3) for t in (low, high)]
+    step = (low.shape[1] - cut) // 2
+    quarters = [t[:, cut + x * step : cut + (x + 1) * step] for t in (low, high) for x in range(2)]
+    extra_at, down_at = width, width + VEC
+    extra = [q[:, extra_at:down_at] for q in quarters]
+    up = [q[:, n * size : (n + 1) * size] for n in range(shards) for q in quarters]
+    down = jnp.concatenate([q[:, down_at:] for q in quarters], axis=0)
+    ends = low[:, 3 * PAIR_DIM : cut] + high[:, 3 * PAIR_DIM : cut]
+    columns = jnp.concatenate([ends[:, :4], extra[-1][:, : 4 + QUARTERS]], axis=1)
+    cat = lambda parts: jnp.concatenate(parts, axis=1)
+    return cat(qkv), cat(extra[: width // VEC]), cat(up), down, columns
+
+
+def finish_kernel(meta, own, got, *outs, shards):
+    size = own.shape[0]
+
+    def use(core):
+        *mats, columns = final_parts(core, own[...].astype(F32), got[...].astype(F32), shards)
+        for mat, out in zip(mats, outs):
+            tiles = mat.shape[1] // 128
+            for t in range(tiles):
+                out[pl.ds(t, mat.shape[0], stride=tiles), :] = mat[:, t * 128 : (t + 1) * 128]
+        count = columns.shape[1]
+        square = jnp.concatenate([columns, jnp.zeros((size, 128 - count), F32)], axis=1)
+        square = jnp.concatenate([square, jnp.zeros((128 - size, 128), F32)], axis=0)
+        outs[4][...] = square.T[:16]
+
+    for c in range(2):
+        pl.when(core_of(meta) == c)(partial(use, c))
+
+
+def finish(meta, own, got, shards):
+    size = own.shape[0]
+    width = shards * size
+    if size % 16:
+        core = core_of(meta) == 1
+        own, got = own.astype(F32), got.astype(F32)
+        parts = final_parts(0, jnp.where(core, got, own), jnp.where(core, own, got), shards)
+        return [p.reshape(-1) for p in parts[:4]], parts[4].T
+    sizes = [size * 3 * width, size * width, size * QUARTERS * width, size * QUARTERS * width]
+    out_shape = [jax.ShapeDtypeStruct((n // 128, 128), F32) for n in sizes + [16 * 128]]
+    out_specs = [whole(t) for t in out_shape]
+    kernel = partial(finish_kernel, shards=shards)
+    outs = call(kernel, "finish", 1, [whole(own), whole(got)], out_specs, out_shape, [], (meta, own, got))
+    return [t.reshape(-1) for t in outs[:4]], outs[4]
+
+
 def turned(shards):
     count = shards.bit_length() - 1
     return [sum(((n >> b) & 1) << (count - 1 - b) for b in range(count)) for n in range(shards)]
@@ -574,7 +643,7 @@
 
 
 def join(upper, own, other, dim):
-    return jnp.where(upper, jnp.stack([other, own], axis=dim), jnp.stack([own, other], axis=dim))
+    return jnp.stack([jnp.where(upper, other, own), jnp.where(upper, own, other)], axis=dim)
 
 
 def added(keep, got):
@@ -631,51 +700,49 @@
     sides = sides_of({"dp": (1, 2), "fsdp": bits})
     core, column = sides["dp", 1][0], sides["dp", 2][0]
 
-    vectors = jnp.stack([ln1_gain, ln1_bias, q_bias, v_bias]).T
+    vectors = [ln1_gain, ln1_bias, q_bias, v_bias, proj_bias, ln2_gain, ln2_bias, down_bias]
+    vectors = jnp.concatenate([jnp.stack(vectors), up_bias.reshape(QUARTERS, size)]).T
     pair = w_qkv.reshape(size, 3, 2, PAIR_DIM)
     pair = lax.dynamic_index_in_dim(pair, core, 2, keepdims=False).reshape(size, 3 * PAIR_DIM)
-    pair = jnp.concatenate([pair, vectors, jnp.zeros((size, VEC_PAIR - 4), BF16)], axis=1)
+    pair = jnp.concatenate([pair, vectors[:, :4], jnp.zeros((size, VEC_PAIR - 4), BF16)], axis=1)
+    f = Gather(sides, pair, tail_keys)
+    w_up, w_down, w_proj, _ = lax.optimization_barrier((w_up, w_down, w_proj, pair))
     quarter = 2 * core + column
-    vectors = jnp.stack([proj_bias, ln2_gain, ln2_bias, down_bias]).T
-    extra = jnp.concatenate(
-        [
-            w_proj.reshape(size, width),
-            vectors,
-            up_bias.reshape(QUARTERS, size).T,
-            jnp.zeros((size, VEC - 4 - QUARTERS), BF16),
-        ],
-        axis=1,
-    )
+    extra = [w_proj.reshape(size, width), vectors[:, 4:], jnp.zeros((size, VEC - 4 - QUARTERS), BF16)]
+    extra = lax.dynamic_slice_in_dim(jnp.concatenate(extra, axis=1), quarter * VEC, VEC, 1)
     up = lax.dynamic_index_in_dim(w_up.reshape(size, shards, QUARTERS, size), quarter, 2, False)
-    part_a = jnp.concatenate(
-        [up.reshape(size, width), lax.dynamic_slice_in_dim(extra, quarter * VEC, VEC, 1)], axis=1
-    )
+    part_a = jnp.concatenate([up.reshape(size, width), extra], axis=1)
     part_b = lax.dynamic_index_in_dim(w_down.reshape(QUARTERS, size, width), quarter, 0, False)
-
-    f = Gather(sides, pair, tail_keys)
-    ab = Gather(sides, jnp.concatenate([part_a, part_b], axis=1), [("dp", 2)] + tail_keys)
+    ab = Gather(sides, jnp.concatenate([part_a, part_b], axis=1), tail_keys)
+
+    for bit in far:
+        f.grow("fsdp", bit)
     for bit in far:
         ab.grow("fsdp", bit)
     for bit in near:
         f.grow("fsdp", bit)
-    ab.grow("dp", 2, f.part)
-    for bit in far:
-        f.grow("fsdp", bit)
     for bit in near:
-        ab.grow("fsdp", bit, f.part)
+        ab.grow("fsdp", bit)
     f.grow("fsdp", y)
     own = f.part.reshape(width, -1)
-    ab.part = after(ab.part, own)
+    cut = width + VEC
+    keys = [("dp", 2)] + tail_keys
+    a, b = Gather(sides, ab.part[..., :cut], keys), Gather(sides, ab.part[..., cut:], keys)
+    a.have, b.have = list(ab.have), list(ab.have)
+    a.grow("dp", 2)
+    b.grow("fsdp", y)
     wf = (own, swap(own, "dp", 1))
 
-    upper = jnp.broadcast_to(sides["fsdp", y][2], (8, ab.part.shape[-1])).astype(jnp.int32)
+    upper = jnp.stack([sides["fsdp", y][2], sides["dp", 2][2]])
+    upper = jnp.broadcast_to(upper[:, None, None], (2, 8, cut)).astype(jnp.int32)
     table, sides, upper = lax.optimization_barrier((table, sides, upper))
     attn0, attn1, qkv0, qkv1, xhat, lse0, lse1, wpad0, wpad1, upper = attn_fwd(
-        table, tokens, wf, (ab.part,), (upper,)
-    )
-    ab.grow("fsdp", y, upper=upper[0] != 0)
-    w = ab.part.reshape(2, width, -1)
-    w = (w, swap(w, "dp", 1))
+        table, tokens, wf, (a.part, b.part), (upper,)
+    )
+    a.grow("fsdp", y, upper=upper[0, 0] != 0)
+    b.grow("dp", 2, upper=upper[1, 0, :width] != 0)
+    wa, wb = a.part.reshape(2, width, cut), b.part.reshape(2, width, width)
+    w = (wa, swap(wa, "dp", 1), wb, swap(wb, "dp", 1))
     x1, act, dx1, dattn0, dattn1, keep_a, send_a, keep_b, send_b = mlp(
         table, tokens, cotangent, (attn0, attn1), w, shards
     )
@@ -704,52 +771,32 @@
     d0, keep_g, keep_a, keep_b = attn_bwd(
         table, qkv0, xhat, lse0, dattn0, wpad0, wf[0], True, shards, (send_a, send_b, send_g), (keep_a, keep_b)
     )
-    keep_g, send_g = pick(sides, by_bits(added(keep_g, got_g), 0), "fsdp", y, 0)
-    keep_a, send_a = pick(sides, added(keep_a, got_a), "fsdp", y, 0)
+    part = jnp.concatenate([by_bits(added(keep_g, got_g), 0), added(keep_a, got_a)], axis=-1)
+    keep, send = pick(sides, part, "fsdp", y, 0)
     keep_b, send_b = pick(sides, added(keep_b, got_b), "dp", 2, 0)
-    got_g = swap(send_g, "fsdp", y)
-    got_a, got_b = swap(send_a, "fsdp", y), swap(send_b, "dp", 2)
-    layer_out, keep_g, keep_a, keep_b = layer_output(
-        table, x1, act, w, (send_g, send_a, send_b), (keep_g, keep_a, keep_b)
-    )
-    part_g = added(keep_g, got_g)
-    part = jnp.concatenate([added(keep_a, got_a), added(keep_b, got_b)], axis=-1)
+    got, got_b = swap(send, "fsdp", y), swap(send_b, "dp", 2)
+    layer_out, keep, keep_b = layer_output(table, x1, act, w[2:], (send, send_b), (keep, keep_b))
+    part = jnp.concatenate([added(keep, got), added(keep_b, got_b)], axis=-1)
     for count, bit in enumerate(bits[1:]):
-        keep_g, send_g = pick(sides, part_g, "fsdp", bit, 0)
         keep, send = pick(sides, part, "fsdp", bit, 0)
-        got_g, got = swap(send_g, "fsdp", bit), swap(send, "fsdp", bit)
+        got = swap(send, "fsdp", bit)
         if count == 0:
-            grad_input, keep_g, keep = input_grad(
-                table, tokens, (d0, d1), (wpad0, wpad1), wf[0], dx1, (send_g, send), (keep_g, keep)
+            grad_input, keep = input_grad(
+                table, tokens, (d0, d1), (wpad0, wpad1), wf[0], dx1, (send,), (keep,)
             )
-        part_g, part = added(keep_g, got_g), added(keep, got)
-    part_g = added(part_g, swap(part_g, "dp", 2))
-    part = join(sides["dp", 2][2], part, swap(part, "dp", 2), 0)
-    part_g = join(sides["dp", 1][2], part_g, swap(part_g, "dp", 1), 0).astype(F32)
-    part = join(sides["dp", 1][2], part, swap(part, "dp", 1), 0).astype(F32)
-
-    grad_qkv = part_g[:, :, : 3 * PAIR_DIM].reshape(2, size, 3, PAIR_DIM).transpose(1, 2, 0, 3)
-    ends = (part_g[0, :, 3 * PAIR_DIM : 3 * PAIR_DIM + 4] + part_g[1, :, 3 * PAIR_DIM : 3 * PAIR_DIM + 4]).T
-    part = part.reshape(QUARTERS, size, -1)
-    grad_up = part[:, :, :width].reshape(QUARTERS, size, shards, size).transpose(1, 2, 0, 3)
-    extra = part[:, :, width : width + VEC].transpose(1, 0, 2).reshape(size, QUARTERS * VEC)
-    more = extra[:, width : width + 4 + QUARTERS].T
+        part = added(keep, got)
+    got = swap(part, "dp", 2)
+    cut = keep_g.shape[-1]
+    part_g = added(part[:, :cut], got[:, :cut])
+    low, high = part[:, cut:], got[:, cut:]
+    upper = sides["dp", 2][2]
+    part = [part_g, jnp.where(upper, high, low), jnp.where(upper, low, high)]
+    part = jnp.concatenate(part, axis=1)
+    flat, vectors = finish(table, part, swap(part, "dp", 1), shards)
+    g = [vectors[r, :size] for r in range(8)] + [vectors[8 : 8 + QUARTERS, :size].reshape(-1)]
+    qkv, proj, up, down = flat
     return (
-        layer_out,
-        grad_input,
-        ends[0],
-        ends[1],
-        grad_qkv.reshape(-1),
-        ends[2],
-        ends[3],
-        extra[:, :width].reshape(-1),
-        more[0],
-        more[1],
-        more[2],
-        grad_up.reshape(-1),
-        more[4:].reshape(-1),
-        part[:, :, width + VEC :].reshape(-1),
-        more[3],
+        layer_out, grad_input, g[0], g[1], qkv, g[2], g[3], proj, g[4], g[5], g[6], up, g[8], down, g[7]
     )
 
 

time: 167 us -> 141 us (0.84)
  Pallas kernels: 86.2 us -> 76 us
  waiting for transfers between devices: 36.6 us -> 29 us
  local copies, waits for them, and re-layouts: 14.3 us -> 8.87 us
  other arithmetic: 6.16 us -> 3.66 us
    pallas_call x6 -> x7, Pallas kernels: 86.2 us -> 76 us  [call(): pl.pallas_call(ordered, grid_spec=pltpu.PrefetchScalarGridSpec(num_scalar...]
    ppermute x25 -> x23, waiting for transfers between devices: 36.6 us -> 29 us  [swap(): return lax.ppermute(value, axis, [(i, i ^ bit) for i in range(size)])]
    reshape x8 -> x2, local copies, waits for them, and re-layouts: 4.9 us -> 0.77 us  [the longest x1 0.65 us: body(): vectors[8:8 + QUARTERS, :size].reshape(-1)]
    another operation x9 -> x21, other arithmetic: 2.87 us -> 1.15 us  [the longest x18 0.8 us: join(): jnp.stack([jnp.where(upper, other, own), jnp.where(upper, own, other)], a...]
    ppermute x25 -> x23, starting transfers between devices: 22.7 us -> 21.9 us  [swap(): return lax.ppermute(value, axis, [(i, i ^ bit) for i in range(size)])]
  transfers between devices with their start and end apart: 25 -> 23, of which waited for: 11 -> 11; matrix products, arithmetic and copies ran while one was open for 4% -> 5% of each run, Pallas kernels for 35% -> 34%
where the time goes in v3:
time: 141 us
  Pallas kernels  76 us (54%)
  waiting for transfers between devices  29 us (21%)
  starting transfers between devices  21.9 us (16%)
  local copies, waits for them, and re-layouts  8.87 us (6%)
  other arithmetic  3.66 us (3%)
    pallas_call x7, Pallas kernels, call(): pl.pallas_call(ordered, grid_spec=pltpu.PrefetchScalarGridSpec(num_scalar...  76 us
    ppermute x23, waiting for transfers between devices, swap(): return lax.ppermute(value, axis, [(i, i ^ bit) for i in range(size)])  29 us
    ppermute x23, starting transfers between devices, swap(): return lax.ppermute(value, axis, [(i, i ^ bit) for i in range(size)])  21.9 us
  transfers between devices with their start and end apart: 23, of which 11 were waited for; matrix products, arithmetic and copies ran while one was open for 5% of the time, Pallas kernels for 34%

profile of v3, /device:TPU:0, one launch (start us, length us, event | category | flops | bytes accessed | tf_op | source)
XLA Modules:
  0.0 140.6 jit_solution(17051688039665323681)
XLA Ops:
  4.2 4.0 %collective-permute-start = (bf16[48,640]{1,0:T(8,128)(2,1)S(1)}, bf16[48,640]{1,0:T(8,128)(2,1)S(1)}, u32[]{:S(2)}, u32[]{:S(2)}) collective-permute-start(bf16[48,640]{1,0:T(8,128)(2,1)S(1)} %maximum_maximum_fusion), channel_id=1, source_target_pairs={{0,16},{4,20},{8,24},{12,28},{16,0},{20,4},{24,8},{28,12},{1,17},{... | collective-permute-start | bytes 184328 | tf_op jit(solution)/shard_map/ppermute | solution.py:626
  14.0 1.9 %collective-permute-start.1 = (bf16[2,48,640]{2,1,0:T(8,128)(2,1)S(1)}, bf16[2,48,640]{2,1,0:T(8,128)(2,1)S(1)}, u32[]{:S(2)}, u32[]{:S(2)}) collective-permute-start(bf16[2,48,640]{2,1,0:T(8,128)(2,1)S(1)} %pad_maximum_fusion.9), channel_id=1, source_target_pairs={{0,8},{4,12},{8,0},{12,4},{16,24},{20,28},{24,16},{28,20},{1,9},{5... | collective-permute-start | bytes 368648 | tf_op jit(solution)/shard_map/ppermute | solution.py:626
  15.9 2.5 %collective-permute-done.4 = bf16[48,896]{1,0:T(8,128)(2,1)S(1)} collective-permute-done((bf16[48,896]{1,0:T(8,128)(2,1)S(1)}, bf16[48,896]{1,0:T(8,128)(2,1)S(1)}, u32[]{:S(2)}, u32[]{:S(2)}) %collective-permute-start.4) | collective-permute-done | bytes 86048 | tf_op jit(solution)/shard_map/ppermute | solution.py:626
  18.6 2.2 %collective-permute-done.1 = bf16[2,48,640]{2,1,0:T(8,128)(2,1)S(1)} collective-permute-done((bf16[2,48,640]{2,1,0:T(8,128)(2,1)S(1)}, bf16[2,48,640]{2,1,0:T(8,128)(2,1)S(1)}, u32[]{:S(2)}, u32[]{:S(2)}) %collective-permute-start.1) | collective-permute-done | bytes 122912 | tf_op jit(solution)/shard_map/ppermute | solution.py:626
  20.8 1.9 %collective-permute-start.2 = (bf16[2,2,48,640]{3,2,0,1:T(8,128)(2,1)S(1)}, bf16[2,2,48,640]{3,2,0,1:T(8,128)(2,1)S(1)}, u32[]{:S(2)}, u32[]{:S(2)}) collective-permute-start(bf16[2,2,48,640]{3,2,0,1:T(8,128)(2,1)S(1)} %pad_maximum_fusion.5), channel_id=1, source_target_pairs={{0,4},{4,0},{8,12},{12,8},{16,20},{20,16},{24,28},{28,24},{1,5},{5... | collective-permute-start | bytes 737288 | tf_op jit(solution)/shard_map/ppermute | solution.py:626
  22.7 1.3 collective-permute-done.5
  24.1 1.6 %collective-permute-start.7 = (bf16[2,2,48,384]{3,2,1,0:T(8,128)(2,1)S(1)}, bf16[2,2,48,384]{3,2,1,0:T(8,128)(2,1)S(1)}, u32[]{:S(2)}, u32[]{:S(2)}) collective-permute-start(bf16[2,2,48,384]{3,2,1,0:T(8,128)(2,1)S(1)} %pad_maximum_fusion.8), channel_id=1, source_target_pairs={{0,4},{4,0},{8,12},{12,8},{16,20},{20,16},{24,28},{28,24},{1,5},{5... | collective-permute-start | bytes 442376 | tf_op jit(solution)/shard_map/ppermute | solution.py:626
  25.7 1.6 %collective-permute-start.6 = (bf16[2,2,48,512]{3,2,1,0:T(8,128)(2,1)S(1)}, bf16[2,2,48,512]{3,2,1,0:T(8,128)(2,1)S(1)}, u32[]{:S(2)}, u32[]{:S(2)}) collective-permute-start(bf16[2,2,48,512]{3,2,1,0:T(8,128)(2,1)S(1)} %fusion.9), channel_id=1, source_target_pairs={{0,2},{1,3},{2,0},{3,1},{4,6},{5,7},{6,4},{7,5},{8,10},{9,11},{10,... | collective-permute-start | bytes 589832 | tf_op jit(solution)/shard_map/ppermute | solution.py:626
  28.7 2.7 %collective-permute-done.6 = bf16[2,2,48,512]{3,2,1,0:T(8,128)(2,1)S(1)} collective-permute-done((bf16[2,2,48,512]{3,2,1,0:T(8,128)(2,1)S(1)}, bf16[2,2,48,512]{3,2,1,0:T(8,128)(2,1)S(1)}, u32[]{:S(2)}, u32[]{:S(2)}) %collective-permute-start.6) | collective-permute-done | bytes 196640 | tf_op jit(solution)/shard_map/ppermute | solution.py:626
  32.2 1.6 %collective-permute-start.10 = (bf16[2,2,2,48,384]{4,3,2,1,0:T(8,128)(2,1)S(1)}, bf16[2,2,2,48,384]{4,3,2,1,0:T(8,128)(2,1)S(1)}, u32[]{:S(2)}, u32[]{:S(2)}) collective-permute-start(bf16[2,2,2,48,384]{4,3,2,1,0:T(8,128)(2,1)S(1)} %pad_maximum_fusion.4.refs_5_), channel_id=1, source_target_pairs={{0,2},{1,3},{2,0},{3,1},{4,6},{5,7},{6,4},{7,5},{8,10},{9,11},{10,... | collective-permute-start | bytes 884744 | tf_op jit(solution)/shard_map/ppermute | solution.py:626
  33.7 12.3 %attn_fwd.1 = (bf16[2048,256]{1,0:T(8,128)(2,1)S(1)}, bf16[2048,256]{1,0:T(8,128)(2,1)S(1)}, bf16[8,400,768]{2,1,0:T(8,128)(2,1)S(1)}, bf16[8,400,768]{2,1,0:T(8...) custom-call(s32[18]{0:T(128)S(1)} %pad_add_fusion.refs_0_, ...), custom_call_target="tpu_custom_call", output_to_operand_aliasing={{9}: (6, {})} | custom-call | tf_op jit(solution)/shard_map/attn_fwd/pallas_call | solution.py:117
  47.1 2.4 %collective-permute-done.11.refs_8_.refs_4_ = bf16[2,384,384]{2,1,0:T(8,128)(2,1)S(1)} collective-permute-done((bf16[2,384,384]{2,1,0:T(8,128)(2,1)S(1)}, bf16[2,384,384]{2,1,0:T(8,128)(2,1)S(1)}, u32[]{:S(2)}, u32[]{:S(2)}) %collective-permute-start.11) | collective-permute-done | bytes 589856 | tf_op jit(solution)/shard_map/ppermute | solution.py:626
  49.5 26.7 %mlp.1 = (f32[2048,384]{1,0:T(8,128)}, bf16[2048,1536]{1,0:T(8,128)(2,1)}, f32[2048,384]{1,0:T(8,128)}, bf16[2048,256]{1,0:T(8,128)(2,1)S(1)}, bf16[2048,256]{1,...) custom-call(s32[18]{0:T(128)S(1)} %pad_add_fusion.refs_0_, ...), custom_call_target="tpu_custom_call" | custom-call | tf_op jit(solution)/shard_map/mlp/pallas_call | solution.py:117
  76.7 9.4 %attn_bwd.2 = (bf16[8,400,768]{2,1,0:T(8,128)(2,1)S(1)}, bf16[384,640]{1,0:T(8,128)(2,1)S(1)}, bf16[2,384,512]{2,1,0:T(8,128)(2,1)S(1)}, bf16[2,2,192,384]{3,2,1,0:T(8,128)(2,1)S(1)}) custom-call(s32[18]{0:T(128)S(1)} %pad_add_fusion.refs_0_, bf16[8,400,768]{2,1,0:T(8,128)(2,1)S(1)} %get-tuple-element.81.refs_1_, ...), custom_call_target="tpu_custom_call", output_to_operand_aliasing={{2}: (9, {}), {3}: (10, {})} | custom-call | tf_op jit(solution)/shard_map/attn_bwd/pallas_call | solution.py:117
  86.9 3.0 %collective-permute-start.16 = (bf16[2,2,2,48,384]{4,3,2,1,0:T(8,128)(2,1)S(1)}, bf16[2,2,2,48,384]{4,3,2,1,0:T(8,128)(2,1)S(1)}, u32[]{:S(2)}, u32[]{:S(2)}) collective-permute-start(bf16[2,2,2,48,384]{4,3,2,1,0:T(8,128)(2,1)S(1)} %get-tuple-element.130.refs_8_), channel_id=1, source_target_pairs={{0,4},{4,0},{8,12},{12,8},{16,20},{20,16},{24,28},{28,24},{1,5},{5... | collective-permute-start | bytes 884744 | tf_op jit(solution)/shard_map/ppermute | solution.py:626
  90.3 9.6 %attn_bwd.3 = (bf16[8,400,768]{2,1,0:T(8,128)(2,1)S(1)}, bf16[384,640]{1,0:T(8,128)(2,1)S(1)}, bf16[2,2,2,48,512]{4,3,2,1,0:T(8,128)(2,1)S(1)}, bf16[2,2,2,48,384]{4,3,2,1,0:T(8,128)(2,1)S(1)}) custom-call(s32[18]{0:T(128)S(1)} %pad_add_fusion.refs_0_, ...), custom_call_target="tpu_custom_call", output_to_operand_aliasing={{2}: (10, {}), {3}: (11, {})} | custom-call | tf_op jit(solution)/shard_map/attn_bwd/pallas_call | solution.py:117
  100.1 1.4 %collective-permute-done.15 = bf16[2,2,2,48,512]{4,3,2,1,0:T(8,128)(2,1)S(1)} collective-permute-done((bf16[2,2,2,48,512]{4,3,2,1,0:T(8,128)(2,1)S(1)}, bf16[2,2,2,48,512]{4,3,2,1,0:T(8,128)(2,1)S(1)}, u32[]{:S(2)}, u32[]{:S(2)}) %collective-permute-start.15) | collective-permute-done | bytes 393248 | tf_op jit(solution)/shard_map/ppermute | solution.py:626
  102.7 8.2 %layer_out.1 = (bf16[2048,384]{1,0:T(8,128)(2,1)}, bf16[2,2,48,1152]{3,2,1,0:T(8,128)(2,1)S(1)}, bf16[2,2,48,384]{3,2,1,0:T(8,128)(2,1)S(1)}) custom-call(s32[18]{0:T(128)S(1)} %pad_add_fusion.refs_0_, f32[2048,384]{1,0:T(8,128)} %get-tuple-element.74.refs_1_, ...), custom_call_target="tpu_custom_call", output_to_operand_aliasing={{1}: (7, {}), {2}: (8, {})} | custom-call | tf_op jit(solution)/shard_map/layer_out/pallas_call | solution.py:117
  111.0 2.3 %collective-permute-done.17 = bf16[2,2,48,1152]{3,2,1,0:T(8,128)(2,1)S(1)} collective-permute-done((bf16[2,2,48,1152]{3,2,1,0:T(8,128)(2,1)S(1)}, bf16[2,2,48,1152]{3,2,1,0:T(8,128)(2,1)S(1)}, u32[]{:S(2)}, u32[]{:S(2)}) %collective-permute-start.17) | collective-permute-done | bytes 442400 | tf_op jit(solution)/shard_map/ppermute | solution.py:626
  113.7 8.3 %input_grad.1 = (bf16[2048,384]{1,0:T(8,128)(2,1)}, bf16[2,48,1536]{2,1,0:T(8,128)(2,1)S(1)}) custom-call(s32[18]{0:T(128)S(1)} %pad_add_fusion.refs_0_, bf16[2048,384]{1,0:T(8,128)(2,1)S(1)} %copy-done, bf16[8,400,768]{2,1,0:T(8,128)(2,1)S(1)} %get-tuple-element.100.refs_2_, ...), custom_call_target="tpu_custom_call", output_to_operand_aliasing={{1}: (9, {})} | custom-call | tf_op jit(solution)/shard_map/input_grad/pallas_call | solution.py:117
  123.4 7.4 %collective-permute-done.20 = bf16[48,1536]{1,0:T(8,128)(2,1)S(1)} collective-permute-done((bf16[48,1536]{1,0:T(8,128)(2,1)S(1)}, bf16[48,1536]{1,0:T(8,128)(2,1)S(1)}, u32[]{:S(2)}, u32[]{:S(2)}) %collective-permute-start.20) | collective-permute-done | bytes 147488 | tf_op jit(solution)/shard_map/ppermute | solution.py:626
  132.1 4.0 %collective-permute-done.21 = bf16[48,1536]{1,0:T(8,128)(2,1)S(1)} collective-permute-done((bf16[48,1536]{1,0:T(8,128)(2,1)S(1)}, bf16[48,1536]{1,0:T(8,128)(2,1)S(1)}, u32[]{:S(2)}, u32[]{:S(2)}) %collective-permute-start.21) | collective-permute-done | bytes 147488 | tf_op jit(solution)/shard_map/ppermute | solution.py:626
  136.3 1.5 %collective-permute-done.22.refs_2_ = bf16[48,2432]{1,0:T(8,128)(2,1)S(1)} collective-permute-done((bf16[48,2432]{1,0:T(8,128)(2,1)S(1)}, bf16[48,2432]{1,0:T(8,128)(2,1)S(1)}, u32[]{:S(2)}, u32[]{:S(2)}) %collective-permute-start.22) | collective-permute-done | bytes 233504 | tf_op jit(solution)/shard_map/ppermute | solution.py:626
  137.7 1.7 %finish.1 = (f32[432,128]{1,0:T(8,128)}, f32[144,128]{1,0:T(8,128)}, f32[576,128]{1,0:T(8,128)}, f32[576,128]{1,0:T(8,128)}, f32[16,128]{1,0:T(8,128)S(1)}) custom-call(s32[18]{0:T(128)S(1)} %pad_add_fusion.refs_0_, bf16[48,2432]{1,0:T(8,128)(2,1)S(1)} %pad_maximum_fusion.6.refs_1_, bf16[48,2432]{1,0:T(8,128)(2,1)S(1)} %collective-permute-done.22.refs_2_), custom_call_target="tpu_custom_call" | custom-call | tf_op jit(solution)/shard_map/finish/pallas_call | solution.py:117
  (119 shorter events, 20.2 us)
Async XLA Ops:
  0.7 11.5 %copy-start.5 = (s32[256]{0:T(256)S(1)}, s32[256]{0:T(256)}, u32[]{:S(2)}) copy-start(s32[256]{0:T(256)} %param.19) | copy-start | bytes 3076
  4.2 9.7 %collective-permute-start = (bf16[48,640]{1,0:T(8,128)(2,1)S(1)}, bf16[48,640]{1,0:T(8,128)(2,1)S(1)}, u32[]{:S(2)}, u32[]{:S(2)}) collective-permute-start(bf16[48,640]{1,0:T(8,128)(2,1)S(1)} %maximum_maximum_fusion), channel_id=1, source_target_pairs={{0,16},{4,20},{8,24},{12,28},{16,0},{20,4},{24,8},{28,12},{1,17},{... | collective-permute-start | bytes 184328 | tf_op jit(solution)/shard_map/ppermute | solution.py:626
  11.4 7.0 %collective-permute-start.4 = (bf16[48,896]{1,0:T(8,128)(2,1)S(1)}, bf16[48,896]{1,0:T(8,128)(2,1)S(1)}, u32[]{:S(2)}, u32[]{:S(2)}) collective-permute-start(bf16[48,896]{1,0:T(8,128)(2,1)S(1)} %pad_maximum_fusion.10), channel_id=1, source_target_pairs={{0,16},{4,20},{8,24},{12,28},{16,0},{20,4},{24,8},{28,12},{1,17},{... | collective-permute-start | bytes 258056 | tf_op jit(solution)/shard_map/ppermute | solution.py:626
  14.0 6.7 %collective-permute-start.1 = (bf16[2,48,640]{2,1,0:T(8,128)(2,1)S(1)}, bf16[2,48,640]{2,1,0:T(8,128)(2,1)S(1)}, u32[]{:S(2)}, u32[]{:S(2)}) collective-permute-start(bf16[2,48,640]{2,1,0:T(8,128)(2,1)S(1)} %pad_maximum_fusion.9), channel_id=1, source_target_pairs={{0,8},{4,12},{8,0},{12,4},{16,24},{20,28},{24,16},{28,20},{1,9},{5... | collective-permute-start | bytes 368648 | tf_op jit(solution)/shard_map/ppermute | solution.py:626
  18.5 5.5 %collective-permute-start.5 = (bf16[2,48,896]{2,1,0:T(8,128)(2,1)S(1)}, bf16[2,48,896]{2,1,0:T(8,128)(2,1)S(1)}, u32[]{:S(2)}, u32[]{:S(2)}) collective-permute-start(bf16[2,48,896]{2,1,0:T(8,128)(2,1)S(1)} %pad_maximum_fusion.7), channel_id=1, source_target_pairs={{0,8},{4,12},{8,0},{12,4},{16,24},{20,28},{24,16},{28,20},{1,9},{5... | collective-permute-start | bytes 516104 | tf_op jit(solution)/shard_map/ppermute | solution.py:626
  20.8 7.6 %collective-permute-start.2 = (bf16[2,2,48,640]{3,2,0,1:T(8,128)(2,1)S(1)}, bf16[2,2,48,640]{3,2,0,1:T(8,128)(2,1)S(1)}, u32[]{:S(2)}, u32[]{:S(2)}) collective-permute-start(bf16[2,2,48,640]{3,2,0,1:T(8,128)(2,1)S(1)} %pad_maximum_fusion.5), channel_id=1, source_target_pairs={{0,4},{4,0},{8,12},{12,8},{16,20},{20,16},{24,28},{28,24},{1,5},{5... | collective-permute-start | bytes 737288 | tf_op jit(solution)/shard_map/ppermute | solution.py:626
  24.1 8.0 %collective-permute-start.7 = (bf16[2,2,48,384]{3,2,1,0:T(8,128)(2,1)S(1)}, bf16[2,2,48,384]{3,2,1,0:T(8,128)(2,1)S(1)}, u32[]{:S(2)}, u32[]{:S(2)}) collective-permute-start(bf16[2,2,48,384]{3,2,1,0:T(8,128)(2,1)S(1)} %pad_maximum_fusion.8), channel_id=1, source_target_pairs={{0,4},{4,0},{8,12},{12,8},{16,20},{20,16},{24,28},{28,24},{1,5},{5... | collective-permute-start | bytes 442376 | tf_op jit(solution)/shard_map/ppermute | solution.py:626
  25.7 5.7 %collective-permute-start.6 = (bf16[2,2,48,512]{3,2,1,0:T(8,128)(2,1)S(1)}, bf16[2,2,48,512]{3,2,1,0:T(8,128)(2,1)S(1)}, u32[]{:S(2)}, u32[]{:S(2)}) collective-permute-start(bf16[2,2,48,512]{3,2,1,0:T(8,128)(2,1)S(1)} %fusion.9), channel_id=1, source_target_pairs={{0,2},{1,3},{2,0},{3,1},{4,6},{5,7},{6,4},{7,5},{8,10},{9,11},{10,... | collective-permute-start | bytes 589832 | tf_op jit(solution)/shard_map/ppermute | solution.py:626
  28.7 5.1 %collective-permute-start.3 = (bf16[384,640]{1,0:T(8,128)(2,1)S(1)}, bf16[384,640]{1,0:T(8,128)(2,1)S(1)}, u32[]{:S(2)}, u32[]{:S(2)}) collective-permute-start(bf16[384,640]{1,0:T(8,128)(2,1)S(1)} %bitcast.107), channel_id=1, source_target_pairs={{0,1},{1,0},{2,3},{3,2},{4,5},{5,4},{6,7},{7,6},{8,9},{9,8},{10,11... | collective-permute-start | bytes 1474568 | tf_op jit(solution)/shard_map/ppermute | solution.py:626
  31.5 14.6 %collective-permute-start.8 = (bf16[2,2,2,48,512]{4,3,2,1,0:T(8,128)(2,1)S(1)}, bf16[2,2,2,48,512]{4,3,2,1,0:T(8,128)(2,1)S(1)}, u32[]{:S(2)}, u32[]{:S(2)}) collective-permute-start(bf16[2,2,2,48,512]{4,3,2,1,0:T(8,128)(2,1)S(1)} %pad_maximum_fusion.3.refs_4_), channel_id=1, source_target_pairs={{0,4},{4,0},{8,12},{12,8},{16,20},{20,16},{24,28},{28,24},{1,5},{5... | collective-permute-start | bytes 1179656 | tf_op jit(solution)/shard_map/ppermute | solution.py:626
  32.2 14.2 %collective-permute-start.10 = (bf16[2,2,2,48,384]{4,3,2,1,0:T(8,128)(2,1)S(1)}, bf16[2,2,2,48,384]{4,3,2,1,0:T(8,128)(2,1)S(1)}, u32[]{:S(2)}, u32[]{:S(2)}) collective-permute-start(bf16[2,2,2,48,384]{4,3,2,1,0:T(8,128)(2,1)S(1)} %pad_maximum_fusion.4.refs_5_), channel_id=1, source_target_pairs={{0,2},{1,3},{2,0},{3,1},{4,6},{5,7},{6,4},{7,5},{8,10},{9,11},{10,... | collective-permute-start | bytes 884744 | tf_op jit(solution)/shard_map/ppermute | solution.py:626
  46.3 3.2 %collective-permute-start.9 = (bf16[2,384,512]{2,1,0:T(8,128)(2,1)S(1)}, bf16[2,384,512]{2,1,0:T(8,128)(2,1)S(1)}, u32[]{:S(2)}, u32[]{:S(2)}) collective-permute-start(bf16[2,384,512]{2,1,0:T(8,128)(2,1)S(1)} %bitcast.111), channel_id=1, source_target_pairs={{0,1},{1,0},{2,3},{3,2},{4,5},{5,4},{6,7},{7,6},{8,9},{9,8},{10,11... | collective-permute-start | bytes 2359304 | tf_op jit(solution)/shard_map/ppermute | solution.py:626
  46.6 2.9 %collective-permute-start.11 = (bf16[2,384,384]{2,1,0:T(8,128)(2,1)S(1)}, bf16[2,384,384]{2,1,0:T(8,128)(2,1)S(1)}, u32[]{:S(2)}, u32[]{:S(2)}) collective-permute-start(bf16[2,384,384]{2,1,0:T(8,128)(2,1)S(1)} %pad_maximum_fusion.1.refs_7_.refs_3_), channel_id=1, source_target_pairs={{0,1},{1,0},{2,3},{3,2},{4,5},{5,4},{6,7},{7,6},{8,9},{9,8},{10,11... | collective-permute-start | bytes 1769480 | tf_op jit(solution)/shard_map/ppermute | solution.py:626
  76.2 10.5 %collective-permute-start.13 = (bf16[2,2,192,384]{3,2,1,0:T(8,128)(2,1)S(1)}, bf16[2,2,192,384]{3,2,1,0:T(8,128)(2,1)S(1)}, u32[]{:S(2)}, u32[]{:S(2)}) collective-permute-start(bf16[2,2,192,384]{3,2,1,0:T(8,128)(2,1)S(1)} %get-tuple-element.86.refs_8_), channel_id=1, source_target_pairs={{0,1},{1,0},{2,3},{3,2},{4,5},{5,4},{6,7},{7,6},{8,9},{9,8},{10,11... | collective-permute-start | bytes 1769480 | tf_op jit(solution)/shard_map/ppermute | solution.py:626
  76.3 13.6 %collective-permute-start.12 = (bf16[2,384,512]{2,1,0:T(8,128)(2,1)S(1)}, bf16[2,384,512]{2,1,0:T(8,128)(2,1)S(1)}, u32[]{:S(2)}, u32[]{:S(2)}) collective-permute-start(bf16[2,384,512]{2,1,0:T(8,128)(2,1)S(1)} %get-tuple-element.85.refs_7_), channel_id=1, source_target_pairs={{0,1},{1,0},{2,3},{3,2},{4,5},{5,4},{6,7},{7,6},{8,9},{9,8},{10,11... | collective-permute-start | bytes 2359304 | tf_op jit(solution)/shard_map/ppermute | solution.py:626
  86.0 13.8 %collective-permute-start.14 = (bf16[384,640]{1,0:T(8,128)(2,1)S(1)}, bf16[384,640]{1,0:T(8,128)(2,1)S(1)}, u32[]{:S(2)}, u32[]{:S(2)}) collective-permute-start(bf16[384,640]{1,0:T(8,128)(2,1)S(1)} %get-tuple-element.93.refs_9_), channel_id=1, source_target_pairs={{0,1},{1,0},{2,3},{3,2},{4,5},{5,4},{6,7},{7,6},{8,9},{9,8},{10,11... | collective-permute-start | bytes 1474568 | tf_op jit(solution)/shard_map/ppermute | solution.py:626
  86.9 13.1 %collective-permute-start.16 = (bf16[2,2,2,48,384]{4,3,2,1,0:T(8,128)(2,1)S(1)}, bf16[2,2,2,48,384]{4,3,2,1,0:T(8,128)(2,1)S(1)}, u32[]{:S(2)}, u32[]{:S(2)}) collective-permute-start(bf16[2,2,2,48,384]{4,3,2,1,0:T(8,128)(2,1)S(1)} %get-tuple-element.130.refs_8_), channel_id=1, source_target_pairs={{0,4},{4,0},{8,12},{12,8},{16,20},{20,16},{24,28},{28,24},{1,5},{5... | collective-permute-start | bytes 884744 | tf_op jit(solution)/shard_map/ppermute | solution.py:626
  90.2 11.3 %collective-permute-start.15 = (bf16[2,2,2,48,512]{4,3,2,1,0:T(8,128)(2,1)S(1)}, bf16[2,2,2,48,512]{4,3,2,1,0:T(8,128)(2,1)S(1)}, u32[]{:S(2)}, u32[]{:S(2)}) collective-permute-start(bf16[2,2,2,48,512]{4,3,2,1,0:T(8,128)(2,1)S(1)} %get-tuple-element.124.refs_7_), channel_id=1, source_target_pairs={{0,2},{1,3},{2,0},{3,1},{4,6},{5,7},{6,4},{7,5},{8,10},{9,11},{10,... | collective-permute-start | bytes 1179656 | tf_op jit(solution)/shard_map/ppermute | solution.py:626
  101.7 11.5 %collective-permute-start.17 = (bf16[2,2,48,1152]{3,2,1,0:T(8,128)(2,1)S(1)}, bf16[2,2,48,1152]{3,2,1,0:T(8,128)(2,1)S(1)}, u32[]{:S(2)}, u32[]{:S(2)}) collective-permute-start(bf16[2,2,48,1152]{3,2,1,0:T(8,128)(2,1)S(1)} %get-tuple-element.120.refs_5_), channel_id=1, source_target_pairs={{0,4},{4,0},{8,12},{12,8},{16,20},{20,16},{24,28},{28,24},{1,5},{5... | collective-permute-start | bytes 1327112 | tf_op jit(solution)/shard_map/ppermute | solution.py:626
  102.2 8.8 %collective-permute-start.18 = (bf16[2,2,48,384]{3,2,1,0:T(8,128)(2,1)S(1)}, bf16[2,2,48,384]{3,2,1,0:T(8,128)(2,1)S(1)}, u32[]{:S(2)}, u32[]{:S(2)}) collective-permute-start(bf16[2,2,48,384]{3,2,1,0:T(8,128)(2,1)S(1)} %get-tuple-element.140.refs_6_), channel_id=1, source_target_pairs={{0,2},{1,3},{2,0},{3,1},{4,6},{5,7},{6,4},{7,5},{8,10},{9,11},{10,... | collective-permute-start | bytes 442376 | tf_op jit(solution)/shard_map/ppermute | solution.py:626
  113.5 8.6 %collective-permute-start.19 = (bf16[2,48,1536]{2,1,0:T(8,128)(2,1)S(1)}, bf16[2,48,1536]{2,1,0:T(8,128)(2,1)S(1)}, u32[]{:S(2)}, u32[]{:S(2)}) collective-permute-start(bf16[2,48,1536]{2,1,0:T(8,128)(2,1)S(1)} %get-tuple-element.128.refs_8_), channel_id=1, source_target_pairs={{0,8},{4,12},{8,0},{12,4},{16,24},{20,28},{24,16},{28,20},{1,9},{5... | collective-permute-start | bytes 884744 | tf_op jit(solution)/shard_map/ppermute | solution.py:626
  122.2 8.7 %collective-permute-start.20 = (bf16[48,1536]{1,0:T(8,128)(2,1)S(1)}, bf16[48,1536]{1,0:T(8,128)(2,1)S(1)}, u32[]{:S(2)}, u32[]{:S(2)}) collective-permute-start(bf16[48,1536]{1,0:T(8,128)(2,1)S(1)} %dynamic-slice_bitcast_fusion.4), channel_id=1, source_target_pairs={{0,16},{4,20},{8,24},{12,28},{16,0},{20,4},{24,8},{28,12},{1,17},{... | collective-permute-start | bytes 442376 | tf_op jit(solution)/shard_map/ppermute | solution.py:626
  130.9 5.2 %collective-permute-start.21 = (bf16[48,1536]{1,0:T(8,128)(2,1)S(1)}, bf16[48,1536]{1,0:T(8,128)(2,1)S(1)}, u32[]{:S(2)}, u32[]{:S(2)}) collective-permute-start(bf16[48,1536]{1,0:T(8,128)(2,1)S(1)} %fusion.8), channel_id=1, source_target_pairs={{0,2},{1,3},{2,0},{3,1},{4,6},{5,7},{6,4},{7,5},{8,10},{9,11},{10,... | collective-permute-start | bytes 442376 | tf_op jit(solution)/shard_map/ppermute | solution.py:626
  136.2 1.6 %collective-permute-start.22 = (bf16[48,2432]{1,0:T(8,128)(2,1)S(1)}, bf16[48,2432]{1,0:T(8,128)(2,1)S(1)}, u32[]{:S(2)}, u32[]{:S(2)}) collective-permute-start(bf16[48,2432]{1,0:T(8,128)(2,1)S(1)} %pad_maximum_fusion.6.refs_1_), channel_id=1, source_target_pairs={{0,1},{1,0},{2,3},{3,2},{4,5},{5,4},{6,7},{7,6},{8,9},{9,8},{10,11... | collective-permute-start | bytes 700424 | tf_op jit(solution)/shard_map/ppermute | solution.py:626
  (5 other events, 40.8 us)

commit v4 on v3

--- a/solution.py
+++ b/solution.py
@@ -22,7 +22,7 @@
 SCALE = 1.0 / math.sqrt(HEAD_DIM)
 EXP_SCALE = SCALE * math.log2(math.e)
 MIB = 1024 * 1024
-VMEM = {"attn_fwd": 12, "mlp": 26, "attn_bwd": 8, "layer_out": 8, "input_grad": 10, "finish": 10}
+VMEM = {"attn_fwd": 12, "mlp": 24, "attn_bwd": 8, "layer_out": 8, "input_grad": 10, "finish": 10}
 F32 = jnp.float32
 BF16 = jnp.bfloat16
 
@@ -363,9 +363,9 @@
     hidden = QUARTERS * width
     by_row = lambda cols: pl.BlockSpec((block, cols), lambda i, m: (i, 0))
     out_shape = [
-        pltpu.HBM((rows, width), F32),
+        jax.ShapeDtypeStruct((rows, width), F32),
         pltpu.HBM((rows, hidden), BF16),
-        pltpu.HBM((rows, width), F32),
+        jax.ShapeDtypeStruct((rows, width), F32),
         jax.ShapeDtypeStruct((rows, PAIR_PAD), BF16),
         jax.ShapeDtypeStruct((rows, PAIR_PAD), BF16),
     ]
@@ -411,7 +411,6 @@
         (meta, x1, act, *w),
         waits,
         carry,
-        (1, 2),
     )
 
 
@@ -692,8 +691,6 @@
     size = width // shards
     devices = shards * lax.axis_size("dp")
     device = lax.axis_index("fsdp") * lax.axis_size("dp") + lax.axis_index("dp")
-    table = image_table(size_group, assignment, device, size_group.shape[0] // devices)
-
     bits = [1 << b for b in range(shards.bit_length() - 1)]
     far, near, y = bits[2:], bits[1:2], bits[0]
     tail_keys = [("fsdp", b) for b in reversed(bits)]
@@ -723,6 +720,8 @@
         f.grow("fsdp", bit)
     for bit in near:
         ab.grow("fsdp", bit)
+    size_group, assignment, _ = lax.optimization_barrier((size_group, assignment, f.part))
+    table = image_table(size_group, assignment, device, size_group.shape[0] // devices)
     f.grow("fsdp", y)
     own = f.part.reshape(width, -1)
     cut = width + VEC
@@ -775,15 +774,14 @@
     keep, send = pick(sides, part, "fsdp", y, 0)
     keep_b, send_b = pick(sides, added(keep_b, got_b), "dp", 2, 0)
     got, got_b = swap(send, "fsdp", y), swap(send_b, "dp", 2)
-    layer_out, keep, keep_b = layer_output(table, x1, act, w[2:], (send, send_b), (keep, keep_b))
+    grads_of = (table, tokens, (d0, d1), (wpad0, wpad1), wf[0], dx1)
+    grad_input, keep, keep_b = input_grad(*grads_of, (send, send_b), (keep, keep_b))
     part = jnp.concatenate([added(keep, got), added(keep_b, got_b)], axis=-1)
     for count, bit in enumerate(bits[1:]):
         keep, send = pick(sides, part, "fsdp", bit, 0)
         got = swap(send, "fsdp", bit)
         if count == 0:
-            grad_input, keep = input_grad(
-                table, tokens, (d0, d1), (wpad0, wpad1), wf[0], dx1, (send,), (keep,)
-            )
+            layer_out, keep = layer_output(table, x1, act, w[2:], (send,), (keep,))
         part = added(keep, got)
     got = swap(part, "dp", 2)
     cut = keep_g.shape[-1]

time: 141 us -> 140 us (level)
  starting transfers between devices: 21.9 us -> 25.9 us
  Pallas kernels: 76 us -> 72.7 us
  waiting for transfers between devices: 29 us -> 27.4 us
    ppermute x23, starting transfers between devices: 21.9 us -> 25.9 us  [swap(): return lax.ppermute(value, axis, [(i, i ^ bit) for i in range(size)])]
    pallas_call x7, Pallas kernels: 76 us -> 72.7 us  [call(): pl.pallas_call(ordered, grid_spec=pltpu.PrefetchScalarGridSpec(num_scalar...]
    ppermute x23, waiting for transfers between devices: 29 us -> 27.4 us  [swap(): return lax.ppermute(value, axis, [(i, i ^ bit) for i in range(size)])]
  transfers between devices with their start and end apart: 23 -> 23, of which waited for: 11 -> 9; matrix products, arithmetic and copies ran while one was open for 5% -> 5% of each run, Pallas kernels for 34% -> 32%
where the time goes in v4:
time: 140 us
  Pallas kernels  72.7 us (52%)
  waiting for transfers between devices  27.4 us (20%)
  starting transfers between devices  25.9 us (18%)
  local copies, waits for them, and re-layouts  8.85 us (6%)
  other arithmetic  3.68 us (3%)
    pallas_call x7, Pallas kernels, call(): pl.pallas_call(ordered, grid_spec=pltpu.PrefetchScalarGridSpec(num_scalar...  72.7 us
    ppermute x23, waiting for transfers between devices, swap(): return lax.ppermute(value, axis, [(i, i ^ bit) for i in range(size)])  27.4 us
    ppermute x23, starting transfers between devices, swap(): return lax.ppermute(value, axis, [(i, i ^ bit) for i in range(size)])  25.9 us
  transfers between devices with their start and end apart: 23, of which 9 were waited for; matrix products, arithmetic and copies ran while one was open for 5% of the time, Pallas kernels for 32%

profile of v4, /device:TPU:0, one launch (start us, length us, event | category | flops | bytes accessed | tf_op | source)
XLA Modules:
  0.0 139.7 jit_solution(12019960648209982955)
XLA Ops:
  4.2 4.0 %collective-permute-start = (bf16[48,640]{1,0:T(8,128)(2,1)S(1)}, bf16[48,640]{1,0:T(8,128)(2,1)S(1)}, u32[]{:S(2)}, u32[]{:S(2)}) collective-permute-start(bf16[48,640]{1,0:T(8,128)(2,1)S(1)} %maximum_maximum_fusion), channel_id=1, source_target_pairs={{0,16},{4,20},{8,24},{12,28},{16,0},{20,4},{24,8},{28,12},{1,17},{... | collective-permute-start | bytes 184328 | tf_op jit(solution)/shard_map/ppermute | solution.py:625
  11.7 1.9 %collective-permute-start.1 = (bf16[2,48,640]{2,1,0:T(8,128)(2,1)S(1)}, bf16[2,48,640]{2,1,0:T(8,128)(2,1)S(1)}, u32[]{:S(2)}, u32[]{:S(2)}) collective-permute-start(bf16[2,48,640]{2,1,0:T(8,128)(2,1)S(1)} %pad_maximum_fusion.9), channel_id=1, source_target_pairs={{0,8},{4,12},{8,0},{12,4},{16,24},{20,28},{24,16},{28,20},{1,9},{5... | collective-permute-start | bytes 368648 | tf_op jit(solution)/shard_map/ppermute | solution.py:625
  13.6 4.1 %collective-permute-done.4 = bf16[48,896]{1,0:T(8,128)(2,1)S(1)} collective-permute-done((bf16[48,896]{1,0:T(8,128)(2,1)S(1)}, bf16[48,896]{1,0:T(8,128)(2,1)S(1)}, u32[]{:S(2)}, u32[]{:S(2)}) %collective-permute-start.4) | collective-permute-done | bytes 86048 | tf_op jit(solution)/shard_map/ppermute | solution.py:625
  17.8 1.6 %collective-permute-start.5 = (bf16[2,48,896]{2,1,0:T(8,128)(2,1)S(1)}, bf16[2,48,896]{2,1,0:T(8,128)(2,1)S(1)}, u32[]{:S(2)}, u32[]{:S(2)}) collective-permute-start(bf16[2,48,896]{2,1,0:T(8,128)(2,1)S(1)} %pad_maximum_fusion.7), channel_id=1, source_target_pairs={{0,8},{4,12},{8,0},{12,4},{16,24},{20,28},{24,16},{28,20},{1,9},{5... | collective-permute-start | bytes 516104 | tf_op jit(solution)/shard_map/ppermute | solution.py:625
  19.5 1.6 %collective-permute-start.2 = (bf16[2,2,48,640]{3,2,0,1:T(8,128)(2,1)S(1)}, bf16[2,2,48,640]{3,2,0,1:T(8,128)(2,1)S(1)}, u32[]{:S(2)}, u32[]{:S(2)}) collective-permute-start(bf16[2,2,48,640]{3,2,0,1:T(8,128)(2,1)S(1)} %pad_maximum_fusion.5), channel_id=1, source_target_pairs={{0,4},{4,0},{8,12},{12,8},{16,20},{20,16},{24,28},{28,24},{1,5},{5... | collective-permute-start | bytes 737288 | tf_op jit(solution)/shard_map/ppermute | solution.py:625
  23.4 1.6 %collective-permute-start.7 = (bf16[2,2,48,384]{3,2,1,0:T(8,128)(2,1)S(1)}, bf16[2,2,48,384]{3,2,1,0:T(8,128)(2,1)S(1)}, u32[]{:S(2)}, u32[]{:S(2)}) collective-permute-start(bf16[2,2,48,384]{3,2,1,0:T(8,128)(2,1)S(1)} %pad_maximum_fusion.8), channel_id=1, source_target_pairs={{0,4},{4,0},{8,12},{12,8},{16,20},{20,16},{24,28},{28,24},{1,5},{5... | collective-permute-start | bytes 442376 | tf_op jit(solution)/shard_map/ppermute | solution.py:625
  25.0 1.6 %collective-permute-start.6 = (bf16[2,2,48,512]{3,2,1,0:T(8,128)(2,1)S(1)}, bf16[2,2,48,512]{3,2,1,0:T(8,128)(2,1)S(1)}, u32[]{:S(2)}, u32[]{:S(2)}) collective-permute-start(bf16[2,2,48,512]{3,2,1,0:T(8,128)(2,1)S(1)} %fusion.9), channel_id=1, source_target_pairs={{0,2},{1,3},{2,0},{3,1},{4,6},{5,7},{6,4},{7,5},{8,10},{9,11},{10,... | collective-permute-start | bytes 589832 | tf_op jit(solution)/shard_map/ppermute | solution.py:625
  27.6 3.1 %collective-permute-done.6 = bf16[2,2,48,512]{3,2,1,0:T(8,128)(2,1)S(1)} collective-permute-done((bf16[2,2,48,512]{3,2,1,0:T(8,128)(2,1)S(1)}, bf16[2,2,48,512]{3,2,1,0:T(8,128)(2,1)S(1)}, u32[]{:S(2)}, u32[]{:S(2)}) %collective-permute-start.6) | collective-permute-done | bytes 196640 | tf_op jit(solution)/shard_map/ppermute | solution.py:625
  31.5 1.6 %collective-permute-start.10 = (bf16[2,2,2,48,384]{4,3,2,1,0:T(8,128)(2,1)S(1)}, bf16[2,2,2,48,384]{4,3,2,1,0:T(8,128)(2,1)S(1)}, u32[]{:S(2)}, u32[]{:S(2)}) collective-permute-start(bf16[2,2,2,48,384]{4,3,2,1,0:T(8,128)(2,1)S(1)} %pad_maximum_fusion.4.refs_5_), channel_id=1, source_target_pairs={{0,2},{1,3},{2,0},{3,1},{4,6},{5,7},{6,4},{7,5},{8,10},{9,11},{10,... | collective-permute-start | bytes 884744 | tf_op jit(solution)/shard_map/ppermute | solution.py:625
  33.1 12.3 %attn_fwd.1 = (bf16[2048,256]{1,0:T(8,128)(2,1)S(1)}, bf16[2048,256]{1,0:T(8,128)(2,1)S(1)}, bf16[8,400,768]{2,1,0:T(8,128)(2,1)S(1)}, bf16[8,400,768]{2,1,0:T(8...) custom-call(s32[18]{0:T(128)S(1)} %pad_add_fusion.refs_0_, ...), custom_call_target="tpu_custom_call", output_to_operand_aliasing={{9}: (6, {})} | custom-call | tf_op jit(solution)/shard_map/attn_fwd/pallas_call | solution.py:117
  46.5 2.4 %collective-permute-done.11.refs_8_.refs_4_ = bf16[2,384,384]{2,1,0:T(8,128)(2,1)S(1)} collective-permute-done((bf16[2,384,384]{2,1,0:T(8,128)(2,1)S(1)}, bf16[2,384,384]{2,1,0:T(8,128)(2,1)S(1)}, u32[]{:S(2)}, u32[]{:S(2)}) %collective-permute-start.11) | collective-permute-done | bytes 589856 | tf_op jit(solution)/shard_map/ppermute | solution.py:625
  48.8 26.1 %mlp.1 = (f32[2048,384]{1,0:T(8,128)S(1)}, bf16[2048,1536]{1,0:T(8,128)(2,1)}, f32[2048,384]{1,0:T(8,128)S(1)}, bf16[2048,256]{1,0:T(8,128)(2,1)S(1)}, bf16[2048...) custom-call(s32[18]{0:T(128)S(1)} %pad_add_fusion.refs_0_, ...), custom_call_target="tpu_custom_call" | custom-call | tf_op jit(solution)/shard_map/mlp/pallas_call | solution.py:117
  75.4 9.4 %attn_bwd.2 = (bf16[8,400,768]{2,1,0:T(8,128)(2,1)S(1)}, bf16[384,640]{1,0:T(8,128)(2,1)S(1)}, bf16[2,384,512]{2,1,0:T(8,128)(2,1)S(1)}, bf16[2,2,192,384]{3,2,1,0:T(8,128)(2,1)S(1)}) custom-call(s32[18]{0:T(128)S(1)} %pad_add_fusion.refs_0_, bf16[8,400,768]{2,1,0:T(8,128)(2,1)S(1)} %get-tuple-element.85.refs_1_, ...), custom_call_target="tpu_custom_call", output_to_operand_aliasing={{2}: (9, {}), {3}: (10, {})} | custom-call | tf_op jit(solution)/shard_map/attn_bwd/pallas_call | solution.py:117
  86.7 1.7 %collective-permute-start.15 = (bf16[2,2,2,48,512]{4,3,2,1,0:T(8,128)(2,1)S(1)}, bf16[2,2,2,48,512]{4,3,2,1,0:T(8,128)(2,1)S(1)}, u32[]{:S(2)}, u32[]{:S(2)}) collective-permute-start(bf16[2,2,2,48,512]{4,3,2,1,0:T(8,128)(2,1)S(1)} %get-tuple-element.128.refs_7_), channel_id=1, source_target_pairs={{0,2},{1,3},{2,0},{3,1},{4,6},{5,7},{6,4},{7,5},{8,10},{9,11},{10,... | collective-permute-start | bytes 1179656 | tf_op jit(solution)/shard_map/ppermute | solution.py:625
  88.4 9.6 %attn_bwd.3 = (bf16[8,400,768]{2,1,0:T(8,128)(2,1)S(1)}, bf16[384,640]{1,0:T(8,128)(2,1)S(1)}, bf16[2,2,2,48,512]{4,3,2,1,0:T(8,128)(2,1)S(1)}, bf16[2,2,2,48,384]{4,3,2,1,0:T(8,128)(2,1)S(1)}) custom-call(s32[18]{0:T(128)S(1)} %pad_add_fusion.refs_0_, ...), custom_call_target="tpu_custom_call", output_to_operand_aliasing={{2}: (10, {}), {3}: (11, {})} | custom-call | tf_op jit(solution)/shard_map/attn_bwd/pallas_call | solution.py:117
  100.2 8.4 %input_grad.1 = (bf16[2048,384]{1,0:T(8,128)(2,1)}, bf16[2,2,48,1152]{3,2,1,0:T(8,128)(2,1)S(1)}, bf16[2,2,48,384]{3,2,1,0:T(8,128)(2,1)S(1)}) custom-call(s32[18]{0:T(128)S(1)} %pad_add_fusion.refs_0_, bf16[2048,384]{1,0:T(8,128)(2,1)S(1)} %copy-done, ...), custom_call_target="tpu_custom_call", output_to_operand_aliasing={{1}: (10, {}), {2}: (11, {})} | custom-call | tf_op jit(solution)/shard_map/input_grad/pallas_call | solution.py:117
  108.6 1.6 %collective-permute-done.17 = bf16[2,2,48,1152]{3,2,1,0:T(8,128)(2,1)S(1)} collective-permute-done((bf16[2,2,48,1152]{3,2,1,0:T(8,128)(2,1)S(1)}, bf16[2,2,48,1152]{3,2,1,0:T(8,128)(2,1)S(1)}, u32[]{:S(2)}, u32[]{:S(2)}) %collective-permute-start.17) | collective-permute-done | bytes 442400 | tf_op jit(solution)/shard_map/ppermute | solution.py:625
  110.4 3.3 %collective-permute-start.19 = (bf16[2,48,1536]{2,1,0:T(8,128)(2,1)S(1)}, bf16[2,48,1536]{2,1,0:T(8,128)(2,1)S(1)}, u32[]{:S(2)}, u32[]{:S(2)}) collective-permute-start(bf16[2,48,1536]{2,1,0:T(8,128)(2,1)S(1)} %get-tuple-element.132.refs_5_), channel_id=1, source_target_pairs={{0,8},{4,12},{8,0},{12,4},{16,24},{20,28},{24,16},{28,20},{1,9},{5... | collective-permute-start | bytes 884744 | tf_op jit(solution)/shard_map/ppermute | solution.py:625
  113.7 5.3 %layer_out.1 = (bf16[2048,384]{1,0:T(8,128)(2,1)}, bf16[2,48,1536]{2,1,0:T(8,128)(2,1)S(1)}) custom-call(s32[18]{0:T(128)S(1)} %pad_add_fusion.refs_0_, f32[2048,384]{1,0:T(8,128)S(1)} %get-tuple-element.78.refs_1_, bf16[2048,1536]{1,0:T(8,128)(2,1)S(1)} %bitcast.112, ...), custom_call_target="tpu_custom_call", output_to_operand_aliasing={{1}: (6, {})} | custom-call | tf_op jit(solution)/shard_map/layer_out/pallas_call | solution.py:117
  119.0 1.7 %collective-permute-done.19 = bf16[2,48,1536]{2,1,0:T(8,128)(2,1)S(1)} collective-permute-done((bf16[2,48,1536]{2,1,0:T(8,128)(2,1)S(1)}, bf16[2,48,1536]{2,1,0:T(8,128)(2,1)S(1)}, u32[]{:S(2)}, u32[]{:S(2)}) %collective-permute-start.19) | collective-permute-done | bytes 294944 | tf_op jit(solution)/shard_map/ppermute | solution.py:625
  120.8 2.1 %collective-permute-start.20 = (bf16[48,1536]{1,0:T(8,128)(2,1)S(1)}, bf16[48,1536]{1,0:T(8,128)(2,1)S(1)}, u32[]{:S(2)}, u32[]{:S(2)}) collective-permute-start(bf16[48,1536]{1,0:T(8,128)(2,1)S(1)} %dynamic-slice_bitcast_fusion.4), channel_id=1, source_target_pairs={{0,16},{4,20},{8,24},{12,28},{16,0},{20,4},{24,8},{28,12},{1,17},{... | collective-permute-start | bytes 442376 | tf_op jit(solution)/shard_map/ppermute | solution.py:625
  122.8 7.1 %collective-permute-done.20 = bf16[48,1536]{1,0:T(8,128)(2,1)S(1)} collective-permute-done((bf16[48,1536]{1,0:T(8,128)(2,1)S(1)}, bf16[48,1536]{1,0:T(8,128)(2,1)S(1)}, u32[]{:S(2)}, u32[]{:S(2)}) %collective-permute-start.20) | collective-permute-done | bytes 147488 | tf_op jit(solution)/shard_map/ppermute | solution.py:625
  130.1 5.1 %collective-permute-done.21 = bf16[48,1536]{1,0:T(8,128)(2,1)S(1)} collective-permute-done((bf16[48,1536]{1,0:T(8,128)(2,1)S(1)}, bf16[48,1536]{1,0:T(8,128)(2,1)S(1)}, u32[]{:S(2)}, u32[]{:S(2)}) %collective-permute-start.21) | collective-permute-done | bytes 147488 | tf_op jit(solution)/shard_map/ppermute | solution.py:625
  136.8 1.7 %finish.1 = (f32[432,128]{1,0:T(8,128)}, f32[144,128]{1,0:T(8,128)}, f32[576,128]{1,0:T(8,128)}, f32[576,128]{1,0:T(8,128)}, f32[16,128]{1,0:T(8,128)S(1)}) custom-call(s32[18]{0:T(128)S(1)} %pad_add_fusion.refs_0_, bf16[48,2432]{1,0:T(8,128)(2,1)S(1)} %pad_maximum_fusion.6.refs_1_, bf16[48,2432]{1,0:T(8,128)(2,1)S(1)} %collective-permute-done.22.refs_2_), custom_call_target="tpu_custom_call" | custom-call | tf_op jit(solution)/shard_map/finish/pallas_call | solution.py:117
  (126 shorter events, 19.9 us)
Async XLA Ops:
  4.2 7.4 %collective-permute-start = (bf16[48,640]{1,0:T(8,128)(2,1)S(1)}, bf16[48,640]{1,0:T(8,128)(2,1)S(1)}, u32[]{:S(2)}, u32[]{:S(2)}) collective-permute-start(bf16[48,640]{1,0:T(8,128)(2,1)S(1)} %maximum_maximum_fusion), channel_id=1, source_target_pairs={{0,16},{4,20},{8,24},{12,28},{16,0},{20,4},{24,8},{28,12},{1,17},{... | collective-permute-start | bytes 184328 | tf_op jit(solution)/shard_map/ppermute | solution.py:625
  11.4 6.3 %collective-permute-start.4 = (bf16[48,896]{1,0:T(8,128)(2,1)S(1)}, bf16[48,896]{1,0:T(8,128)(2,1)S(1)}, u32[]{:S(2)}, u32[]{:S(2)}) collective-permute-start(bf16[48,896]{1,0:T(8,128)(2,1)S(1)} %pad_maximum_fusion.10), channel_id=1, source_target_pairs={{0,16},{4,20},{8,24},{12,28},{16,0},{20,4},{24,8},{28,12},{1,17},{... | collective-permute-start | bytes 258056 | tf_op jit(solution)/shard_map/ppermute | solution.py:625
  11.7 7.7 %collective-permute-start.1 = (bf16[2,48,640]{2,1,0:T(8,128)(2,1)S(1)}, bf16[2,48,640]{2,1,0:T(8,128)(2,1)S(1)}, u32[]{:S(2)}, u32[]{:S(2)}) collective-permute-start(bf16[2,48,640]{2,1,0:T(8,128)(2,1)S(1)} %pad_maximum_fusion.9), channel_id=1, source_target_pairs={{0,8},{4,12},{8,0},{12,4},{16,24},{20,28},{24,16},{28,20},{1,9},{5... | collective-permute-start | bytes 368648 | tf_op jit(solution)/shard_map/ppermute | solution.py:625
  17.8 5.5 %collective-permute-start.5 = (bf16[2,48,896]{2,1,0:T(8,128)(2,1)S(1)}, bf16[2,48,896]{2,1,0:T(8,128)(2,1)S(1)}, u32[]{:S(2)}, u32[]{:S(2)}) collective-permute-start(bf16[2,48,896]{2,1,0:T(8,128)(2,1)S(1)} %pad_maximum_fusion.7), channel_id=1, source_target_pairs={{0,8},{4,12},{8,0},{12,4},{16,24},{20,28},{24,16},{28,20},{1,9},{5... | collective-permute-start | bytes 516104 | tf_op jit(solution)/shard_map/ppermute | solution.py:625
  19.5 7.8 %collective-permute-start.2 = (bf16[2,2,48,640]{3,2,0,1:T(8,128)(2,1)S(1)}, bf16[2,2,48,640]{3,2,0,1:T(8,128)(2,1)S(1)}, u32[]{:S(2)}, u32[]{:S(2)}) collective-permute-start(bf16[2,2,48,640]{3,2,0,1:T(8,128)(2,1)S(1)} %pad_maximum_fusion.5), channel_id=1, source_target_pairs={{0,4},{4,0},{8,12},{12,8},{16,20},{20,16},{24,28},{28,24},{1,5},{5... | collective-permute-start | bytes 737288 | tf_op jit(solution)/shard_map/ppermute | solution.py:625
  23.4 8.0 %collective-permute-start.7 = (bf16[2,2,48,384]{3,2,1,0:T(8,128)(2,1)S(1)}, bf16[2,2,48,384]{3,2,1,0:T(8,128)(2,1)S(1)}, u32[]{:S(2)}, u32[]{:S(2)}) collective-permute-start(bf16[2,2,48,384]{3,2,1,0:T(8,128)(2,1)S(1)} %pad_maximum_fusion.8), channel_id=1, source_target_pairs={{0,4},{4,0},{8,12},{12,8},{16,20},{20,16},{24,28},{28,24},{1,5},{5... | collective-permute-start | bytes 442376 | tf_op jit(solution)/shard_map/ppermute | solution.py:625
  25.0 5.7 %collective-permute-start.6 = (bf16[2,2,48,512]{3,2,1,0:T(8,128)(2,1)S(1)}, bf16[2,2,48,512]{3,2,1,0:T(8,128)(2,1)S(1)}, u32[]{:S(2)}, u32[]{:S(2)}) collective-permute-start(bf16[2,2,48,512]{3,2,1,0:T(8,128)(2,1)S(1)} %fusion.9), channel_id=1, source_target_pairs={{0,2},{1,3},{2,0},{3,1},{4,6},{5,7},{6,4},{7,5},{8,10},{9,11},{10,... | collective-permute-start | bytes 589832 | tf_op jit(solution)/shard_map/ppermute | solution.py:625
  27.5 5.6 %collective-permute-start.3 = (bf16[384,640]{1,0:T(8,128)(2,1)S(1)}, bf16[384,640]{1,0:T(8,128)(2,1)S(1)}, u32[]{:S(2)}, u32[]{:S(2)}) collective-permute-start(bf16[384,640]{1,0:T(8,128)(2,1)S(1)} %bitcast.107), channel_id=1, source_target_pairs={{0,1},{1,0},{2,3},{3,2},{4,5},{5,4},{6,7},{7,6},{8,9},{9,8},{10,11... | collective-permute-start | bytes 1474568 | tf_op jit(solution)/shard_map/ppermute | solution.py:625
  30.8 14.6 %collective-permute-start.8 = (bf16[2,2,2,48,512]{4,3,2,1,0:T(8,128)(2,1)S(1)}, bf16[2,2,2,48,512]{4,3,2,1,0:T(8,128)(2,1)S(1)}, u32[]{:S(2)}, u32[]{:S(2)}) collective-permute-start(bf16[2,2,2,48,512]{4,3,2,1,0:T(8,128)(2,1)S(1)} %pad_maximum_fusion.3.refs_4_), channel_id=1, source_target_pairs={{0,4},{4,0},{8,12},{12,8},{16,20},{20,16},{24,28},{28,24},{1,5},{5... | collective-permute-start | bytes 1179656 | tf_op jit(solution)/shard_map/ppermute | solution.py:625
  31.5 14.2 %collective-permute-start.10 = (bf16[2,2,2,48,384]{4,3,2,1,0:T(8,128)(2,1)S(1)}, bf16[2,2,2,48,384]{4,3,2,1,0:T(8,128)(2,1)S(1)}, u32[]{:S(2)}, u32[]{:S(2)}) collective-permute-start(bf16[2,2,2,48,384]{4,3,2,1,0:T(8,128)(2,1)S(1)} %pad_maximum_fusion.4.refs_5_), channel_id=1, source_target_pairs={{0,2},{1,3},{2,0},{3,1},{4,6},{5,7},{6,4},{7,5},{8,10},{9,11},{10,... | collective-permute-start | bytes 884744 | tf_op jit(solution)/shard_map/ppermute | solution.py:625
  45.6 3.2 %collective-permute-start.9 = (bf16[2,384,512]{2,1,0:T(8,128)(2,1)S(1)}, bf16[2,384,512]{2,1,0:T(8,128)(2,1)S(1)}, u32[]{:S(2)}, u32[]{:S(2)}) collective-permute-start(bf16[2,384,512]{2,1,0:T(8,128)(2,1)S(1)} %bitcast.113), channel_id=1, source_target_pairs={{0,1},{1,0},{2,3},{3,2},{4,5},{5,4},{6,7},{7,6},{8,9},{9,8},{10,11... | collective-permute-start | bytes 2359304 | tf_op jit(solution)/shard_map/ppermute | solution.py:625
  45.9 2.9 %collective-permute-start.11 = (bf16[2,384,384]{2,1,0:T(8,128)(2,1)S(1)}, bf16[2,384,384]{2,1,0:T(8,128)(2,1)S(1)}, u32[]{:S(2)}, u32[]{:S(2)}) collective-permute-start(bf16[2,384,384]{2,1,0:T(8,128)(2,1)S(1)} %pad_maximum_fusion.1.refs_7_.refs_3_), channel_id=1, source_target_pairs={{0,1},{1,0},{2,3},{3,2},{4,5},{5,4},{6,7},{7,6},{8,9},{9,8},{10,11... | collective-permute-start | bytes 1769480 | tf_op jit(solution)/shard_map/ppermute | solution.py:625
  48.8 26.1 %copy-start.1 = (bf16[2,384,384]{2,1,0:T(8,128)(2,1)}, bf16[2,384,384]{2,1,0:T(8,128)(2,1)S(1)}, u32[]{:S(2)}) copy-start(bf16[2,384,384]{2,1,0:T(8,128)(2,1)S(1)} %collective-permute-done.11.refs_8_.refs_4_) | copy-start | bytes 1769476
  74.9 10.0 %collective-permute-start.13 = (bf16[2,2,192,384]{3,2,1,0:T(8,128)(2,1)S(1)}, bf16[2,2,192,384]{3,2,1,0:T(8,128)(2,1)S(1)}, u32[]{:S(2)}, u32[]{:S(2)}) collective-permute-start(bf16[2,2,192,384]{3,2,1,0:T(8,128)(2,1)S(1)} %get-tuple-element.90.refs_8_), channel_id=1, source_target_pairs={{0,1},{1,0},{2,3},{3,2},{4,5},{5,4},{6,7},{7,6},{8,9},{9,8},{10,11... | collective-permute-start | bytes 1769480 | tf_op jit(solution)/shard_map/ppermute | solution.py:625
  75.1 11.3 %collective-permute-start.12 = (bf16[2,384,512]{2,1,0:T(8,128)(2,1)S(1)}, bf16[2,384,512]{2,1,0:T(8,128)(2,1)S(1)}, u32[]{:S(2)}, u32[]{:S(2)}) collective-permute-start(bf16[2,384,512]{2,1,0:T(8,128)(2,1)S(1)} %get-tuple-element.89.refs_7_), channel_id=1, source_target_pairs={{0,1},{1,0},{2,3},{3,2},{4,5},{5,4},{6,7},{7,6},{8,9},{9,8},{10,11... | collective-permute-start | bytes 2359304 | tf_op jit(solution)/shard_map/ppermute | solution.py:625
  84.8 13.1 %collective-permute-start.14 = (bf16[384,640]{1,0:T(8,128)(2,1)S(1)}, bf16[384,640]{1,0:T(8,128)(2,1)S(1)}, u32[]{:S(2)}, u32[]{:S(2)}) collective-permute-start(bf16[384,640]{1,0:T(8,128)(2,1)S(1)} %get-tuple-element.97.refs_9_), channel_id=1, source_target_pairs={{0,1},{1,0},{2,3},{3,2},{4,5},{5,4},{6,7},{7,6},{8,9},{9,8},{10,11... | collective-permute-start | bytes 1474568 | tf_op jit(solution)/shard_map/ppermute | solution.py:625
  85.1 13.0 %collective-permute-start.16 = (bf16[2,2,2,48,384]{4,3,2,1,0:T(8,128)(2,1)S(1)}, bf16[2,2,2,48,384]{4,3,2,1,0:T(8,128)(2,1)S(1)}, u32[]{:S(2)}, u32[]{:S(2)}) collective-permute-start(bf16[2,2,2,48,384]{4,3,2,1,0:T(8,128)(2,1)S(1)} %get-tuple-element.134.refs_8_), channel_id=1, source_target_pairs={{0,4},{4,0},{8,12},{12,8},{16,20},{20,16},{24,28},{28,24},{1,5},{5... | collective-permute-start | bytes 884744 | tf_op jit(solution)/shard_map/ppermute | solution.py:625
  86.7 11.5 %collective-permute-start.15 = (bf16[2,2,2,48,512]{4,3,2,1,0:T(8,128)(2,1)S(1)}, bf16[2,2,2,48,512]{4,3,2,1,0:T(8,128)(2,1)S(1)}, u32[]{:S(2)}, u32[]{:S(2)}) collective-permute-start(bf16[2,2,2,48,512]{4,3,2,1,0:T(8,128)(2,1)S(1)} %get-tuple-element.128.refs_7_), channel_id=1, source_target_pairs={{0,2},{1,3},{2,0},{3,1},{4,6},{5,7},{6,4},{7,5},{8,10},{9,11},{10,... | collective-permute-start | bytes 1179656 | tf_op jit(solution)/shard_map/ppermute | solution.py:625
  98.4 11.8 %collective-permute-start.17 = (bf16[2,2,48,1152]{3,2,1,0:T(8,128)(2,1)S(1)}, bf16[2,2,48,1152]{3,2,1,0:T(8,128)(2,1)S(1)}, u32[]{:S(2)}, u32[]{:S(2)}) collective-permute-start(bf16[2,2,48,1152]{3,2,1,0:T(8,128)(2,1)S(1)} %get-tuple-element.124.refs_8_), channel_id=1, source_target_pairs={{0,4},{4,0},{8,12},{12,8},{16,20},{20,16},{24,28},{28,24},{1,5},{5... | collective-permute-start | bytes 1327112 | tf_op jit(solution)/shard_map/ppermute | solution.py:625
  99.1 9.4 %collective-permute-start.18 = (bf16[2,2,48,384]{3,2,1,0:T(8,128)(2,1)S(1)}, bf16[2,2,48,384]{3,2,1,0:T(8,128)(2,1)S(1)}, u32[]{:S(2)}, u32[]{:S(2)}) collective-permute-start(bf16[2,2,48,384]{3,2,1,0:T(8,128)(2,1)S(1)} %get-tuple-element.144.refs_9_), channel_id=1, source_target_pairs={{0,2},{1,3},{2,0},{3,1},{4,6},{5,7},{6,4},{7,5},{8,10},{9,11},{10,... | collective-permute-start | bytes 442376 | tf_op jit(solution)/shard_map/ppermute | solution.py:625
  110.4 10.3 %collective-permute-start.19 = (bf16[2,48,1536]{2,1,0:T(8,128)(2,1)S(1)}, bf16[2,48,1536]{2,1,0:T(8,128)(2,1)S(1)}, u32[]{:S(2)}, u32[]{:S(2)}) collective-permute-start(bf16[2,48,1536]{2,1,0:T(8,128)(2,1)S(1)} %get-tuple-element.132.refs_5_), channel_id=1, source_target_pairs={{0,8},{4,12},{8,0},{12,4},{16,24},{20,28},{24,16},{28,20},{1,9},{5... | collective-permute-start | bytes 884744 | tf_op jit(solution)/shard_map/ppermute | solution.py:625
  120.8 9.2 %collective-permute-start.20 = (bf16[48,1536]{1,0:T(8,128)(2,1)S(1)}, bf16[48,1536]{1,0:T(8,128)(2,1)S(1)}, u32[]{:S(2)}, u32[]{:S(2)}) collective-permute-start(bf16[48,1536]{1,0:T(8,128)(2,1)S(1)} %dynamic-slice_bitcast_fusion.4), channel_id=1, source_target_pairs={{0,16},{4,20},{8,24},{12,28},{16,0},{20,4},{24,8},{28,12},{1,17},{... | collective-permute-start | bytes 442376 | tf_op jit(solution)/shard_map/ppermute | solution.py:625
  130.0 5.2 %collective-permute-start.21 = (bf16[48,1536]{1,0:T(8,128)(2,1)S(1)}, bf16[48,1536]{1,0:T(8,128)(2,1)S(1)}, u32[]{:S(2)}, u32[]{:S(2)}) collective-permute-start(bf16[48,1536]{1,0:T(8,128)(2,1)S(1)} %fusion.8), channel_id=1, source_target_pairs={{0,2},{1,3},{2,0},{3,1},{4,6},{5,7},{6,4},{7,5},{8,10},{9,11},{10,... | collective-permute-start | bytes 442376 | tf_op jit(solution)/shard_map/ppermute | solution.py:625
  135.3 1.6 %collective-permute-start.22 = (bf16[48,2432]{1,0:T(8,128)(2,1)S(1)}, bf16[48,2432]{1,0:T(8,128)(2,1)S(1)}, u32[]{:S(2)}, u32[]{:S(2)}) collective-permute-start(bf16[48,2432]{1,0:T(8,128)(2,1)S(1)} %pad_maximum_fusion.6.refs_1_), channel_id=1, source_target_pairs={{0,1},{1,0},{2,3},{3,2},{4,5},{5,4},{6,7},{7,6},{8,9},{9,8},{10,11... | collective-permute-start | bytes 700424 | tf_op jit(solution)/shard_map/ppermute | solution.py:625
  (8 other events, 72.2 us)

commit v5 on v4

--- a/solution.py
+++ b/solution.py
@@ -22,7 +22,7 @@
 SCALE = 1.0 / math.sqrt(HEAD_DIM)
 EXP_SCALE = SCALE * math.log2(math.e)
 MIB = 1024 * 1024
-VMEM = {"attn_fwd": 12, "mlp": 24, "attn_bwd": 8, "layer_out": 8, "input_grad": 10, "finish": 10}
+VMEM = {"attn_fwd": 12, "mlp": 21, "attn_bwd": 8, "layer_out": 8, "input_grad": 10, "finish": 10}
 F32 = jnp.float32
 BF16 = jnp.bfloat16
 
@@ -364,7 +364,7 @@
     by_row = lambda cols: pl.BlockSpec((block, cols), lambda i, m: (i, 0))
     out_shape = [
         jax.ShapeDtypeStruct((rows, width), F32),
-        pltpu.HBM((rows, hidden), BF16),
+        jax.ShapeDtypeStruct((rows, hidden), BF16),
         jax.ShapeDtypeStruct((rows, width), F32),
         jax.ShapeDtypeStruct((rows, PAIR_PAD), BF16),
         jax.ShapeDtypeStruct((rows, PAIR_PAD), BF16),
@@ -582,7 +582,12 @@
         count = columns.shape[1]
         square = jnp.concatenate([columns, jnp.zeros((size, 128 - count), F32)], axis=1)
         square = jnp.concatenate([square, jnp.zeros((128 - size, 128), F32)], axis=0)
-        outs[4][...] = square.T[:16]
+        rows = square.T[:16]
+        flat = jnp.concatenate([rows[r : r + 1, :size] for r in range(8, 8 + QUARTERS)], axis=1)
+        outs[4][...] = rows
+        for n, at in enumerate(range(0, flat.shape[1], 128)):
+            piece = flat[:, at : at + 128]
+            outs[4][8 + n : 9 + n, : piece.shape[1]] = piece
 
     for c in range(2):
         pl.when(core_of(meta) == c)(partial(use, c))
@@ -595,13 +600,16 @@
         core = core_of(meta) == 1
         own, got = own.astype(F32), got.astype(F32)
         parts = final_parts(0, jnp.where(core, got, own), jnp.where(core, own, got), shards)
-        return [p.reshape(-1) for p in parts[:4]], parts[4].T
+        rows = parts[4].T
+        return [p.reshape(-1) for p in parts[:4]], rows, rows[8 : 8 + QUARTERS].reshape(-1)
     sizes = [size * 3 * width, size * width, size * QUARTERS * width, size * QUARTERS * width]
     out_shape = [jax.ShapeDtypeStruct((n // 128, 128), F32) for n in sizes + [16 * 128]]
     out_specs = [whole(t) for t in out_shape]
     kernel = partial(finish_kernel, shards=shards)
     outs = call(kernel, "finish", 1, [whole(own), whole(got)], out_specs, out_shape, [], (meta, own, got))
-    return [t.reshape(-1) for t in outs[:4]], outs[4]
+    count = QUARTERS * size
+    pieces = [outs[4][8 + n, : min(128, count - at)] for n, at in enumerate(range(0, count, 128))]
+    return [t.reshape(-1) for t in outs[:4]], outs[4], jnp.concatenate(pieces)
 
 
 def turned(shards):
@@ -736,7 +744,7 @@
     upper = jnp.broadcast_to(upper[:, None, None], (2, 8, cut)).astype(jnp.int32)
     table, sides, upper = lax.optimization_barrier((table, sides, upper))
     attn0, attn1, qkv0, qkv1, xhat, lse0, lse1, wpad0, wpad1, upper = attn_fwd(
-        table, tokens, wf, (a.part, b.part), (upper,)
+        table, tokens, wf, (), (upper,)
     )
     a.grow("fsdp", y, upper=upper[0, 0] != 0)
     b.grow("dp", 2, upper=upper[1, 0, :width] != 0)
@@ -790,8 +798,8 @@
     upper = sides["dp", 2][2]
     part = [part_g, jnp.where(upper, high, low), jnp.where(upper, low, high)]
     part = jnp.concatenate(part, axis=1)
-    flat, vectors = finish(table, part, swap(part, "dp", 1), shards)
-    g = [vectors[r, :size] for r in range(8)] + [vectors[8 : 8 + QUARTERS, :size].reshape(-1)]
+    flat, vectors, up_bias = finish(table, part, swap(part, "dp", 1), shards)
+    g = [vectors[r, :size] for r in range(8)] + [up_bias]
     qkv, proj, up, down = flat
     return (
         layer_out, grad_input, g[0], g[1], qkv, g[2], g[3], proj, g[4], g[5], g[6], up, g[8], down, g[7]

time: 140 us -> 139 us (level)
  starting transfers between devices: 25.9 us -> 29.2 us
  waiting for transfers between devices: 27.4 us -> 24.8 us
    ppermute x23, starting transfers between devices: 25.9 us -> 29.2 us  [swap(): return lax.ppermute(value, axis, [(i, i ^ bit) for i in range(size)])]
    ppermute x23, waiting for transfers between devices: 27.4 us -> 24.8 us  [swap(): return lax.ppermute(value, axis, [(i, i ^ bit) for i in range(size)])]
  transfers between devices with their start and end apart: 23 -> 23, of which waited for: 9 -> 10; matrix products, arithmetic and copies ran while one was open for 5% -> 5% of each run, Pallas kernels for 32% -> 32%
where the time goes in v5:
time: 139 us
  Pallas kernels  71.8 us (52%)
  starting transfers between devices  29.2 us (21%)
  waiting for transfers between devices  24.8 us (18%)
  local copies, waits for them, and re-layouts  8.27 us (6%)
  other arithmetic  4.22 us (3%)
    pallas_call x7, Pallas kernels, call(): pl.pallas_call(ordered, grid_spec=pltpu.PrefetchScalarGridSpec(num_scalar...  71.8 us
    ppermute x23, starting transfers between devices, swap(): return lax.ppermute(value, axis, [(i, i ^ bit) for i in range(size)])  29.2 us
    ppermute x23, waiting for transfers between devices, swap(): return lax.ppermute(value, axis, [(i, i ^ bit) for i in range(size)])  24.8 us
  transfers between devices with their start and end apart: 23, of which 10 were waited for; matrix products, arithmetic and copies ran while one was open for 5% of the time, Pallas kernels for 32%

profile of v5, /device:TPU:0, one launch (start us, length us, event | category | flops | bytes accessed | tf_op | source)
XLA Modules:
  0.0 139.4 jit_solution(2906455992637054789)
XLA Ops:
  4.2 4.0 %collective-permute-start = (bf16[48,640]{1,0:T(8,128)(2,1)S(1)}, bf16[48,640]{1,0:T(8,128)(2,1)S(1)}, u32[]{:S(2)}, u32[]{:S(2)}) collective-permute-start(bf16[48,640]{1,0:T(8,128)(2,1)S(1)} %maximum_maximum_fusion), channel_id=1, source_target_pairs={{0,16},{4,20},{8,24},{12,28},{16,0},{20,4},{24,8},{28,12},{1,17},{... | collective-permute-start | bytes 184328 | tf_op jit(solution)/shard_map/ppermute | solution.py:633
  11.7 1.9 %collective-permute-start.1 = (bf16[2,48,640]{2,1,0:T(8,128)(2,1)S(1)}, bf16[2,48,640]{2,1,0:T(8,128)(2,1)S(1)}, u32[]{:S(2)}, u32[]{:S(2)}) collective-permute-start(bf16[2,48,640]{2,1,0:T(8,128)(2,1)S(1)} %pad_maximum_fusion.9), channel_id=1, source_target_pairs={{0,8},{4,12},{8,0},{12,4},{16,24},{20,28},{24,16},{28,20},{1,9},{5... | collective-permute-start | bytes 368648 | tf_op jit(solution)/shard_map/ppermute | solution.py:633
  13.6 4.1 %collective-permute-done.4 = bf16[48,896]{1,0:T(8,128)(2,1)S(1)} collective-permute-done((bf16[48,896]{1,0:T(8,128)(2,1)S(1)}, bf16[48,896]{1,0:T(8,128)(2,1)S(1)}, u32[]{:S(2)}, u32[]{:S(2)}) %collective-permute-start.4) | collective-permute-done | bytes 86048 | tf_op jit(solution)/shard_map/ppermute | solution.py:633
  17.8 1.6 %collective-permute-start.5 = (bf16[2,48,896]{2,1,0:T(8,128)(2,1)S(1)}, bf16[2,48,896]{2,1,0:T(8,128)(2,1)S(1)}, u32[]{:S(2)}, u32[]{:S(2)}) collective-permute-start(bf16[2,48,896]{2,1,0:T(8,128)(2,1)S(1)} %pad_maximum_fusion.7), channel_id=1, source_target_pairs={{0,8},{4,12},{8,0},{12,4},{16,24},{20,28},{24,16},{28,20},{1,9},{5... | collective-permute-start | bytes 516104 | tf_op jit(solution)/shard_map/ppermute | solution.py:633
  19.5 1.6 %collective-permute-start.2 = (bf16[2,2,48,640]{3,2,0,1:T(8,128)(2,1)S(1)}, bf16[2,2,48,640]{3,2,0,1:T(8,128)(2,1)S(1)}, u32[]{:S(2)}, u32[]{:S(2)}) collective-permute-start(bf16[2,2,48,640]{3,2,0,1:T(8,128)(2,1)S(1)} %pad_maximum_fusion.5), channel_id=1, source_target_pairs={{0,4},{4,0},{8,12},{12,8},{16,20},{20,16},{24,28},{28,24},{1,5},{5... | collective-permute-start | bytes 737288 | tf_op jit(solution)/shard_map/ppermute | solution.py:633
  23.4 1.6 %collective-permute-start.9 = (bf16[2,2,48,384]{3,2,0,1:T(8,128)(2,1)S(1)}, bf16[2,2,48,384]{3,2,0,1:T(8,128)(2,1)S(1)}, u32[]{:S(2)}, u32[]{:S(2)}) collective-permute-start(bf16[2,2,48,384]{3,2,0,1:T(8,128)(2,1)S(1)} %pad_maximum_fusion.8), channel_id=1, source_target_pairs={{0,4},{4,0},{8,12},{12,8},{16,20},{20,16},{24,28},{28,24},{1,5},{5... | collective-permute-start | bytes 442376 | tf_op jit(solution)/shard_map/ppermute | solution.py:633
  25.0 1.6 %collective-permute-start.6 = (bf16[2,2,48,512]{3,2,0,1:T(8,128)(2,1)S(1)}, bf16[2,2,48,512]{3,2,0,1:T(8,128)(2,1)S(1)}, u32[]{:S(2)}, u32[]{:S(2)}) collective-permute-start(bf16[2,2,48,512]{3,2,0,1:T(8,128)(2,1)S(1)} %fusion.9), channel_id=1, source_target_pairs={{0,2},{1,3},{2,0},{3,1},{4,6},{5,7},{6,4},{7,5},{8,10},{9,11},{10,... | collective-permute-start | bytes 589832 | tf_op jit(solution)/shard_map/ppermute | solution.py:633
  27.6 3.1 %collective-permute-done.6 = bf16[2,2,48,512]{3,2,0,1:T(8,128)(2,1)S(1)} collective-permute-done((bf16[2,2,48,512]{3,2,0,1:T(8,128)(2,1)S(1)}, bf16[2,2,48,512]{3,2,0,1:T(8,128)(2,1)S(1)}, u32[]{:S(2)}, u32[]{:S(2)}) %collective-permute-start.6) | collective-permute-done | bytes 196640 | tf_op jit(solution)/shard_map/ppermute | solution.py:633
  31.5 1.6 %collective-permute-start.10 = (bf16[2,2,2,48,384]{4,3,0,1,2:T(8,128)(2,1)S(1)}, bf16[2,2,2,48,384]{4,3,0,1,2:T(8,128)(2,1)S(1)}, u32[]{:S(2)}, u32[]{:S(2)}) collective-permute-start(bf16[2,2,2,48,384]{4,3,0,1,2:T(8,128)(2,1)S(1)} %pad_maximum_fusion.4), channel_id=1, source_target_pairs={{0,2},{1,3},{2,0},{3,1},{4,6},{5,7},{6,4},{7,5},{8,10},{9,11},{10,... | collective-permute-start | bytes 884744 | tf_op jit(solution)/shard_map/ppermute | solution.py:633
  33.1 12.3 %attn_fwd.1 = (bf16[2048,256]{1,0:T(8,128)(2,1)S(1)}, bf16[2048,256]{1,0:T(8,128)(2,1)S(1)}, bf16[8,400,768]{2,1,0:T(8,128)(2,1)S(1)}, bf16[8,400,768]{2,1,0:T(8...) custom-call(s32[18]{0:T(128)S(1)} %pad_add_fusion.refs_0_, ...), custom_call_target="tpu_custom_call", output_to_operand_aliasing={{9}: (4, {})} | custom-call | tf_op jit(solution)/shard_map/attn_fwd/pallas_call | solution.py:117
  46.6 2.3 %collective-permute-done.11.refs_8_.refs_4_ = bf16[2,384,384]{2,1,0:T(8,128)(2,1)S(1)} collective-permute-done((bf16[2,384,384]{2,1,0:T(8,128)(2,1)S(1)}, bf16[2,384,384]{2,1,0:T(8,128)(2,1)S(1)}, u32[]{:S(2)}, u32[]{:S(2)}) %collective-permute-start.11) | collective-permute-done | bytes 589856 | tf_op jit(solution)/shard_map/ppermute | solution.py:633
  48.8 25.1 %mlp.1 = (f32[2048,384]{1,0:T(8,128)S(1)}, bf16[2048,1536]{1,0:T(8,128)(2,1)S(1)}, f32[2048,384]{1,0:T(8,128)S(1)}, bf16[2048,256]{1,0:T(8,128)(2,1)S(1)}, bf16[...) custom-call(s32[18]{0:T(128)S(1)} %pad_add_fusion.refs_0_, ...), custom_call_target="tpu_custom_call" | custom-call | tf_op jit(solution)/shard_map/mlp/pallas_call | solution.py:117
  74.6 9.4 %attn_bwd.2 = (bf16[8,400,768]{2,1,0:T(8,128)(2,1)S(1)}, bf16[384,640]{1,0:T(8,128)(2,1)S(1)}, bf16[2,384,512]{2,1,0:T(8,128)(2,1)S(1)}, bf16[2,2,192,384]{3,2,1,0:T(8,128)(2,1)S(1)}) custom-call(s32[18]{0:T(128)S(1)} %pad_add_fusion.refs_0_, bf16[8,400,768]{2,1,0:T(8,128)(2,1)S(1)} %get-tuple-element.85.refs_1_, ...), custom_call_target="tpu_custom_call", output_to_operand_aliasing={{2}: (9, {}), {3}: (10, {})} | custom-call | tf_op jit(solution)/shard_map/attn_bwd/pallas_call | solution.py:117
  84.7 3.5 %collective-permute-start.16 = (bf16[2,2,2,48,384]{4,3,2,1,0:T(8,128)(2,1)S(1)}, bf16[2,2,2,48,384]{4,3,2,1,0:T(8,128)(2,1)S(1)}, u32[]{:S(2)}, u32[]{:S(2)}) collective-permute-start(bf16[2,2,2,48,384]{4,3,2,1,0:T(8,128)(2,1)S(1)} %get-tuple-element.134.refs_8_), channel_id=1, source_target_pairs={{0,4},{4,0},{8,12},{12,8},{16,20},{20,16},{24,28},{28,24},{1,5},{5... | collective-permute-start | bytes 884744 | tf_op jit(solution)/shard_map/ppermute | solution.py:633
  88.6 9.6 %attn_bwd.3 = (bf16[8,400,768]{2,1,0:T(8,128)(2,1)S(1)}, bf16[384,640]{1,0:T(8,128)(2,1)S(1)}, bf16[2,2,2,48,512]{4,3,2,1,0:T(8,128)(2,1)S(1)}, bf16[2,2,2,48,384]{4,3,2,1,0:T(8,128)(2,1)S(1)}) custom-call(s32[18]{0:T(128)S(1)} %pad_add_fusion.refs_0_, ...), custom_call_target="tpu_custom_call", output_to_operand_aliasing={{2}: (10, {}), {3}: (11, {})} | custom-call | tf_op jit(solution)/shard_map/attn_bwd/pallas_call | solution.py:117
  101.2 8.4 %input_grad.1 = (bf16[2048,384]{1,0:T(8,128)(2,1)}, bf16[2,2,48,1152]{3,2,1,0:T(8,128)(2,1)S(1)}, bf16[2,2,48,384]{3,2,1,0:T(8,128)(2,1)S(1)}) custom-call(s32[18]{0:T(128)S(1)} %pad_add_fusion.refs_0_, bf16[2048,384]{1,0:T(8,128)(2,1)S(1)} %copy-done, ...), custom_call_target="tpu_custom_call", output_to_operand_aliasing={{1}: (10, {}), {2}: (11, {})} | custom-call | tf_op jit(solution)/shard_map/input_grad/pallas_call | solution.py:117
  109.6 2.0 %collective-permute-done.17 = bf16[2,2,48,1152]{3,2,1,0:T(8,128)(2,1)S(1)} collective-permute-done((bf16[2,2,48,1152]{3,2,1,0:T(8,128)(2,1)S(1)}, bf16[2,2,48,1152]{3,2,1,0:T(8,128)(2,1)S(1)}, u32[]{:S(2)}, u32[]{:S(2)}) %collective-permute-start.17) | collective-permute-done | bytes 442400 | tf_op jit(solution)/shard_map/ppermute | solution.py:633
  111.8 2.9 %collective-permute-start.19 = (bf16[2,48,1536]{2,1,0:T(8,128)(2,1)S(1)}, bf16[2,48,1536]{2,1,0:T(8,128)(2,1)S(1)}, u32[]{:S(2)}, u32[]{:S(2)}) collective-permute-start(bf16[2,48,1536]{2,1,0:T(8,128)(2,1)S(1)} %get-tuple-element.132.refs_5_), channel_id=1, source_target_pairs={{0,8},{4,12},{8,0},{12,4},{16,24},{20,28},{24,16},{28,20},{1,9},{5... | collective-permute-start | bytes 884744 | tf_op jit(solution)/shard_map/ppermute | solution.py:633
  114.6 5.3 %layer_out.1 = (bf16[2048,384]{1,0:T(8,128)(2,1)}, bf16[2,48,1536]{2,1,0:T(8,128)(2,1)S(1)}) custom-call(s32[18]{0:T(128)S(1)} %pad_add_fusion.refs_0_, f32[2048,384]{1,0:T(8,128)S(1)} %get-tuple-element.78.refs_1_, bf16[2048,1536]{1,0:T(8,128)(2,1)S(1)} %get-tuple-element.79.refs_2_, ...), custom_call_target="tpu_custom_call", output_to_operand_aliasing={{1}: (6, {})} | custom-call | tf_op jit(solution)/shard_map/layer_out/pallas_call | solution.py:117
  120.5 6.1 %collective-permute-done.20 = bf16[48,1536]{1,0:T(8,128)(2,1)S(1)} collective-permute-done((bf16[48,1536]{1,0:T(8,128)(2,1)S(1)}, bf16[48,1536]{1,0:T(8,128)(2,1)S(1)}, u32[]{:S(2)}, u32[]{:S(2)}) %collective-permute-start.20) | collective-permute-done | bytes 147488 | tf_op jit(solution)/shard_map/ppermute | solution.py:633
  126.6 5.2 %collective-permute-start.21 = (bf16[48,1536]{1,0:T(8,128)(2,1)S(1)}, bf16[48,1536]{1,0:T(8,128)(2,1)S(1)}, u32[]{:S(2)}, u32[]{:S(2)}) collective-permute-start(bf16[48,1536]{1,0:T(8,128)(2,1)S(1)} %fusion.8), channel_id=1, source_target_pairs={{0,2},{1,3},{2,0},{3,1},{4,6},{5,7},{6,4},{7,5},{8,10},{9,11},{10,... | collective-permute-start | bytes 442376 | tf_op jit(solution)/shard_map/ppermute | solution.py:633
  131.8 3.1 %collective-permute-done.21 = bf16[48,1536]{1,0:T(8,128)(2,1)S(1)} collective-permute-done((bf16[48,1536]{1,0:T(8,128)(2,1)S(1)}, bf16[48,1536]{1,0:T(8,128)(2,1)S(1)}, u32[]{:S(2)}, u32[]{:S(2)}) %collective-permute-start.21) | collective-permute-done | bytes 147488 | tf_op jit(solution)/shard_map/ppermute | solution.py:633
  135.1 1.5 %collective-permute-done.22.refs_2_ = bf16[48,2432]{1,0:T(8,128)(2,1)S(1)} collective-permute-done((bf16[48,2432]{1,0:T(8,128)(2,1)S(1)}, bf16[48,2432]{1,0:T(8,128)(2,1)S(1)}, u32[]{:S(2)}, u32[]{:S(2)}) %collective-permute-start.22) | collective-permute-done | bytes 233504 | tf_op jit(solution)/shard_map/ppermute | solution.py:633
  136.6 1.7 %finish.1 = (f32[432,128]{1,0:T(8,128)}, f32[144,128]{1,0:T(8,128)}, f32[576,128]{1,0:T(8,128)}, f32[576,128]{1,0:T(8,128)}, f32[16,128]{1,0:T(8,128)S(1)}) custom-call(s32[18]{0:T(128)S(1)} %pad_add_fusion.refs_0_, bf16[48,2432]{1,0:T(8,128)(2,1)S(1)} %pad_maximum_fusion.6.refs_1_, bf16[48,2432]{1,0:T(8,128)(2,1)S(1)} %collective-permute-done.22.refs_2_), custom_call_target="tpu_custom_call" | custom-call | tf_op jit(solution)/shard_map/finish/pallas_call | solution.py:117
  (124 shorter events, 18.8 us)
Async XLA Ops:
  4.2 7.4 %collective-permute-start = (bf16[48,640]{1,0:T(8,128)(2,1)S(1)}, bf16[48,640]{1,0:T(8,128)(2,1)S(1)}, u32[]{:S(2)}, u32[]{:S(2)}) collective-permute-start(bf16[48,640]{1,0:T(8,128)(2,1)S(1)} %maximum_maximum_fusion), channel_id=1, source_target_pairs={{0,16},{4,20},{8,24},{12,28},{16,0},{20,4},{24,8},{28,12},{1,17},{... | collective-permute-start | bytes 184328 | tf_op jit(solution)/shard_map/ppermute | solution.py:633
  11.4 6.3 %collective-permute-start.4 = (bf16[48,896]{1,0:T(8,128)(2,1)S(1)}, bf16[48,896]{1,0:T(8,128)(2,1)S(1)}, u32[]{:S(2)}, u32[]{:S(2)}) collective-permute-start(bf16[48,896]{1,0:T(8,128)(2,1)S(1)} %pad_maximum_fusion.10), channel_id=1, source_target_pairs={{0,16},{4,20},{8,24},{12,28},{16,0},{20,4},{24,8},{28,12},{1,17},{... | collective-permute-start | bytes 258056 | tf_op jit(solution)/shard_map/ppermute | solution.py:633
  11.7 7.7 %collective-permute-start.1 = (bf16[2,48,640]{2,1,0:T(8,128)(2,1)S(1)}, bf16[2,48,640]{2,1,0:T(8,128)(2,1)S(1)}, u32[]{:S(2)}, u32[]{:S(2)}) collective-permute-start(bf16[2,48,640]{2,1,0:T(8,128)(2,1)S(1)} %pad_maximum_fusion.9), channel_id=1, source_target_pairs={{0,8},{4,12},{8,0},{12,4},{16,24},{20,28},{24,16},{28,20},{1,9},{5... | collective-permute-start | bytes 368648 | tf_op jit(solution)/shard_map/ppermute | solution.py:633
  17.8 5.5 %collective-permute-start.5 = (bf16[2,48,896]{2,1,0:T(8,128)(2,1)S(1)}, bf16[2,48,896]{2,1,0:T(8,128)(2,1)S(1)}, u32[]{:S(2)}, u32[]{:S(2)}) collective-permute-start(bf16[2,48,896]{2,1,0:T(8,128)(2,1)S(1)} %pad_maximum_fusion.7), channel_id=1, source_target_pairs={{0,8},{4,12},{8,0},{12,4},{16,24},{20,28},{24,16},{28,20},{1,9},{5... | collective-permute-start | bytes 516104 | tf_op jit(solution)/shard_map/ppermute | solution.py:633
  19.5 7.8 %collective-permute-start.2 = (bf16[2,2,48,640]{3,2,0,1:T(8,128)(2,1)S(1)}, bf16[2,2,48,640]{3,2,0,1:T(8,128)(2,1)S(1)}, u32[]{:S(2)}, u32[]{:S(2)}) collective-permute-start(bf16[2,2,48,640]{3,2,0,1:T(8,128)(2,1)S(1)} %pad_maximum_fusion.5), channel_id=1, source_target_pairs={{0,4},{4,0},{8,12},{12,8},{16,20},{20,16},{24,28},{28,24},{1,5},{5... | collective-permute-start | bytes 737288 | tf_op jit(solution)/shard_map/ppermute | solution.py:633
  23.4 8.0 %collective-permute-start.9 = (bf16[2,2,48,384]{3,2,0,1:T(8,128)(2,1)S(1)}, bf16[2,2,48,384]{3,2,0,1:T(8,128)(2,1)S(1)}, u32[]{:S(2)}, u32[]{:S(2)}) collective-permute-start(bf16[2,2,48,384]{3,2,0,1:T(8,128)(2,1)S(1)} %pad_maximum_fusion.8), channel_id=1, source_target_pairs={{0,4},{4,0},{8,12},{12,8},{16,20},{20,16},{24,28},{28,24},{1,5},{5... | collective-permute-start | bytes 442376 | tf_op jit(solution)/shard_map/ppermute | solution.py:633
  25.0 5.7 %collective-permute-start.6 = (bf16[2,2,48,512]{3,2,0,1:T(8,128)(2,1)S(1)}, bf16[2,2,48,512]{3,2,0,1:T(8,128)(2,1)S(1)}, u32[]{:S(2)}, u32[]{:S(2)}) collective-permute-start(bf16[2,2,48,512]{3,2,0,1:T(8,128)(2,1)S(1)} %fusion.9), channel_id=1, source_target_pairs={{0,2},{1,3},{2,0},{3,1},{4,6},{5,7},{6,4},{7,5},{8,10},{9,11},{10,... | collective-permute-start | bytes 589832 | tf_op jit(solution)/shard_map/ppermute | solution.py:633
  27.5 5.6 %collective-permute-start.3 = (bf16[384,640]{1,0:T(8,128)(2,1)S(1)}, bf16[384,640]{1,0:T(8,128)(2,1)S(1)}, u32[]{:S(2)}, u32[]{:S(2)}) collective-permute-start(bf16[384,640]{1,0:T(8,128)(2,1)S(1)} %bitcast.107), channel_id=1, source_target_pairs={{0,1},{1,0},{2,3},{3,2},{4,5},{5,4},{6,7},{7,6},{8,9},{9,8},{10,11... | collective-permute-start | bytes 1474568 | tf_op jit(solution)/shard_map/ppermute | solution.py:633
  30.8 14.6 %collective-permute-start.7 = (bf16[2,2,2,48,512]{4,3,1,2,0:T(8,128)(2,1)S(1)}, bf16[2,2,2,48,512]{4,3,1,2,0:T(8,128)(2,1)S(1)}, u32[]{:S(2)}, u32[]{:S(2)}) collective-permute-start(bf16[2,2,2,48,512]{4,3,1,2,0:T(8,128)(2,1)S(1)} %pad_maximum_fusion.3), channel_id=1, source_target_pairs={{0,4},{4,0},{8,12},{12,8},{16,20},{20,16},{24,28},{28,24},{1,5},{5... | collective-permute-start | bytes 1179656 | tf_op jit(solution)/shard_map/ppermute | solution.py:633
  31.5 14.2 %collective-permute-start.10 = (bf16[2,2,2,48,384]{4,3,0,1,2:T(8,128)(2,1)S(1)}, bf16[2,2,2,48,384]{4,3,0,1,2:T(8,128)(2,1)S(1)}, u32[]{:S(2)}, u32[]{:S(2)}) collective-permute-start(bf16[2,2,2,48,384]{4,3,0,1,2:T(8,128)(2,1)S(1)} %pad_maximum_fusion.4), channel_id=1, source_target_pairs={{0,2},{1,3},{2,0},{3,1},{4,6},{5,7},{6,4},{7,5},{8,10},{9,11},{10,... | collective-permute-start | bytes 884744 | tf_op jit(solution)/shard_map/ppermute | solution.py:633
  45.6 3.2 %collective-permute-start.8 = (bf16[2,384,512]{2,1,0:T(8,128)(2,1)S(1)}, bf16[2,384,512]{2,1,0:T(8,128)(2,1)S(1)}, u32[]{:S(2)}, u32[]{:S(2)}) collective-permute-start(bf16[2,384,512]{2,1,0:T(8,128)(2,1)S(1)} %bitcast.111), channel_id=1, source_target_pairs={{0,1},{1,0},{2,3},{3,2},{4,5},{5,4},{6,7},{7,6},{8,9},{9,8},{10,11... | collective-permute-start | bytes 2359304 | tf_op jit(solution)/shard_map/ppermute | solution.py:633
  46.0 2.8 %collective-permute-start.11 = (bf16[2,384,384]{2,1,0:T(8,128)(2,1)S(1)}, bf16[2,384,384]{2,1,0:T(8,128)(2,1)S(1)}, u32[]{:S(2)}, u32[]{:S(2)}) collective-permute-start(bf16[2,384,384]{2,1,0:T(8,128)(2,1)S(1)} %pad_maximum_fusion.1.refs_7_.refs_3_), channel_id=1, source_target_pairs={{0,1},{1,0},{2,3},{3,2},{4,5},{5,4},{6,7},{7,6},{8,9},{9,8},{10,11... | collective-permute-start | bytes 1769480 | tf_op jit(solution)/shard_map/ppermute | solution.py:633
  48.8 25.1 %copy-start.1 = (bf16[2,384,384]{2,1,0:T(8,128)(2,1)}, bf16[2,384,384]{2,1,0:T(8,128)(2,1)S(1)}, u32[]{:S(2)}) copy-start(bf16[2,384,384]{2,1,0:T(8,128)(2,1)S(1)} %collective-permute-done.11.refs_8_.refs_4_) | copy-start | bytes 1769476
  74.0 10.5 %collective-permute-start.13 = (bf16[2,2,192,384]{3,2,1,0:T(8,128)(2,1)S(1)}, bf16[2,2,192,384]{3,2,1,0:T(8,128)(2,1)S(1)}, u32[]{:S(2)}, u32[]{:S(2)}) collective-permute-start(bf16[2,2,192,384]{3,2,1,0:T(8,128)(2,1)S(1)} %get-tuple-element.90.refs_8_), channel_id=1, source_target_pairs={{0,1},{1,0},{2,3},{3,2},{4,5},{5,4},{6,7},{7,6},{8,9},{9,8},{10,11... | collective-permute-start | bytes 1769480 | tf_op jit(solution)/shard_map/ppermute | solution.py:633
  74.2 14.1 %collective-permute-start.12 = (bf16[2,384,512]{2,1,0:T(8,128)(2,1)S(1)}, bf16[2,384,512]{2,1,0:T(8,128)(2,1)S(1)}, u32[]{:S(2)}, u32[]{:S(2)}) collective-permute-start(bf16[2,384,512]{2,1,0:T(8,128)(2,1)S(1)} %get-tuple-element.89.refs_7_), channel_id=1, source_target_pairs={{0,1},{1,0},{2,3},{3,2},{4,5},{5,4},{6,7},{7,6},{8,9},{9,8},{10,11... | collective-permute-start | bytes 2359304 | tf_op jit(solution)/shard_map/ppermute | solution.py:633
  83.9 14.3 %collective-permute-start.14 = (bf16[384,640]{1,0:T(8,128)(2,1)S(1)}, bf16[384,640]{1,0:T(8,128)(2,1)S(1)}, u32[]{:S(2)}, u32[]{:S(2)}) collective-permute-start(bf16[384,640]{1,0:T(8,128)(2,1)S(1)} %get-tuple-element.97.refs_9_), channel_id=1, source_target_pairs={{0,1},{1,0},{2,3},{3,2},{4,5},{5,4},{6,7},{7,6},{8,9},{9,8},{10,11... | collective-permute-start | bytes 1474568 | tf_op jit(solution)/shard_map/ppermute | solution.py:633
  84.7 13.6 %collective-permute-start.16 = (bf16[2,2,2,48,384]{4,3,2,1,0:T(8,128)(2,1)S(1)}, bf16[2,2,2,48,384]{4,3,2,1,0:T(8,128)(2,1)S(1)}, u32[]{:S(2)}, u32[]{:S(2)}) collective-permute-start(bf16[2,2,2,48,384]{4,3,2,1,0:T(8,128)(2,1)S(1)} %get-tuple-element.134.refs_8_), channel_id=1, source_target_pairs={{0,4},{4,0},{8,12},{12,8},{16,20},{20,16},{24,28},{28,24},{1,5},{5... | collective-permute-start | bytes 884744 | tf_op jit(solution)/shard_map/ppermute | solution.py:633
  88.6 11.3 %collective-permute-start.15 = (bf16[2,2,2,48,512]{4,3,2,1,0:T(8,128)(2,1)S(1)}, bf16[2,2,2,48,512]{4,3,2,1,0:T(8,128)(2,1)S(1)}, u32[]{:S(2)}, u32[]{:S(2)}) collective-permute-start(bf16[2,2,2,48,512]{4,3,2,1,0:T(8,128)(2,1)S(1)} %get-tuple-element.128.refs_7_), channel_id=1, source_target_pairs={{0,2},{1,3},{2,0},{3,1},{4,6},{5,7},{6,4},{7,5},{8,10},{9,11},{10,... | collective-permute-start | bytes 1179656 | tf_op jit(solution)/shard_map/ppermute | solution.py:633
  100.1 11.5 %collective-permute-start.17 = (bf16[2,2,48,1152]{3,2,1,0:T(8,128)(2,1)S(1)}, bf16[2,2,48,1152]{3,2,1,0:T(8,128)(2,1)S(1)}, u32[]{:S(2)}, u32[]{:S(2)}) collective-permute-start(bf16[2,2,48,1152]{3,2,1,0:T(8,128)(2,1)S(1)} %get-tuple-element.124.refs_8_), channel_id=1, source_target_pairs={{0,4},{4,0},{8,12},{12,8},{16,20},{20,16},{24,28},{28,24},{1,5},{5... | collective-permute-start | bytes 1327112 | tf_op jit(solution)/shard_map/ppermute | solution.py:633
  100.5 9.0 %collective-permute-start.18 = (bf16[2,2,48,384]{3,2,1,0:T(8,128)(2,1)S(1)}, bf16[2,2,48,384]{3,2,1,0:T(8,128)(2,1)S(1)}, u32[]{:S(2)}, u32[]{:S(2)}) collective-permute-start(bf16[2,2,48,384]{3,2,1,0:T(8,128)(2,1)S(1)} %get-tuple-element.144.refs_9_), channel_id=1, source_target_pairs={{0,2},{1,3},{2,0},{3,1},{4,6},{5,7},{6,4},{7,5},{8,10},{9,11},{10,... | collective-permute-start | bytes 442376 | tf_op jit(solution)/shard_map/ppermute | solution.py:633
  111.8 8.5 %collective-permute-start.19 = (bf16[2,48,1536]{2,1,0:T(8,128)(2,1)S(1)}, bf16[2,48,1536]{2,1,0:T(8,128)(2,1)S(1)}, u32[]{:S(2)}, u32[]{:S(2)}) collective-permute-start(bf16[2,48,1536]{2,1,0:T(8,128)(2,1)S(1)} %get-tuple-element.132.refs_5_), channel_id=1, source_target_pairs={{0,8},{4,12},{8,0},{12,4},{16,24},{20,28},{24,16},{28,20},{1,9},{5... | collective-permute-start | bytes 884744 | tf_op jit(solution)/shard_map/ppermute | solution.py:633
  120.4 6.2 %collective-permute-start.20 = (bf16[48,1536]{1,0:T(8,128)(2,1)S(1)}, bf16[48,1536]{1,0:T(8,128)(2,1)S(1)}, u32[]{:S(2)}, u32[]{:S(2)}) collective-permute-start(bf16[48,1536]{1,0:T(8,128)(2,1)S(1)} %dynamic-slice_bitcast_fusion.4), channel_id=1, source_target_pairs={{0,16},{4,20},{8,24},{12,28},{16,0},{20,4},{24,8},{28,12},{1,17},{... | collective-permute-start | bytes 442376 | tf_op jit(solution)/shard_map/ppermute | solution.py:633
  126.6 8.3 %collective-permute-start.21 = (bf16[48,1536]{1,0:T(8,128)(2,1)S(1)}, bf16[48,1536]{1,0:T(8,128)(2,1)S(1)}, u32[]{:S(2)}, u32[]{:S(2)}) collective-permute-start(bf16[48,1536]{1,0:T(8,128)(2,1)S(1)} %fusion.8), channel_id=1, source_target_pairs={{0,2},{1,3},{2,0},{3,1},{4,6},{5,7},{6,4},{7,5},{8,10},{9,11},{10,... | collective-permute-start | bytes 442376 | tf_op jit(solution)/shard_map/ppermute | solution.py:633
  135.0 1.6 %collective-permute-start.22 = (bf16[48,2432]{1,0:T(8,128)(2,1)S(1)}, bf16[48,2432]{1,0:T(8,128)(2,1)S(1)}, u32[]{:S(2)}, u32[]{:S(2)}) collective-permute-start(bf16[48,2432]{1,0:T(8,128)(2,1)S(1)} %pad_maximum_fusion.6.refs_1_), channel_id=1, source_target_pairs={{0,1},{1,0},{2,3},{3,2},{4,5},{5,4},{6,7},{7,6},{8,9},{9,8},{10,11... | collective-permute-start | bytes 700424 | tf_op jit(solution)/shard_map/ppermute | solution.py:633
  (6 other events, 45.0 us)

commit v6 on v5

--- a/solution.py
+++ b/solution.py
@@ -337,7 +337,7 @@
             for x in range(2):
                 at = (2 * half + x) * width
                 put_blocks(to_a.at[x], gu[:, at : at + width].astype(BF16), 0, shards)
-                part = gd[:, at : at + width].T.astype(BF16)
+                part = gd[:, at : at + width].astype(BF16).T
                 for y in range(2):
                     put_blocks(to_b.at[y, x], part, 0, shards, y)
 
@@ -347,10 +347,10 @@
                 at = (r ^ (2 * c)) * width
                 rows_of.append(gsum[4:5, at : at + width])
             vec = jnp.concatenate(rows_of + [jnp.zeros((VEC - 8, width), F32)], axis=0).T
-            grad = unpad_heads(gp[...]).T
+            grad = unpad_heads(gp[...].astype(BF16)).T
             first, second = grad[:PAIR_DIM], grad[PAIR_DIM:]
             proj = jnp.concatenate([second, first] if c else [first, second], axis=0)
-            flat = jnp.concatenate([proj, vec], axis=1).astype(BF16)
+            flat = jnp.concatenate([proj, vec.astype(BF16)], axis=1)
             for k in range(QUARTERS):
                 to = (low, high)[k // 2].at[k % 2]
                 put_blocks(to, flat[:, k * VEC : (k + 1) * VEC], width, shards)
@@ -476,7 +476,7 @@
         gain_term = jnp.sum(raw * w, axis=1, keepdims=True)
         bias_term = jnp.sum(col * w, axis=1, keepdims=True)
         vec = wf[:, 3 * PAIR_DIM :].astype(F32)
-        main = unpad_heads(raw * vec[:, 0:1] + vec[:, 1:2] * col).astype(BF16)
+        main = unpad_heads((raw * vec[:, 0:1] + vec[:, 1:2] * col).astype(BF16))
         put_blocks(grads, main, 0, shards)
         q_sum = unpad_heads(gsum[0:1, :PAIR_PAD])
         v_sum = unpad_heads(gsum[0:1, 2 * PAIR_PAD :])

time: 139 us -> 137 us (0.986)
  starting transfers between devices: 29.2 us -> 27 us
    ppermute x23, starting transfers between devices: 29.2 us -> 27 us  [swap(): return lax.ppermute(value, axis, [(i, i ^ bit) for i in range(size)])]
  transfers between devices with their start and end apart: 23 -> 23, of which waited for: 10 -> 10; matrix products, arithmetic and copies ran while one was open for 5% -> 5% of each run, Pallas kernels for 32% -> 33%
where the time goes in v6:
time: 137 us
  Pallas kernels  72 us (53%)
  starting transfers between devices  27 us (20%)
  waiting for transfers between devices  24.4 us (18%)
  local copies, waits for them, and re-layouts  8.27 us (6%)
  other arithmetic  4.23 us (3%)
    pallas_call x7, Pallas kernels, call(): pl.pallas_call(ordered, grid_spec=pltpu.PrefetchScalarGridSpec(num_scalar...  72 us
    ppermute x23, starting transfers between devices, swap(): return lax.ppermute(value, axis, [(i, i ^ bit) for i in range(size)])  27 us
    ppermute x23, waiting for transfers between devices, swap(): return lax.ppermute(value, axis, [(i, i ^ bit) for i in range(size)])  24.4 us
  transfers between devices with their start and end apart: 23, of which 10 were waited for; matrix products, arithmetic and copies ran while one was open for 5% of the time, Pallas kernels for 33%

profile of v6, /device:TPU:0, one launch (start us, length us, event | category | flops | bytes accessed | tf_op | source)
XLA Modules:
  0.0 137.0 jit_solution(10194299784568870161)
XLA Ops:
  4.2 4.0 %collective-permute-start = (bf16[48,640]{1,0:T(8,128)(2,1)S(1)}, bf16[48,640]{1,0:T(8,128)(2,1)S(1)}, u32[]{:S(2)}, u32[]{:S(2)}) collective-permute-start(bf16[48,640]{1,0:T(8,128)(2,1)S(1)} %maximum_maximum_fusion), channel_id=1, source_target_pairs={{0,16},{4,20},{8,24},{12,28},{16,0},{20,4},{24,8},{28,12},{1,17},{... | collective-permute-start | bytes 184328 | tf_op jit(solution)/shard_map/ppermute | solution.py:633
  11.7 1.9 %collective-permute-start.1 = (bf16[2,48,640]{2,1,0:T(8,128)(2,1)S(1)}, bf16[2,48,640]{2,1,0:T(8,128)(2,1)S(1)}, u32[]{:S(2)}, u32[]{:S(2)}) collective-permute-start(bf16[2,48,640]{2,1,0:T(8,128)(2,1)S(1)} %pad_maximum_fusion.9), channel_id=1, source_target_pairs={{0,8},{4,12},{8,0},{12,4},{16,24},{20,28},{24,16},{28,20},{1,9},{5... | collective-permute-start | bytes 368648 | tf_op jit(solution)/shard_map/ppermute | solution.py:633
  13.6 4.1 %collective-permute-done.4 = bf16[48,896]{1,0:T(8,128)(2,1)S(1)} collective-permute-done((bf16[48,896]{1,0:T(8,128)(2,1)S(1)}, bf16[48,896]{1,0:T(8,128)(2,1)S(1)}, u32[]{:S(2)}, u32[]{:S(2)}) %collective-permute-start.4) | collective-permute-done | bytes 86048 | tf_op jit(solution)/shard_map/ppermute | solution.py:633
  17.8 1.6 %collective-permute-start.5 = (bf16[2,48,896]{2,1,0:T(8,128)(2,1)S(1)}, bf16[2,48,896]{2,1,0:T(8,128)(2,1)S(1)}, u32[]{:S(2)}, u32[]{:S(2)}) collective-permute-start(bf16[2,48,896]{2,1,0:T(8,128)(2,1)S(1)} %pad_maximum_fusion.7), channel_id=1, source_target_pairs={{0,8},{4,12},{8,0},{12,4},{16,24},{20,28},{24,16},{28,20},{1,9},{5... | collective-permute-start | bytes 516104 | tf_op jit(solution)/shard_map/ppermute | solution.py:633
  19.5 1.6 %collective-permute-start.2 = (bf16[2,2,48,640]{3,2,0,1:T(8,128)(2,1)S(1)}, bf16[2,2,48,640]{3,2,0,1:T(8,128)(2,1)S(1)}, u32[]{:S(2)}, u32[]{:S(2)}) collective-permute-start(bf16[2,2,48,640]{3,2,0,1:T(8,128)(2,1)S(1)} %pad_maximum_fusion.5), channel_id=1, source_target_pairs={{0,4},{4,0},{8,12},{12,8},{16,20},{20,16},{24,28},{28,24},{1,5},{5... | collective-permute-start | bytes 737288 | tf_op jit(solution)/shard_map/ppermute | solution.py:633
  23.4 1.6 %collective-permute-start.9 = (bf16[2,2,48,384]{3,2,0,1:T(8,128)(2,1)S(1)}, bf16[2,2,48,384]{3,2,0,1:T(8,128)(2,1)S(1)}, u32[]{:S(2)}, u32[]{:S(2)}) collective-permute-start(bf16[2,2,48,384]{3,2,0,1:T(8,128)(2,1)S(1)} %pad_maximum_fusion.8), channel_id=1, source_target_pairs={{0,4},{4,0},{8,12},{12,8},{16,20},{20,16},{24,28},{28,24},{1,5},{5... | collective-permute-start | bytes 442376 | tf_op jit(solution)/shard_map/ppermute | solution.py:633
  25.0 1.6 %collective-permute-start.6 = (bf16[2,2,48,512]{3,2,0,1:T(8,128)(2,1)S(1)}, bf16[2,2,48,512]{3,2,0,1:T(8,128)(2,1)S(1)}, u32[]{:S(2)}, u32[]{:S(2)}) collective-permute-start(bf16[2,2,48,512]{3,2,0,1:T(8,128)(2,1)S(1)} %fusion.9), channel_id=1, source_target_pairs={{0,2},{1,3},{2,0},{3,1},{4,6},{5,7},{6,4},{7,5},{8,10},{9,11},{10,... | collective-permute-start | bytes 589832 | tf_op jit(solution)/shard_map/ppermute | solution.py:633
  27.6 3.1 %collective-permute-done.6 = bf16[2,2,48,512]{3,2,0,1:T(8,128)(2,1)S(1)} collective-permute-done((bf16[2,2,48,512]{3,2,0,1:T(8,128)(2,1)S(1)}, bf16[2,2,48,512]{3,2,0,1:T(8,128)(2,1)S(1)}, u32[]{:S(2)}, u32[]{:S(2)}) %collective-permute-start.6) | collective-permute-done | bytes 196640 | tf_op jit(solution)/shard_map/ppermute | solution.py:633
  31.5 1.6 %collective-permute-start.10 = (bf16[2,2,2,48,384]{4,3,0,1,2:T(8,128)(2,1)S(1)}, bf16[2,2,2,48,384]{4,3,0,1,2:T(8,128)(2,1)S(1)}, u32[]{:S(2)}, u32[]{:S(2)}) collective-permute-start(bf16[2,2,2,48,384]{4,3,0,1,2:T(8,128)(2,1)S(1)} %pad_maximum_fusion.4), channel_id=1, source_target_pairs={{0,2},{1,3},{2,0},{3,1},{4,6},{5,7},{6,4},{7,5},{8,10},{9,11},{10,... | collective-permute-start | bytes 884744 | tf_op jit(solution)/shard_map/ppermute | solution.py:633
  33.1 12.4 %attn_fwd.1 = (bf16[2048,256]{1,0:T(8,128)(2,1)S(1)}, bf16[2048,256]{1,0:T(8,128)(2,1)S(1)}, bf16[8,400,768]{2,1,0:T(8,128)(2,1)S(1)}, bf16[8,400,768]{2,1,0:T(8...) custom-call(s32[18]{0:T(128)S(1)} %pad_add_fusion.refs_0_, ...), custom_call_target="tpu_custom_call", output_to_operand_aliasing={{9}: (4, {})} | custom-call | tf_op jit(solution)/shard_map/attn_fwd/pallas_call | solution.py:117
  46.7 2.3 %collective-permute-done.11.refs_8_.refs_4_ = bf16[2,384,384]{2,1,0:T(8,128)(2,1)S(1)} collective-permute-done((bf16[2,384,384]{2,1,0:T(8,128)(2,1)S(1)}, bf16[2,384,384]{2,1,0:T(8,128)(2,1)S(1)}, u32[]{:S(2)}, u32[]{:S(2)}) %collective-permute-start.11) | collective-permute-done | bytes 589856 | tf_op jit(solution)/shard_map/ppermute | solution.py:633
  48.9 25.0 %mlp.1 = (f32[2048,384]{1,0:T(8,128)S(1)}, bf16[2048,1536]{1,0:T(8,128)(2,1)S(1)}, f32[2048,384]{1,0:T(8,128)S(1)}, bf16[2048,256]{1,0:T(8,128)(2,1)S(1)}, bf16[...) custom-call(s32[18]{0:T(128)S(1)} %pad_add_fusion.refs_0_, ...), custom_call_target="tpu_custom_call" | custom-call | tf_op jit(solution)/shard_map/mlp/pallas_call | solution.py:117
  74.6 9.4 %attn_bwd.2 = (bf16[8,400,768]{2,1,0:T(8,128)(2,1)S(1)}, bf16[384,640]{1,0:T(8,128)(2,1)S(1)}, bf16[2,384,512]{2,1,0:T(8,128)(2,1)S(1)}, bf16[2,2,192,384]{3,2,1,0:T(8,128)(2,1)S(1)}) custom-call(s32[18]{0:T(128)S(1)} %pad_add_fusion.refs_0_, bf16[8,400,768]{2,1,0:T(8,128)(2,1)S(1)} %get-tuple-element.85.refs_1_, ...), custom_call_target="tpu_custom_call", output_to_operand_aliasing={{2}: (9, {}), {3}: (10, {})} | custom-call | tf_op jit(solution)/shard_map/attn_bwd/pallas_call | solution.py:117
  84.4 1.8 %collective-permute-start.16 = (bf16[2,2,2,48,384]{4,3,2,1,0:T(8,128)(2,1)S(1)}, bf16[2,2,2,48,384]{4,3,2,1,0:T(8,128)(2,1)S(1)}, u32[]{:S(2)}, u32[]{:S(2)}) collective-permute-start(bf16[2,2,2,48,384]{4,3,2,1,0:T(8,128)(2,1)S(1)} %get-tuple-element.134.refs_8_), channel_id=1, source_target_pairs={{0,4},{4,0},{8,12},{12,8},{16,20},{20,16},{24,28},{28,24},{1,5},{5... | collective-permute-start | bytes 884744 | tf_op jit(solution)/shard_map/ppermute | solution.py:633
  86.6 9.6 %attn_bwd.3 = (bf16[8,400,768]{2,1,0:T(8,128)(2,1)S(1)}, bf16[384,640]{1,0:T(8,128)(2,1)S(1)}, bf16[2,2,2,48,512]{4,3,2,1,0:T(8,128)(2,1)S(1)}, bf16[2,2,2,48,384]{4,3,2,1,0:T(8,128)(2,1)S(1)}) custom-call(s32[18]{0:T(128)S(1)} %pad_add_fusion.refs_0_, ...), custom_call_target="tpu_custom_call", output_to_operand_aliasing={{2}: (10, {}), {3}: (11, {})} | custom-call | tf_op jit(solution)/shard_map/attn_bwd/pallas_call | solution.py:117
  99.0 8.4 %input_grad.1 = (bf16[2048,384]{1,0:T(8,128)(2,1)}, bf16[2,2,48,1152]{3,2,1,0:T(8,128)(2,1)S(1)}, bf16[2,2,48,384]{3,2,1,0:T(8,128)(2,1)S(1)}) custom-call(s32[18]{0:T(128)S(1)} %pad_add_fusion.refs_0_, bf16[2048,384]{1,0:T(8,128)(2,1)S(1)} %copy-done, ...), custom_call_target="tpu_custom_call", output_to_operand_aliasing={{1}: (10, {}), {2}: (11, {})} | custom-call | tf_op jit(solution)/shard_map/input_grad/pallas_call | solution.py:117
  107.5 2.0 %collective-permute-done.17 = bf16[2,2,48,1152]{3,2,1,0:T(8,128)(2,1)S(1)} collective-permute-done((bf16[2,2,48,1152]{3,2,1,0:T(8,128)(2,1)S(1)}, bf16[2,2,48,1152]{3,2,1,0:T(8,128)(2,1)S(1)}, u32[]{:S(2)}, u32[]{:S(2)}) %collective-permute-start.17) | collective-permute-done | bytes 442400 | tf_op jit(solution)/shard_map/ppermute | solution.py:633
  111.0 5.3 %layer_out.1 = (bf16[2048,384]{1,0:T(8,128)(2,1)}, bf16[2,48,1536]{2,1,0:T(8,128)(2,1)S(1)}) custom-call(s32[18]{0:T(128)S(1)} %pad_add_fusion.refs_0_, f32[2048,384]{1,0:T(8,128)S(1)} %get-tuple-element.78.refs_1_, bf16[2048,1536]{1,0:T(8,128)(2,1)S(1)} %get-tuple-element.79.refs_2_, ...), custom_call_target="tpu_custom_call", output_to_operand_aliasing={{1}: (6, {})} | custom-call | tf_op jit(solution)/shard_map/layer_out/pallas_call | solution.py:117
  117.2 3.7 %collective-permute-start.20 = (bf16[48,1536]{1,0:T(8,128)(2,1)S(1)}, bf16[48,1536]{1,0:T(8,128)(2,1)S(1)}, u32[]{:S(2)}, u32[]{:S(2)}) collective-permute-start(bf16[48,1536]{1,0:T(8,128)(2,1)S(1)} %dynamic-slice_bitcast_fusion.4), channel_id=1, source_target_pairs={{0,16},{4,20},{8,24},{12,28},{16,0},{20,4},{24,8},{28,12},{1,17},{... | collective-permute-start | bytes 442376 | tf_op jit(solution)/shard_map/ppermute | solution.py:633
  120.9 5.4 %collective-permute-done.20 = bf16[48,1536]{1,0:T(8,128)(2,1)S(1)} collective-permute-done((bf16[48,1536]{1,0:T(8,128)(2,1)S(1)}, bf16[48,1536]{1,0:T(8,128)(2,1)S(1)}, u32[]{:S(2)}, u32[]{:S(2)}) %collective-permute-start.20) | collective-permute-done | bytes 147488 | tf_op jit(solution)/shard_map/ppermute | solution.py:633
  126.3 3.1 %collective-permute-start.21 = (bf16[48,1536]{1,0:T(8,128)(2,1)S(1)}, bf16[48,1536]{1,0:T(8,128)(2,1)S(1)}, u32[]{:S(2)}, u32[]{:S(2)}) collective-permute-start(bf16[48,1536]{1,0:T(8,128)(2,1)S(1)} %fusion.8), channel_id=1, source_target_pairs={{0,2},{1,3},{2,0},{3,1},{4,6},{5,7},{6,4},{7,5},{8,10},{9,11},{10,... | collective-permute-start | bytes 442376 | tf_op jit(solution)/shard_map/ppermute | solution.py:633
  129.5 3.1 %collective-permute-done.21 = bf16[48,1536]{1,0:T(8,128)(2,1)S(1)} collective-permute-done((bf16[48,1536]{1,0:T(8,128)(2,1)S(1)}, bf16[48,1536]{1,0:T(8,128)(2,1)S(1)}, u32[]{:S(2)}, u32[]{:S(2)}) %collective-permute-start.21) | collective-permute-done | bytes 147488 | tf_op jit(solution)/shard_map/ppermute | solution.py:633
  132.7 1.5 %collective-permute-done.22.refs_2_ = bf16[48,2432]{1,0:T(8,128)(2,1)S(1)} collective-permute-done((bf16[48,2432]{1,0:T(8,128)(2,1)S(1)}, bf16[48,2432]{1,0:T(8,128)(2,1)S(1)}, u32[]{:S(2)}, u32[]{:S(2)}) %collective-permute-start.22) | collective-permute-done | bytes 233504 | tf_op jit(solution)/shard_map/ppermute | solution.py:633
  134.2 1.7 %finish.1 = (f32[432,128]{1,0:T(8,128)}, f32[144,128]{1,0:T(8,128)}, f32[576,128]{1,0:T(8,128)}, f32[576,128]{1,0:T(8,128)}, f32[16,128]{1,0:T(8,128)S(1)}) custom-call(s32[18]{0:T(128)S(1)} %pad_add_fusion.refs_0_, bf16[48,2432]{1,0:T(8,128)(2,1)S(1)} %pad_maximum_fusion.6.refs_1_, bf16[48,2432]{1,0:T(8,128)(2,1)S(1)} %collective-permute-done.22.refs_2_), custom_call_target="tpu_custom_call" | custom-call | tf_op jit(solution)/shard_map/finish/pallas_call | solution.py:117
  (124 shorter events, 20.0 us)
Async XLA Ops:
  4.2 7.4 %collective-permute-start = (bf16[48,640]{1,0:T(8,128)(2,1)S(1)}, bf16[48,640]{1,0:T(8,128)(2,1)S(1)}, u32[]{:S(2)}, u32[]{:S(2)}) collective-permute-start(bf16[48,640]{1,0:T(8,128)(2,1)S(1)} %maximum_maximum_fusion), channel_id=1, source_target_pairs={{0,16},{4,20},{8,24},{12,28},{16,0},{20,4},{24,8},{28,12},{1,17},{... | collective-permute-start | bytes 184328 | tf_op jit(solution)/shard_map/ppermute | solution.py:633
  11.4 6.3 %collective-permute-start.4 = (bf16[48,896]{1,0:T(8,128)(2,1)S(1)}, bf16[48,896]{1,0:T(8,128)(2,1)S(1)}, u32[]{:S(2)}, u32[]{:S(2)}) collective-permute-start(bf16[48,896]{1,0:T(8,128)(2,1)S(1)} %pad_maximum_fusion.10), channel_id=1, source_target_pairs={{0,16},{4,20},{8,24},{12,28},{16,0},{20,4},{24,8},{28,12},{1,17},{... | collective-permute-start | bytes 258056 | tf_op jit(solution)/shard_map/ppermute | solution.py:633
  11.7 7.7 %collective-permute-start.1 = (bf16[2,48,640]{2,1,0:T(8,128)(2,1)S(1)}, bf16[2,48,640]{2,1,0:T(8,128)(2,1)S(1)}, u32[]{:S(2)}, u32[]{:S(2)}) collective-permute-start(bf16[2,48,640]{2,1,0:T(8,128)(2,1)S(1)} %pad_maximum_fusion.9), channel_id=1, source_target_pairs={{0,8},{4,12},{8,0},{12,4},{16,24},{20,28},{24,16},{28,20},{1,9},{5... | collective-permute-start | bytes 368648 | tf_op jit(solution)/shard_map/ppermute | solution.py:633
  17.8 5.5 %collective-permute-start.5 = (bf16[2,48,896]{2,1,0:T(8,128)(2,1)S(1)}, bf16[2,48,896]{2,1,0:T(8,128)(2,1)S(1)}, u32[]{:S(2)}, u32[]{:S(2)}) collective-permute-start(bf16[2,48,896]{2,1,0:T(8,128)(2,1)S(1)} %pad_maximum_fusion.7), channel_id=1, source_target_pairs={{0,8},{4,12},{8,0},{12,4},{16,24},{20,28},{24,16},{28,20},{1,9},{5... | collective-permute-start | bytes 516104 | tf_op jit(solution)/shard_map/ppermute | solution.py:633
  19.5 7.8 %collective-permute-start.2 = (bf16[2,2,48,640]{3,2,0,1:T(8,128)(2,1)S(1)}, bf16[2,2,48,640]{3,2,0,1:T(8,128)(2,1)S(1)}, u32[]{:S(2)}, u32[]{:S(2)}) collective-permute-start(bf16[2,2,48,640]{3,2,0,1:T(8,128)(2,1)S(1)} %pad_maximum_fusion.5), channel_id=1, source_target_pairs={{0,4},{4,0},{8,12},{12,8},{16,20},{20,16},{24,28},{28,24},{1,5},{5... | collective-permute-start | bytes 737288 | tf_op jit(solution)/shard_map/ppermute | solution.py:633
  23.4 8.0 %collective-permute-start.9 = (bf16[2,2,48,384]{3,2,0,1:T(8,128)(2,1)S(1)}, bf16[2,2,48,384]{3,2,0,1:T(8,128)(2,1)S(1)}, u32[]{:S(2)}, u32[]{:S(2)}) collective-permute-start(bf16[2,2,48,384]{3,2,0,1:T(8,128)(2,1)S(1)} %pad_maximum_fusion.8), channel_id=1, source_target_pairs={{0,4},{4,0},{8,12},{12,8},{16,20},{20,16},{24,28},{28,24},{1,5},{5... | collective-permute-start | bytes 442376 | tf_op jit(solution)/shard_map/ppermute | solution.py:633
  25.0 5.7 %collective-permute-start.6 = (bf16[2,2,48,512]{3,2,0,1:T(8,128)(2,1)S(1)}, bf16[2,2,48,512]{3,2,0,1:T(8,128)(2,1)S(1)}, u32[]{:S(2)}, u32[]{:S(2)}) collective-permute-start(bf16[2,2,48,512]{3,2,0,1:T(8,128)(2,1)S(1)} %fusion.9), channel_id=1, source_target_pairs={{0,2},{1,3},{2,0},{3,1},{4,6},{5,7},{6,4},{7,5},{8,10},{9,11},{10,... | collective-permute-start | bytes 589832 | tf_op jit(solution)/shard_map/ppermute | solution.py:633
  27.5 5.6 %collective-permute-start.3 = (bf16[384,640]{1,0:T(8,128)(2,1)S(1)}, bf16[384,640]{1,0:T(8,128)(2,1)S(1)}, u32[]{:S(2)}, u32[]{:S(2)}) collective-permute-start(bf16[384,640]{1,0:T(8,128)(2,1)S(1)} %bitcast.107), channel_id=1, source_target_pairs={{0,1},{1,0},{2,3},{3,2},{4,5},{5,4},{6,7},{7,6},{8,9},{9,8},{10,11... | collective-permute-start | bytes 1474568 | tf_op jit(solution)/shard_map/ppermute | solution.py:633
  30.8 14.7 %collective-permute-start.7 = (bf16[2,2,2,48,512]{4,3,1,2,0:T(8,128)(2,1)S(1)}, bf16[2,2,2,48,512]{4,3,1,2,0:T(8,128)(2,1)S(1)}, u32[]{:S(2)}, u32[]{:S(2)}) collective-permute-start(bf16[2,2,2,48,512]{4,3,1,2,0:T(8,128)(2,1)S(1)} %pad_maximum_fusion.3), channel_id=1, source_target_pairs={{0,4},{4,0},{8,12},{12,8},{16,20},{20,16},{24,28},{28,24},{1,5},{5... | collective-permute-start | bytes 1179656 | tf_op jit(solution)/shard_map/ppermute | solution.py:633
  31.5 14.3 %collective-permute-start.10 = (bf16[2,2,2,48,384]{4,3,0,1,2:T(8,128)(2,1)S(1)}, bf16[2,2,2,48,384]{4,3,0,1,2:T(8,128)(2,1)S(1)}, u32[]{:S(2)}, u32[]{:S(2)}) collective-permute-start(bf16[2,2,2,48,384]{4,3,0,1,2:T(8,128)(2,1)S(1)} %pad_maximum_fusion.4), channel_id=1, source_target_pairs={{0,2},{1,3},{2,0},{3,1},{4,6},{5,7},{6,4},{7,5},{8,10},{9,11},{10,... | collective-permute-start | bytes 884744 | tf_op jit(solution)/shard_map/ppermute | solution.py:633
  45.7 3.2 %collective-permute-start.8 = (bf16[2,384,512]{2,1,0:T(8,128)(2,1)S(1)}, bf16[2,384,512]{2,1,0:T(8,128)(2,1)S(1)}, u32[]{:S(2)}, u32[]{:S(2)}) collective-permute-start(bf16[2,384,512]{2,1,0:T(8,128)(2,1)S(1)} %bitcast.111), channel_id=1, source_target_pairs={{0,1},{1,0},{2,3},{3,2},{4,5},{5,4},{6,7},{7,6},{8,9},{9,8},{10,11... | collective-permute-start | bytes 2359304 | tf_op jit(solution)/shard_map/ppermute | solution.py:633
  46.1 2.8 %collective-permute-start.11 = (bf16[2,384,384]{2,1,0:T(8,128)(2,1)S(1)}, bf16[2,384,384]{2,1,0:T(8,128)(2,1)S(1)}, u32[]{:S(2)}, u32[]{:S(2)}) collective-permute-start(bf16[2,384,384]{2,1,0:T(8,128)(2,1)S(1)} %pad_maximum_fusion.1.refs_7_.refs_3_), channel_id=1, source_target_pairs={{0,1},{1,0},{2,3},{3,2},{4,5},{5,4},{6,7},{7,6},{8,9},{9,8},{10,11... | collective-permute-start | bytes 1769480 | tf_op jit(solution)/shard_map/ppermute | solution.py:633
  48.9 25.1 %copy-start.1 = (bf16[2,384,384]{2,1,0:T(8,128)(2,1)}, bf16[2,384,384]{2,1,0:T(8,128)(2,1)S(1)}, u32[]{:S(2)}) copy-start(bf16[2,384,384]{2,1,0:T(8,128)(2,1)S(1)} %collective-permute-done.11.refs_8_.refs_4_) | copy-start | bytes 1769476
  74.0 10.1 %collective-permute-start.13 = (bf16[2,2,192,384]{3,2,1,0:T(8,128)(2,1)S(1)}, bf16[2,2,192,384]{3,2,1,0:T(8,128)(2,1)S(1)}, u32[]{:S(2)}, u32[]{:S(2)}) collective-permute-start(bf16[2,2,192,384]{3,2,1,0:T(8,128)(2,1)S(1)} %get-tuple-element.90.refs_8_), channel_id=1, source_target_pairs={{0,1},{1,0},{2,3},{3,2},{4,5},{5,4},{6,7},{7,6},{8,9},{9,8},{10,11... | collective-permute-start | bytes 1769480 | tf_op jit(solution)/shard_map/ppermute | solution.py:633
  74.2 11.9 %collective-permute-start.12 = (bf16[2,384,512]{2,1,0:T(8,128)(2,1)S(1)}, bf16[2,384,512]{2,1,0:T(8,128)(2,1)S(1)}, u32[]{:S(2)}, u32[]{:S(2)}) collective-permute-start(bf16[2,384,512]{2,1,0:T(8,128)(2,1)S(1)} %get-tuple-element.89.refs_7_), channel_id=1, source_target_pairs={{0,1},{1,0},{2,3},{3,2},{4,5},{5,4},{6,7},{7,6},{8,9},{9,8},{10,11... | collective-permute-start | bytes 2359304 | tf_op jit(solution)/shard_map/ppermute | solution.py:633
  84.0 12.2 %collective-permute-start.14 = (bf16[384,640]{1,0:T(8,128)(2,1)S(1)}, bf16[384,640]{1,0:T(8,128)(2,1)S(1)}, u32[]{:S(2)}, u32[]{:S(2)}) collective-permute-start(bf16[384,640]{1,0:T(8,128)(2,1)S(1)} %get-tuple-element.97.refs_9_), channel_id=1, source_target_pairs={{0,1},{1,0},{2,3},{3,2},{4,5},{5,4},{6,7},{7,6},{8,9},{9,8},{10,11... | collective-permute-start | bytes 1474568 | tf_op jit(solution)/shard_map/ppermute | solution.py:633
  84.4 12.0 %collective-permute-start.16 = (bf16[2,2,2,48,384]{4,3,2,1,0:T(8,128)(2,1)S(1)}, bf16[2,2,2,48,384]{4,3,2,1,0:T(8,128)(2,1)S(1)}, u32[]{:S(2)}, u32[]{:S(2)}) collective-permute-start(bf16[2,2,2,48,384]{4,3,2,1,0:T(8,128)(2,1)S(1)} %get-tuple-element.134.refs_8_), channel_id=1, source_target_pairs={{0,4},{4,0},{8,12},{12,8},{16,20},{20,16},{24,28},{28,24},{1,5},{5... | collective-permute-start | bytes 884744 | tf_op jit(solution)/shard_map/ppermute | solution.py:633
  86.5 11.3 %collective-permute-start.15 = (bf16[2,2,2,48,512]{4,3,2,1,0:T(8,128)(2,1)S(1)}, bf16[2,2,2,48,512]{4,3,2,1,0:T(8,128)(2,1)S(1)}, u32[]{:S(2)}, u32[]{:S(2)}) collective-permute-start(bf16[2,2,2,48,512]{4,3,2,1,0:T(8,128)(2,1)S(1)} %get-tuple-element.128.refs_7_), channel_id=1, source_target_pairs={{0,2},{1,3},{2,0},{3,1},{4,6},{5,7},{6,4},{7,5},{8,10},{9,11},{10,... | collective-permute-start | bytes 1179656 | tf_op jit(solution)/shard_map/ppermute | solution.py:633
  98.0 11.5 %collective-permute-start.17 = (bf16[2,2,48,1152]{3,2,1,0:T(8,128)(2,1)S(1)}, bf16[2,2,48,1152]{3,2,1,0:T(8,128)(2,1)S(1)}, u32[]{:S(2)}, u32[]{:S(2)}) collective-permute-start(bf16[2,2,48,1152]{3,2,1,0:T(8,128)(2,1)S(1)} %get-tuple-element.124.refs_8_), channel_id=1, source_target_pairs={{0,4},{4,0},{8,12},{12,8},{16,20},{20,16},{24,28},{28,24},{1,5},{5... | collective-permute-start | bytes 1327112 | tf_op jit(solution)/shard_map/ppermute | solution.py:633
  98.4 9.1 %collective-permute-start.18 = (bf16[2,2,48,384]{3,2,1,0:T(8,128)(2,1)S(1)}, bf16[2,2,48,384]{3,2,1,0:T(8,128)(2,1)S(1)}, u32[]{:S(2)}, u32[]{:S(2)}) collective-permute-start(bf16[2,2,48,384]{3,2,1,0:T(8,128)(2,1)S(1)} %get-tuple-element.144.refs_9_), channel_id=1, source_target_pairs={{0,2},{1,3},{2,0},{3,1},{4,6},{5,7},{6,4},{7,5},{8,10},{9,11},{10,... | collective-permute-start | bytes 442376 | tf_op jit(solution)/shard_map/ppermute | solution.py:633
  109.7 7.4 %collective-permute-start.19 = (bf16[2,48,1536]{2,1,0:T(8,128)(2,1)S(1)}, bf16[2,48,1536]{2,1,0:T(8,128)(2,1)S(1)}, u32[]{:S(2)}, u32[]{:S(2)}) collective-permute-start(bf16[2,48,1536]{2,1,0:T(8,128)(2,1)S(1)} %get-tuple-element.132.refs_5_), channel_id=1, source_target_pairs={{0,8},{4,12},{8,0},{12,4},{16,24},{20,28},{24,16},{28,20},{1,9},{5... | collective-permute-start | bytes 884744 | tf_op jit(solution)/shard_map/ppermute | solution.py:633
  117.2 9.1 %collective-permute-start.20 = (bf16[48,1536]{1,0:T(8,128)(2,1)S(1)}, bf16[48,1536]{1,0:T(8,128)(2,1)S(1)}, u32[]{:S(2)}, u32[]{:S(2)}) collective-permute-start(bf16[48,1536]{1,0:T(8,128)(2,1)S(1)} %dynamic-slice_bitcast_fusion.4), channel_id=1, source_target_pairs={{0,16},{4,20},{8,24},{12,28},{16,0},{20,4},{24,8},{28,12},{1,17},{... | collective-permute-start | bytes 442376 | tf_op jit(solution)/shard_map/ppermute | solution.py:633
  126.3 6.2 %collective-permute-start.21 = (bf16[48,1536]{1,0:T(8,128)(2,1)S(1)}, bf16[48,1536]{1,0:T(8,128)(2,1)S(1)}, u32[]{:S(2)}, u32[]{:S(2)}) collective-permute-start(bf16[48,1536]{1,0:T(8,128)(2,1)S(1)} %fusion.8), channel_id=1, source_target_pairs={{0,2},{1,3},{2,0},{3,1},{4,6},{5,7},{6,4},{7,5},{8,10},{9,11},{10,... | collective-permute-start | bytes 442376 | tf_op jit(solution)/shard_map/ppermute | solution.py:633
  132.7 1.6 %collective-permute-start.22 = (bf16[48,2432]{1,0:T(8,128)(2,1)S(1)}, bf16[48,2432]{1,0:T(8,128)(2,1)S(1)}, u32[]{:S(2)}, u32[]{:S(2)}) collective-permute-start(bf16[48,2432]{1,0:T(8,128)(2,1)S(1)} %pad_maximum_fusion.6.refs_1_), channel_id=1, source_target_pairs={{0,1},{1,0},{2,3},{3,2},{4,5},{5,4},{6,7},{7,6},{8,9},{9,8},{10,11... | collective-permute-start | bytes 700424 | tf_op jit(solution)/shard_map/ppermute | solution.py:633
  (6 other events, 43.5 us)
